TPU v7x, 32 devices: a whole 2x2x4 slice. The times are simulated.
32 devices in a mesh: dp: 8 (over y, x, core), tensor: 4 (over z).
Axes of the slice: x: 2, y: 2, z: 4, core: 2. Of those that a mesh axis runs over, the one named last changes fastest.
Arguments:
- tokens: bfloat16 [16, 1024, 2048], P('dp', 'tensor'), may hold values from -6 to 6
- segments: int32 [16, 1024], P('dp'), may hold values from 0 to 3, as said below
- attn_norm: bfloat16 [2048], P('dp'), may hold values from 0.099609375 to 1.8984375
- w_query: bfloat16 [2048, 2048], P('dp', 'tensor'), may hold values from -0.125 to 0.125
- w_key: bfloat16 [2048, 512], P('dp', 'tensor'), may hold values from -0.125 to 0.125
- w_value: bfloat16 [2048, 512], P('dp', 'tensor'), may hold values from -0.125 to 0.125
- w_out: bfloat16 [2048, 2048], P('tensor', 'dp'), may hold values from -1 to 1
- mlp_norm: bfloat16 [2048], P('dp'), may hold values from 0.099609375 to 1.8984375
- w_gate: bfloat16 [2048, 8192], P('dp', 'tensor'), may hold values from -0.125 to 0.125
- w_up: bfloat16 [2048, 8192], P('dp', 'tensor'), may hold values from -0.125 to 0.125
- w_down: bfloat16 [8192, 2048], P('tensor', 'dp'), may hold values from -0.0625 to 0.0625
- cotangent: bfloat16 [16, 1024, 2048], P('dp', 'tensor'), may hold values from -6 to 6
Outputs:
- mixed: bfloat16 [16, 1024, 2048], P('dp', 'tensor')
- grad_tokens: bfloat16 [16, 1024, 2048], P('dp', 'tensor')
- grad_attn_norm: float32 [2048], P(('dp', 'tensor'))
- grad_query: float32 [2048, 2048], P('dp', 'tensor')
- grad_key: float32 [2048, 512], P('dp', 'tensor')
- grad_value: float32 [2048, 512], P('dp', 'tensor')
- grad_out: float32 [2048, 2048], P('tensor', 'dp')
- sensitivity_perceptron_rescale: float32 [2048], P(('dp', 'tensor'))
- grad_gate: float32 [2048, 8192], P('dp', 'tensor')
- grad_up: float32 [2048, 8192], P('dp', 'tensor')
- grad_down: float32 [8192, 2048], P('tensor', 'dp')
Inputs may be any that keep to these rules, and one draw needn't show every extreme that they name: `segments`: in each sequence the document numbers start at 0, never fall and end at 3; the first and the last document are never empty, and number 2 may be skipped. Document 1 begins within the first 256 positions and ends within the last 256 positions.
All inputs are finite; a program needn't handle non-finite values.
Results may differ from a plain program's by a relative error of at most 0.02.
Values may be sent and summed in bfloat16 or wider, within the bound.
No kernel may reach another device: no remote copies, remote signals or barrier semaphores. Data moves between devices by JAX's collectives and lax.ppermute only.
A program may use at most 320 MiB of HBM per device.

v0:
```python
import jax
import jax.numpy as jnp
from jax import lax
from jax.sharding import PartitionSpec as P

HD = 64


EPS = 1e-05
THETA = 500000.0


def rotary_tables(positions, head_size):
    half_size = head_size // 2
    frequency = THETA ** (-2.0 * jnp.arange(half_size, dtype=jnp.float32) / head_size)
    angles = positions.astype(jnp.float32)[:, None] * frequency[None, :]
    cos_table = jnp.cos(angles)
    sine_table = jnp.sin(angles)
    return (
        jnp.concatenate([cos_table, cos_table], -1),
        jnp.concatenate([sine_table, sine_table], -1),
    )


def rotate(values, cos_table, sine_table):
    half_size = values.shape[-1] // 2
    turned = jnp.concatenate([-values[..., half_size:], values[..., :half_size]], -1)
    return values * cos_table[:, None, :] + turned * sine_table[:, None, :]


def rotate_back(values, cos_table, sine_table):
    half_size = values.shape[-1] // 2
    turned = jnp.concatenate([-values[..., half_size:], values[..., :half_size]], -1)
    return values * cos_table[:, None, :] - turned * sine_table[:, None, :]


def masked_logits(query_block, key_rows, query_pos, query_seg, seg_ids):
    scores = jnp.einsum("qgjd,kgd->gjqk", query_block, key_rows, preferred_element_type=jnp.float32)
    key_pos = jnp.arange(key_rows.shape[0], dtype=jnp.int32)
    allowed = (key_pos[None, :] <= query_pos[:, None]) & (seg_ids[None, :] == query_seg[:, None])
    return jnp.where(allowed, scores * HD ** (-0.5), -1e30)


def attend_forward(queries, key_rows, values, seg_ids):
    seq_length = queries.shape[0]
    block_rows = min(512, seq_length)
    outputs = []
    log_sums = []
    for row_start in range(0, seq_length, block_rows):
        query_pos = jnp.arange(row_start, row_start + block_rows, dtype=jnp.int32)
        logits = masked_logits(
            queries[row_start : row_start + block_rows],
            key_rows,
            query_pos,
            seg_ids[row_start : row_start + block_rows],
            seg_ids,
        )
        row_max = jnp.max(logits, -1, keepdims=True)
        exponent = jnp.exp(logits - row_max)
        row_total = jnp.sum(exponent, -1, keepdims=True)
        weights = (exponent / row_total).astype(jnp.bfloat16)
        outputs.append(
            jnp.einsum("gjqk,kgd->qgjd", weights, values, preferred_element_type=jnp.float32)
        )
        log_sums.append(row_max + jnp.log(row_total))
    return (jnp.concatenate(outputs, 0), jnp.concatenate(log_sums, 2))


def attend_backward(queries, key_rows, values, seg_ids, log_sums, grad_heads):
    seq_length = queries.shape[0]
    block_rows = min(512, seq_length)
    grad_queries = []
    grad_keys = jnp.zeros(key_rows.shape, jnp.float32)
    grad_values = jnp.zeros(values.shape, jnp.float32)
    for row_start in range(0, seq_length, block_rows):
        row_range = slice(row_start, row_start + block_rows)
        query_block = queries[row_range]
        grad_block = grad_heads[row_range]
        query_pos = jnp.arange(row_start, row_start + block_rows, dtype=jnp.int32)
        logits = masked_logits(query_block, key_rows, query_pos, seg_ids[row_range], seg_ids)
        probs = jnp.exp(logits - log_sums[:, :, row_range])
        grad_probs = jnp.einsum(
            "qgjd,kgd->gjqk", grad_block, values, preferred_element_type=jnp.float32
        )
        delta_row = jnp.sum(probs * grad_probs, -1, keepdims=True)
        grad_scores = (probs * (grad_probs - delta_row) * HD ** (-0.5)).astype(jnp.bfloat16)
        grad_queries.append(
            jnp.einsum("gjqk,kgd->qgjd", grad_scores, key_rows, preferred_element_type=jnp.float32)
        )
        grad_keys = grad_keys + jnp.einsum(
            "gjqk,qgjd->kgd", grad_scores, query_block, preferred_element_type=jnp.float32
        )
        grad_values = grad_values + jnp.einsum(
            "gjqk,qgjd->kgd",
            probs.astype(jnp.bfloat16),
            grad_block,
            preferred_element_type=jnp.float32,
        )
    return (jnp.concatenate(grad_queries, 0), grad_keys, grad_values)


def norm_backward(grad_scaled, unrounded, norm_scale):
    return norm_scale * (
        grad_scaled - unrounded * jnp.mean(unrounded * grad_scaled, -1, keepdims=True)
    )


def shards(
    tokens,
    segments,
    attn_norm,
    w_query,
    w_key,
    w_value,
    w_out,
    mlp_norm,
    w_gate,
    w_up,
    w_down,
    cotangent,
):
    tp_count = lax.axis_size("tensor")
    dp_count = lax.axis_size("dp")
    seqs_here = tokens.shape[0]
    seq_length = segments.shape[1]
    head_count = w_query.shape[1] // HD
    kv_count = w_key.shape[1] // HD
    group_size = head_count // kv_count
    query_cols = head_count * HD
    key_cols = kv_count * HD
    gain_one, query_all, key_all, value_all, output_projection_full = (
        lax.all_gather(attn_norm, "dp", axis=0, tiled=True),
        lax.all_gather(w_query, "dp", axis=0, tiled=True),
        lax.all_gather(w_key, "dp", axis=0, tiled=True),
        lax.all_gather(w_value, "dp", axis=0, tiled=True),
        lax.all_gather(w_out, "dp", axis=1, tiled=True),
    )
    query_key_value_weight = jnp.concatenate([query_all, key_all, value_all], 1)
    positions = jnp.arange(seq_length, dtype=jnp.int32)
    cos_table, sine_table = rotary_tables(positions, HD)
    tokens_full = tokens.astype(jnp.float32)
    norm_one = lax.rsqrt(jnp.mean(tokens_full * tokens_full, -1, keepdims=True) + EPS)
    unrounded_one = tokens_full * norm_one
    gathered_one = lax.all_gather(unrounded_one.astype(jnp.bfloat16), "tensor", axis=1, tiled=True)
    first_normalized = (gathered_one.astype(jnp.float32) * gain_one.astype(jnp.float32)).astype(
        jnp.bfloat16
    )
    projected = jnp.einsum(
        "tvh,hr->tvr", first_normalized, query_key_value_weight, preferred_element_type=jnp.float32
    )
    asker_unturned = projected[..., :query_cols].reshape(seqs_here, seq_length, head_count, HD)
    key_pre = projected[..., query_cols : query_cols + key_cols].reshape(
        seqs_here, seq_length, kv_count, HD
    )
    values = (
        projected[..., query_cols + key_cols :]
        .astype(jnp.bfloat16)
        .reshape(seqs_here, seq_length, kv_count, HD)
    )
    queries = (
        rotate(asker_unturned, cos_table, sine_table)
        .astype(jnp.bfloat16)
        .reshape(seqs_here, seq_length, kv_count, group_size, HD)
    )
    key_rows = rotate(key_pre, cos_table, sine_table).astype(jnp.bfloat16)
    attended, log_sums = lax.map(
        lambda inputs: attend_forward(*inputs), (queries, key_rows, values, segments)
    )
    head_outputs = attended.reshape(seqs_here, seq_length, query_cols).astype(jnp.bfloat16)
    attention_parts = jnp.einsum(
        "rom,mn->ron", head_outputs, output_projection_full, preferred_element_type=jnp.float32
    )
    residual = tokens_full + lax.psum_scatter(
        attention_parts, "tensor", scatter_dimension=1, tiled=True
    )
    gain_two, gate_projection_full, up_projection_full, lowering_matrix_entire = (
        lax.all_gather(mlp_norm, "dp", axis=0, tiled=True),
        lax.all_gather(w_gate, "dp", axis=0, tiled=True),
        lax.all_gather(w_up, "dp", axis=0, tiled=True),
        lax.all_gather(w_down, "dp", axis=1, tiled=True),
    )
    norm_two = lax.rsqrt(jnp.mean(residual * residual, -1, keepdims=True) + EPS)
    unrounded_two = residual * norm_two
    gathered_two = lax.all_gather(unrounded_two.astype(jnp.bfloat16), "tensor", axis=1, tiled=True)
    latter_rescaled_rows = (gathered_two.astype(jnp.float32) * gain_two.astype(jnp.float32)).astype(
        jnp.bfloat16
    )
    gated_product = jnp.einsum(
        "vcx,xk->vck",
        latter_rescaled_rows,
        gate_projection_full,
        preferred_element_type=jnp.float32,
    )
    upward_projection = jnp.einsum(
        "vcx,xk->vck", latter_rescaled_rows, up_projection_full, preferred_element_type=jnp.float32
    )
    sigma = jax.nn.sigmoid(gated_product)
    inner_activation = (gated_product * sigma * upward_projection).astype(jnp.bfloat16)
    feedforward_parts = jnp.einsum(
        "qty,yj->qtj", inner_activation, lowering_matrix_entire, preferred_element_type=jnp.float32
    )
    mixed = (
        residual
        + lax.psum_scatter(
            feedforward_parts.astype(jnp.bfloat16), "tensor", scatter_dimension=1, tiled=True
        ).astype(jnp.float32)
    ).astype(jnp.bfloat16)
    (
        gain_one,
        query_all,
        key_all,
        value_all,
        output_projection_full,
        gain_two,
        gate_projection_full,
        up_projection_full,
        lowering_matrix_entire,
    ) = (
        lax.all_gather(attn_norm, "dp", axis=0, tiled=True),
        lax.all_gather(w_query, "dp", axis=0, tiled=True),
        lax.all_gather(w_key, "dp", axis=0, tiled=True),
        lax.all_gather(w_value, "dp", axis=0, tiled=True),
        lax.all_gather(w_out, "dp", axis=1, tiled=True),
        lax.all_gather(mlp_norm, "dp", axis=0, tiled=True),
        lax.all_gather(w_gate, "dp", axis=0, tiled=True),
        lax.all_gather(w_up, "dp", axis=0, tiled=True),
        lax.all_gather(w_down, "dp", axis=1, tiled=True),
    )
    query_key_value_weight = jnp.concatenate([query_all, key_all, value_all], 1)
    mixed_gradient = lax.all_gather(cotangent, "tensor", axis=1, tiled=True)
    inner_gradient = jnp.einsum(
        "htc,qc->htq", mixed_gradient, lowering_matrix_entire, preferred_element_type=jnp.float32
    )
    switched_multiple_sensitivity = (
        inner_gradient * upward_projection * sigma * (1.0 + gated_product * (1.0 - sigma))
    ).astype(jnp.bfloat16)
    raising_sensitivity = (inner_gradient * gated_product * sigma).astype(jnp.bfloat16)
    grad_normed_two = jnp.einsum(
        "tkx,wx->tkw",
        switched_multiple_sensitivity,
        gate_projection_full,
        preferred_element_type=jnp.float32,
    )
    grad_normed_two = grad_normed_two + jnp.einsum(
        "tkx,wx->tkw", raising_sensitivity, up_projection_full, preferred_element_type=jnp.float32
    )
    gain_two_terms = jnp.sum(gathered_two.astype(jnp.float32) * grad_normed_two, (0, 1)).reshape(
        dp_count, tp_count, -1
    )
    grad_scaled_two, gain_two_part = (
        lax.psum_scatter(
            (grad_normed_two * gain_two.astype(jnp.float32)).astype(jnp.bfloat16),
            "tensor",
            scatter_dimension=1,
            tiled=True,
        ).astype(jnp.float32),
        lax.psum_scatter(
            gain_two_terms.astype(jnp.bfloat16), "tensor", scatter_dimension=1, tiled=True
        ).astype(jnp.float32),
    )
    grad_residual = cotangent.astype(jnp.float32) + norm_backward(
        grad_scaled_two, unrounded_two, norm_two
    )
    down_weight_gradient = jnp.einsum(
        "ypq,ypa->qa", inner_activation, mixed_gradient, preferred_element_type=jnp.float32
    )
    grad_gate_w = jnp.einsum(
        "rhu,rhi->ui",
        latter_rescaled_rows,
        switched_multiple_sensitivity,
        preferred_element_type=jnp.float32,
    )
    grad_up_w = jnp.einsum(
        "rhu,rhi->ui", latter_rescaled_rows, raising_sensitivity, preferred_element_type=jnp.float32
    )
    mlp_sums = (
        lax.psum_scatter(
            gain_two_part.astype(jnp.bfloat16), "dp", scatter_dimension=0, tiled=True
        ).astype(jnp.float32),
        lax.psum_scatter(
            grad_gate_w.astype(jnp.bfloat16), "dp", scatter_dimension=0, tiled=True
        ).astype(jnp.float32),
        lax.psum_scatter(
            grad_up_w.astype(jnp.bfloat16), "dp", scatter_dimension=0, tiled=True
        ).astype(jnp.float32),
        lax.psum_scatter(
            down_weight_gradient.astype(jnp.bfloat16), "dp", scatter_dimension=1, tiled=True
        ).astype(jnp.float32),
    )
    attention_gradient = lax.all_gather(
        grad_residual.astype(jnp.bfloat16), "tensor", axis=1, tiled=True
    )
    grad_heads = jnp.einsum(
        "fmo,po->fmp",
        attention_gradient,
        output_projection_full,
        preferred_element_type=jnp.float32,
    ).astype(jnp.bfloat16)
    output_weight_gradient = jnp.einsum(
        "wro,wrz->oz", head_outputs, attention_gradient, preferred_element_type=jnp.float32
    )
    grad_heads = grad_heads.reshape(seqs_here, seq_length, kv_count, group_size, HD)
    sensitivity_turned_asker, grad_k_rot, grad_v_raw = lax.map(
        lambda inputs: attend_backward(*inputs),
        (queries, key_rows, values, segments, log_sums, grad_heads),
    )
    grad_q_pre = rotate_back(
        sensitivity_turned_asker.reshape(seqs_here, seq_length, head_count, HD),
        cos_table,
        sine_table,
    )
    grad_k_pre = rotate_back(grad_k_rot, cos_table, sine_table)
    query_key_value_gradient = jnp.concatenate(
        [
            grad_q_pre.reshape(seqs_here, seq_length, query_cols),
            grad_k_pre.reshape(seqs_here, seq_length, key_cols),
            grad_v_raw.reshape(seqs_here, seq_length, key_cols),
        ],
        -1,
    ).astype(jnp.bfloat16)
    grad_normed_one = jnp.einsum(
        "tex,bx->teb",
        query_key_value_gradient,
        query_key_value_weight,
        preferred_element_type=jnp.float32,
    )
    query_key_value_weight_gradient = jnp.einsum(
        "aqr,aqe->re",
        first_normalized,
        query_key_value_gradient,
        preferred_element_type=jnp.float32,
    )
    grad_query_w = query_key_value_weight_gradient[:, :query_cols]
    grad_key_w = query_key_value_weight_gradient[:, query_cols : query_cols + key_cols]
    grad_value_w = query_key_value_weight_gradient[:, query_cols + key_cols :]
    gain_one_terms = jnp.sum(gathered_one.astype(jnp.float32) * grad_normed_one, (0, 1)).reshape(
        dp_count, tp_count, -1
    )
    grad_scaled_one, gain_one_part = (
        lax.psum_scatter(
            (grad_normed_one * gain_one.astype(jnp.float32)).astype(jnp.bfloat16),
            "tensor",
            scatter_dimension=1,
            tiled=True,
        ).astype(jnp.float32),
        lax.psum_scatter(
            gain_one_terms.astype(jnp.bfloat16), "tensor", scatter_dimension=1, tiled=True
        ).astype(jnp.float32),
    )
    grad_tokens = (grad_residual + norm_backward(grad_scaled_one, unrounded_one, norm_one)).astype(
        jnp.bfloat16
    )
    attn_sums = (
        lax.psum_scatter(
            gain_one_part.astype(jnp.bfloat16), "dp", scatter_dimension=0, tiled=True
        ).astype(jnp.float32),
        lax.psum_scatter(
            grad_query_w.astype(jnp.bfloat16), "dp", scatter_dimension=0, tiled=True
        ).astype(jnp.float32),
        lax.psum_scatter(
            grad_key_w.astype(jnp.bfloat16), "dp", scatter_dimension=0, tiled=True
        ).astype(jnp.float32),
        lax.psum_scatter(
            grad_value_w.astype(jnp.bfloat16), "dp", scatter_dimension=0, tiled=True
        ).astype(jnp.float32),
        lax.psum_scatter(
            output_weight_gradient.astype(jnp.bfloat16), "dp", scatter_dimension=1, tiled=True
        ).astype(jnp.float32),
    )
    return (
        mixed,
        grad_tokens,
        attn_sums[0].reshape(-1),
        attn_sums[1],
        attn_sums[2],
        attn_sums[3],
        attn_sums[4],
        mlp_sums[0].reshape(-1),
        mlp_sums[1],
        mlp_sums[2],
        mlp_sums[3],
    )


def solution(mesh):
    placed = (
        P("dp", "tensor", None),
        P("dp", None),
        P("dp"),
        P("dp", "tensor"),
        P("dp", "tensor"),
        P("dp", "tensor"),
        P("tensor", "dp"),
        P("dp"),
        P("dp", "tensor"),
        P("dp", "tensor"),
        P("tensor", "dp"),
        P("dp", "tensor", None),
    )
    return jax.shard_map(
        shards,
        mesh=mesh,
        in_specs=placed,
        out_specs=(
            P("dp", "tensor", None),
            P("dp", "tensor", None),
            P(("dp", "tensor")),
            P("dp", "tensor"),
            P("dp", "tensor"),
            P("dp", "tensor"),
            P("tensor", "dp"),
            P(("dp", "tensor")),
            P("dp", "tensor"),
            P("dp", "tensor"),
            P("tensor", "dp"),
        ),
        check_vma=False,
    )
```

profile of v0, /device:TPU:0, one launch (start us, length us, event | category | flops | bytes accessed | tf_op | source)
XLA Modules:
  0.0 2299.2 jit_solution(12161724984487297327)
XLA Ops:
  54.0 141.7 %all-gather.12.cloned.1.call-done = bf16[2,1024,2048]{2,1,0:T(8,128)(2,1)} async-done(((bf16[2,256,2048]{2,1,0:T(8,128)(2,1)}), bf16[2,1024,2048]{2,1,0:T(8,128)(2,1)}) %all-gather.12.cloned.1.call-update) | async-done | bytes 8388624 | tf_op jit(solution)/shard_map/all_gather | solution.py:144
  209.7 72.5 %while.28 = (s32[]{:T(128)}, bf16[2,1024,2,4,64]{1,4,3,2,0:T(8,128)(2,1)}, f32[2,2,4,1024,1]{3,2,1,4,0:T(4,128)}, bf16[2,1024,2,64]{1,3,2,0:T(8,128)(2,1)S(1)}, ...) while((s32[]{:T(128)}, ...), condition=%wide.region_6.7_spmd.clone, body=%wide.region_1.6_spmd.sunk.clone | while | flops 2253390336 | bytes 127236784 | solution.py:166
  296.6 278.2 %reduce-scatter.12.cloned.1.call-done = f32[2,256,2048]{2,1,0:T(8,128)} async-done(((f32[2,1024,2048]{2,1,0:T(8,128)}), f32[2,256,2048]{2,1,0:T(8,128)}) %reduce-scatter.12.cloned.1.call-update) | async-done | bytes 4194320 | tf_op jit(solution)/shard_map/reduce_scatter | solution.py:173
  591.5 40.3 %all-gather.22.cloned.1.call-done = bf16[2048,2048]{1,0:T(8,128)(2,1)} async-done(((bf16[256,2048]{1,0:T(8,128)(2,1)}), bf16[2048,2048]{1,0:T(8,128)(2,1)}) %all-gather.22.cloned.1.call-update) | async-done | bytes 8388624 | tf_op jit(solution)/shard_map/all_gather | solution.py:179
  631.9 151.7 %all-gather.18.cloned.1.call-done = bf16[2,1024,2048]{2,1,0:T(8,128)(2,1)} async-done(((bf16[2,256,2048]{2,1,0:T(8,128)(2,1)}), bf16[2,1024,2048]{2,1,0:T(8,128)(2,1)}) %all-gather.18.cloned.1.call-update) | async-done | bytes 8388624 | tf_op jit(solution)/shard_map/all_gather | solution.py:184
  783.6 24.5 %fusion.141 = f32[2,1024,2048]{2,1,0:T(8,128)} fusion(bf16[2048,2048]{1,0:T(8,128)(2,1)} %all-gather.22.cloned.1.call-done, bf16[2,1024,2048]{2,1,0:T(8,128)(2,1)} %all-gather.18.cloned.1.call-done, f32[2048]{0:T(1024)S(1)} %bitcast.624), kind=kOutput, calls=%fused_computation.170 | convolution fusion | flops 17192452096 | bytes 33562624 | tf_op jit(solution)/shard_map/vcx,xk->vck/dot_general | solution.py:194
  808.1 30.2 %all-gather.20.cloned.1.call-done = bf16[2048,2048]{1,0:T(8,128)(2,1)} async-done(((bf16[256,2048]{1,0:T(8,128)(2,1)}), bf16[2048,2048]{1,0:T(8,128)(2,1)}) %all-gather.20.cloned.1.call-update) | async-done | bytes 8388624 | tf_op jit(solution)/shard_map/all_gather | solution.py:178
  862.5 127.1 %all-gather.26.cloned.1.call-done = bf16[2,1024,2048]{2,1,0:T(8,128)(2,1)} async-done(((bf16[2,256,2048]{2,1,0:T(8,128)(2,1)}), bf16[2,1024,2048]{2,1,0:T(8,128)(2,1)}) %all-gather.26.cloned.1.call-update) | async-done | bytes 8388624 | tf_op jit(solution)/shard_map/all_gather | solution.py:230
  989.6 56.2 %all-gather.24.cloned.1.call-done = bf16[2048,2048]{1,0:T(8,128)(2,1)} async-done(((bf16[2048,256]{1,0:T(8,128)(2,1)}), bf16[2048,2048]{1,0:T(8,128)(2,1)}) %all-gather.24.cloned.1.call-update) | async-done | bytes 8388624 | tf_op jit(solution)/shard_map/all_gather | solution.py:180
  1045.8 36.9 %multiply_convert_fusion.2 = (bf16[2,1024,2048]{2,1,0:T(8,128)(2,1)}, bf16[2,1024,2048]{2,1,0:T(8,128)(2,1)}, bf16[2,1024,2048]{2,1,0:T(8,128)(2,1)}) fusion(f32[2,1024,2048]{2,1,0:T(8,128)} %fusion.145, f32[2,1024,2048]{2,1,0:T(8,128)} %fusion.141, bf16[2,1024,2048]{2,1,0:T(8,128)(2,1)} %all-gather.26.cloned.1.call-done, ...), kind=kOutput, calls=%fused_computation.160 | convolution fusion | flops 17246978048 | bytes 75497472 | tf_op jit(solution)/shard_map/htc,qc->htq/dot_general | solution.py:231
  1107.0 27.8 %fusion.134 = (bf16[2048]{0:T(1024)(128)(2,1)}, bf16[2,1024,2048]{2,1,0:T(8,128)(2,1)}) fusion(bf16[2,1024,2048]{2,1,0:T(8,128)(2,1)} %all-gather.18.cloned.1.call-done, f32[2,1024,2048]{2,1,0:T(8,128)} %fusion.139, f32[2048]{0:T(1024)S(1)} %bitcast.626, bf16[2,1024,2048]{2,1,0:T(8,128)(2,1)} %get-tuple-element.165, ...), kind=kOutput, calls=%fused_computation.154 | convolution fusion | flops 17205032960 | bytes 50343936 | tf_op jit(solution)/shard_map/tkx,wx->tkw/dot_general | solution.py:238
  1134.9 144.6 %reduce-scatter.16.cloned.1.call-done = bf16[2,256,2048]{2,1,0:T(8,128)(2,1)} async-done(((bf16[2,1024,2048]{2,1,0:T(8,128)(2,1)}), bf16[2,256,2048]{2,1,0:T(8,128)(2,1)}) %reduce-scatter.16.cloned.1.call-update) | async-done | bytes 2097168 | tf_op jit(solution)/shard_map/reduce_scatter | solution.py:251
  1364.5 73.6 %all-gather.28.cloned.1.call-done = bf16[2,1024,2048]{2,1,0:T(8,128)(2,1)} async-done(((bf16[2,256,2048]{2,1,0:T(8,128)(2,1)}), bf16[2,1024,2048]{2,1,0:T(8,128)(2,1)}) %all-gather.28.cloned.1.call-update) | async-done | bytes 8388624 | tf_op jit(solution)/shard_map/all_gather | solution.py:290
  1447.2 342.4 %while.29 = (s32[]{:T(128)}, f32[2,1024,2,4,64]{1,4,3,2,0:T(8,128)}, f32[2,1024,2,64]{1,3,2,0:T(8,128)}, bf16[2,1024,2,64]{1,3,2,0:T(8,128)(2,1)}, bf16[2,1024,2...) while((s32[]{:T(128)}, ...), condition=%wide.region_15.16_spmd.clone, body=%wide.region_12.15_spmd.sunk.clone | while | flops 5590766080 | bytes 470749440 | solution.py:303
  1507.6 28.7 %fusion.287 = f32[512,2,4,64]{0,3,2,1:T(8,128)} fusion(f32[2,1024,512,4]{2,1,3,0:T(8,128)} %fusion.284, f32[2,1024,512,4]{2,1,3,0:T(8,128)} %fusion.285, f32[2,4,512]{2,1,0:T(4,128)S(1)} %copy-done.30, pred[512,1024]{0,1:T(8,128)(4,1)} %get-tuple-element.363, bf16[2,1024,2,64]{1,3,2,0:T(8,128)(2,1)S(1)} %get-tuple-element.424, s32[]{:T(128)S(6)} %copy.163), kind=kOutput, calls=%fused_computation.83.clone.1.clone | convolution fusion | flops 583013376 | bytes 69500928 | tf_op jit(solution)/shard_map/while/body/eval_jaxpr/gjqk,kgd->qgjd/dot_general | solution.py:88
  1545.7 25.8 %fusion.292 = f32[2,64,1024]{2,1,0:T(8,128)} fusion(f32[2,1024,512,4]{2,1,3,0:T(8,128)} %fusion.288, f32[2,1024,512,4]{2,1,3,0:T(8,128)} %copy-done, f32[2,4,512]{2,1,0:T(4,128)S(1)} %copy-done.29, pred[512,1024]{0,1:T(8,128)(4,1)} %get-tuple-element.365, bf16[2,1024,2,4,64]{1,4,3,2,0:T(8,128)(2,1)S(1)} %copy-done.7, s32[]{:T(128)S(6)} %copy.163), kind=kOutput, calls=%fused_computation.87.clone.1.clone | convolution fusion | flops 583013376 | bytes 69238784 | tf_op jit(solution)/shard_map/while/body/eval_jaxpr/gjqk,qgjd->kgd/dot_general | solution.py:90
  1571.5 27.5 %fusion.293 = f32[2,1024,2,64]{1,3,2,0:T(8,128)} fusion(f32[2,1024,2,64]{1,3,2,0:T(8,128)} %get-tuple-element.412, s32[]{:T(128)S(6)} %copy.163, f32[2,64,1024]{2,1,0:T(8,128)} %fusion.292, f32[2,1024,512,4]{2,1,3,0:T(8,128)} %fusion.284, f32[2,1024,512,4]{2,1,3,0:T(8,128)} %fusion.285, f32[2,4,512]{2,1,0:T(4,128)S(1)} %copy-done.30, ...), kind=kOutput, calls=%fused_computation.89.clone.1.clone | convolution fusion | flops 583144448 | bytes 69764608 | tf_op jit(solution)/shard_map/while/body/eval_jaxpr/gjqk,qgjd->kgd/dot_general | solution.py:90
  1599.0 26.8 %fusion.290 = f32[512,2,4,64]{0,3,2,1:T(8,128)S(1)} fusion(f32[2,1024,512,4]{2,1,3,0:T(8,128)} %fusion.288, f32[2,1024,512,4]{2,1,3,0:T(8,128)} %copy-done, f32[2,4,512]{2,1,0:T(4,128)S(1)} %copy-done.29, pred[512,1024]{0,1:T(8,128)(4,1)} %get-tuple-element.365, bf16[2,1024,2,64]{1,3,2,0:T(8,128)(2,1)S(1)} %get-tuple-element.424, s32[]{:T(128)S(6)} %copy.163), kind=kOutput, calls=%fused_computation.84.clone.1.clone | convolution fusion | flops 583013376 | bytes 69500928 | tf_op jit(solution)/shard_map/while/body/eval_jaxpr/gjqk,kgd->qgjd/dot_general | solution.py:88
  1670.9 24.5 %fusion.287 = f32[512,2,4,64]{0,3,2,1:T(8,128)} fusion(f32[2,1024,512,4]{2,1,3,0:T(8,128)} %fusion.284, f32[2,1024,512,4]{2,1,3,0:T(8,128)} %fusion.285, f32[2,4,512]{2,1,0:T(4,128)S(1)} %copy-done.30, pred[512,1024]{0,1:T(8,128)(4,1)} %get-tuple-element.363, bf16[2,1024,2,64]{1,3,2,0:T(8,128)(2,1)S(1)} %get-tuple-element.424, s32[]{:T(128)S(6)} %copy.163), kind=kOutput, calls=%fused_computation.83.clone.1.clone | convolution fusion | flops 583013376 | bytes 69500928 | tf_op jit(solution)/shard_map/while/body/eval_jaxpr/gjqk,kgd->qgjd/dot_general | solution.py:88
  1704.7 24.4 %fusion.292 = f32[2,64,1024]{2,1,0:T(8,128)} fusion(f32[2,1024,512,4]{2,1,3,0:T(8,128)} %fusion.288, f32[2,1024,512,4]{2,1,3,0:T(8,128)} %copy-done, f32[2,4,512]{2,1,0:T(4,128)S(1)} %copy-done.29, pred[512,1024]{0,1:T(8,128)(4,1)} %get-tuple-element.365, bf16[2,1024,2,4,64]{1,4,3,2,0:T(8,128)(2,1)S(1)} %copy-done.7, s32[]{:T(128)S(6)} %copy.163), kind=kOutput, calls=%fused_computation.87.clone.1.clone | convolution fusion | flops 583013376 | bytes 69238784 | tf_op jit(solution)/shard_map/while/body/eval_jaxpr/gjqk,qgjd->kgd/dot_general | solution.py:90
  1729.1 27.4 %fusion.293 = f32[2,1024,2,64]{1,3,2,0:T(8,128)} fusion(f32[2,1024,2,64]{1,3,2,0:T(8,128)} %get-tuple-element.412, s32[]{:T(128)S(6)} %copy.163, f32[2,64,1024]{2,1,0:T(8,128)} %fusion.292, f32[2,1024,512,4]{2,1,3,0:T(8,128)} %fusion.284, f32[2,1024,512,4]{2,1,3,0:T(8,128)} %fusion.285, f32[2,4,512]{2,1,0:T(4,128)S(1)} %copy-done.30, ...), kind=kOutput, calls=%fused_computation.89.clone.1.clone | convolution fusion | flops 583144448 | bytes 69764608 | tf_op jit(solution)/shard_map/while/body/eval_jaxpr/gjqk,qgjd->kgd/dot_general | solution.py:90
  1946.7 43.6 %reduce-scatter.20.cloned.1.call-done = bf16[256,512]{1,0:T(8,128)(2,1)} async-done(((bf16[2048,512]{1,0:T(8,128)(2,1)}), bf16[256,512]{1,0:T(8,128)(2,1)}) %reduce-scatter.20.cloned.1.call-update) | async-done | bytes 262160 | tf_op jit(solution)/shard_map/reduce_scatter | solution.py:357
  1992.1 145.1 %reduce-scatter.18.cloned.1.call-done = bf16[2,256,2048]{2,1,0:T(8,128)(2,1)} async-done(((bf16[2,1024,2048]{2,1,0:T(8,128)(2,1)}), bf16[2,256,2048]{2,1,0:T(8,128)(2,1)}) %reduce-scatter.18.cloned.1.call-update) | async-done | bytes 2097168 | tf_op jit(solution)/shard_map/reduce_scatter | solution.py:340
  2139.6 145.0 %reduce-scatter.14.cloned.1.call-done = bf16[2,256,2048]{2,1,0:T(8,128)(2,1)} async-done(((bf16[2,1024,2048]{2,1,0:T(8,128)(2,1)}), bf16[2,256,2048]{2,1,0:T(8,128)(2,1)}) %reduce-scatter.14.cloned.1.call-update) | async-done | bytes 2097168 | tf_op jit(solution)/shard_map/reduce_scatter | solution.py:204
  (298 shorter events, 606.8 us)
Async XLA Ops:
  7.2 46.8 %all-gather.14.cloned.1.call-start = ((), (), s32[]{:S(2)}) async-start(), calls=%async_computation.12 | async-start | bytes 2359296 | tf_op jit(solution)/shard_map/all_gather | solution.py:133
  9.1 186.7 %all-gather.12.cloned.1.call-start = ((), (), s32[]{:S(2)}) async-start(), calls=%async_computation.11 | async-start | bytes 10485760 | tf_op jit(solution)/shard_map/all_gather | solution.py:144
  15.2 267.1 %all-gather.16.cloned.1.call-start = ((), (), s32[]{:S(2)}) async-start(), calls=%async_computation.13 | async-start | bytes 2359296 | tf_op jit(solution)/shard_map/all_gather | solution.py:136
  15.9 558.9 %reduce-scatter.12.cloned.1.call-start = ((), (), s32[]{:S(2)}) async-start(), calls=%async_computation.14 | async-start | bytes 20971520 | tf_op jit(solution)/shard_map/reduce_scatter | solution.py:173
  296.0 278.8 %copy-start.1 = (bf16[2,256,2048]{2,1,0:T(8,128)(2,1)S(1)}, bf16[2,256,2048]{2,1,0:T(8,128)(2,1)}, u32[]{:S(2)}) copy-start(bf16[2,256,2048]{2,1,0:T(8,128)(2,1)} %param.16) | copy-start | bytes 6291460
  296.0 335.9 %all-gather.22.cloned.1.call-start = ((), (), s32[]{:S(2)}) async-start(), calls=%async_computation.17 | async-start | bytes 9437184 | tf_op jit(solution)/shard_map/all_gather | solution.py:179
  296.6 487.0 %all-gather.18.cloned.1.call-start = ((), (), s32[]{:S(2)}) async-start(), calls=%async_computation.15 | async-start | bytes 10485760 | tf_op jit(solution)/shard_map/all_gather | solution.py:184
  580.3 258.0 %all-gather.20.cloned.1.call-start = ((), (), s32[]{:S(2)}) async-start(), calls=%async_computation.16 | async-start | bytes 9437184 | tf_op jit(solution)/shard_map/all_gather | solution.py:178
  581.1 408.5 %all-gather.26.cloned.1.call-start = ((), (), s32[]{:S(2)}) async-start(), calls=%async_computation.20 | async-start | bytes 10485760 | tf_op jit(solution)/shard_map/all_gather | solution.py:230
  581.8 464.0 %all-gather.24.cloned.1.call-start = ((), (), s32[]{:S(2)}) async-start(), calls=%async_computation.18 | async-start | bytes 9437184 | tf_op jit(solution)/shard_map/all_gather | solution.py:180
  582.5 696.9 %reduce-scatter.16.cloned.1.call-start = ((), (), s32[]{:S(2)}) async-start(), calls=%async_computation.21 | async-start | bytes 10485760 | tf_op jit(solution)/shard_map/reduce_scatter | solution.py:251
  1134.9 303.2 %all-gather.28.cloned.1.call-start = ((), (), s32[]{:S(2)}) async-start(), calls=%async_computation.22 | async-start | bytes 10485760 | tf_op jit(solution)/shard_map/all_gather | solution.py:290
  1287.5 592.3 %reduce-scatter.32.cloned.1.call-start = ((), (), s32[]{:S(2)}) async-start(), calls=%async_computation.30 | async-start | bytes 9437184 | tf_op jit(solution)/shard_map/reduce_scatter | solution.py:286
  1311.3 571.3 %reduce-scatter.30.cloned.1.call-start = ((), (), s32[]{:S(2)}) async-start(), calls=%async_computation.29 | async-start | bytes 9437184 | tf_op jit(solution)/shard_map/reduce_scatter | solution.py:283
  1335.5 549.9 %reduce-scatter.28.cloned.1.call-start = ((), (), s32[]{:S(2)}) async-start(), calls=%async_computation.28 | async-start | bytes 9437184 | tf_op jit(solution)/shard_map/reduce_scatter | solution.py:280
  1364.4 556.2 %reduce-scatter.22.cloned.1.call-start = ((), (), s32[]{:S(2)}) async-start(), calls=%async_computation.25 | async-start | bytes 589824 | tf_op jit(solution)/shard_map/reduce_scatter | solution.py:360
  1828.7 93.5 %reduce-scatter.24.cloned.1.call-start = ((), (), s32[]{:S(2)}) async-start(), calls=%async_computation.26 | async-start | bytes 589824 | tf_op jit(solution)/shard_map/reduce_scatter | solution.py:363
  1829.3 115.6 %reduce-scatter.26.cloned.1.call-start = ((), (), s32[]{:S(2)}) async-start(), calls=%async_computation.27 | async-start | bytes 2359296 | tf_op jit(solution)/shard_map/reduce_scatter | solution.py:366
  1839.2 151.1 %reduce-scatter.20.cloned.1.call-start = ((), (), s32[]{:S(2)}) async-start(), calls=%async_computation.24 | async-start | bytes 2359296 | tf_op jit(solution)/shard_map/reduce_scatter | solution.py:357
  1840.8 296.4 %reduce-scatter.18.cloned.1.call-start = ((), (), s32[]{:S(2)}) async-start(), calls=%async_computation.23 | async-start | bytes 10485760 | tf_op jit(solution)/shard_map/reduce_scatter | solution.py:340
  1854.3 430.3 %reduce-scatter.14.cloned.1.call-start = ((), (), s32[]{:S(2)}) async-start(), calls=%async_computation.19 | async-start | bytes 10485760 | tf_op jit(solution)/shard_map/reduce_scatter | solution.py:204
  1877.9 259.2 %copy-start.3 = (bf16[2,256,2048]{2,1,0:T(8,128)(2,1)S(1)}, bf16[2,256,2048]{2,1,0:T(8,128)(2,1)}, u32[]{:S(2)}) copy-start(bf16[2,256,2048]{2,1,0:T(8,128)(2,1)} %param.16) | copy-start | bytes 6291460
  1878.0 406.6 %copy-start.35 = (f32[2,256]{1,0:T(2,128)S(1)}, f32[2,256]{1,0:T(2,128)}, u32[]{:S(2)}) copy-start(f32[2,256]{1,0:T(2,128)} %copy-done.33) | copy-start | bytes 6148
  1878.0 406.6 %copy-start.39 = (f32[2,256]{1,0:T(2,128)S(1)}, f32[2,256]{1,0:T(2,128)}, u32[]{:S(2)}) copy-start(f32[2,256]{1,0:T(2,128)} %copy-done.38) | copy-start | bytes 6148
  (51 other events, 1967.0 us)
Sparse Core Ops, SparseCore 0:
  10.5 33.4 all-gather.13
  46.1 149.6 all-gather.11
  197.6 26.3 all-gather.15
  296.1 278.6 reduce-scatter.11
  576.7 55.1 all-gather.21
  633.9 149.6 all-gather.17
  785.6 52.5 all-gather.19
  839.9 149.6 all-gather.25
  991.6 54.1 all-gather.23
  1135.0 144.4 reduce-scatter.15
  1287.6 150.3 all-gather.27
  1441.8 69.4 reduce-scatter.31
  1514.7 71.2 reduce-scatter.29
  1589.7 71.2 reduce-scatter.27
  1828.8 33.7 reduce-scatter.21
  1865.8 34.0 reduce-scatter.23
  1903.7 41.2 reduce-scatter.25
  1949.0 41.2 reduce-scatter.19
  1992.6 144.4 reduce-scatter.17
  2139.4 145.1 reduce-scatter.13
where the time goes:
time: 2310 us; the launch traced here: 2300 us
  waiting for transfers between devices  1400 us (61%)
  matrix products  653 us (28%)
  other arithmetic  92.7 us (4%)
  blocking collectives  73.2 us (3%)
  local copies, waits for them, and re-layouts  35.9 us (2%)
  loops' own time  25.7 us (1%)
    reduce_scatter x1, waiting for transfers between devices, shards(): lax.psum_scatter(attention_parts, 'tensor', scatter_dimension=1, tiled=True)  278 us
    all_gather x1, waiting for transfers between devices, shards(): lax.all_gather(unrounded_two.astype(jnp.bfloat16), 'tensor', axis=1, tile...  152 us
    reduce_scatter x1, waiting for transfers between devices, shards(): lax.psum_scatter((grad_normed_one * gain_one.astype(jnp.float32)).astype(...  145 us
    reduce_scatter x1, waiting for transfers between devices, shards(): lax.psum_scatter(feedforward_parts.astype(jnp.bfloat16), 'tensor', scatte...  145 us
    reduce_scatter x1, waiting for transfers between devices, shards(): lax.psum_scatter((grad_normed_two * gain_two.astype(jnp.float32)).astype(...  145 us
    all_gather x1, waiting for transfers between devices, shards(): lax.all_gather(unrounded_one.astype(jnp.bfloat16), 'tensor', axis=1, tile...  142 us
    all_gather x1, waiting for transfers between devices, shards(): mixed_gradient = lax.all_gather(cotangent, 'tensor', axis=1, tiled=True)  127 us
    dot_general x4, matrix products, attend_backward(): jnp.einsum('gjqk,qgjd->kgd', grad_scores, query_block, preferred_element_...  105 us
  transfers between devices with their start and end apart: 20, of which 13 were waited for; matrix products, arithmetic and copies ran while one was open for 29% of the time, Pallas kernels for 0%

commit v1 on v0

v1 whole, which is shorter than its diff:
```python
import functools

import jax
import jax.numpy as jnp
from jax import lax
from jax.experimental import pallas as pl
from jax.experimental.pallas import tpu as pltpu
from jax.sharding import PartitionSpec as P

HD = 64
EPS = 1e-05
THETA = 500000.0
LOG2E = 1.4426950408889634
LANES = 128
PLANE = 4
f32 = jnp.float32
bf16 = jnp.bfloat16


def call(body, flops, moved, vmem=50, **kw):
    return pl.pallas_call(
        body,
        compiler_params=pltpu.CompilerParams(vmem_limit_bytes=vmem * 2**20),
        cost_estimate=pl.CostEstimate(flops=flops, bytes_accessed=moved, transcendentals=0),
        **kw,
    )


def nn(a, b):
    return jnp.dot(a, b, preferred_element_type=f32)


def nt(a, b):
    return lax.dot_general(a, b, (((1,), (1,)), ((), ())), preferred_element_type=f32)


def tn(a, b):
    return lax.dot_general(a, b, (((0,), (0,)), ((), ())), preferred_element_type=f32)


def swap_halves(x):
    lane = lax.broadcasted_iota(jnp.int32, x.shape, 1)
    return jnp.where(lane % HD < HD // 2, pltpu.roll(x, LANES - HD // 2, 1), pltpu.roll(x, HD // 2, 1))


def gather_keys(k_refs, v_refs, blocks):
    k = jnp.concatenate([k_refs[j][0] for j in range(blocks)], 0)
    v = jnp.concatenate([v_refs[j][0] for j in range(blocks)], 0)
    return k, v


def padded_rows(part, e):
    zero = jnp.zeros_like(part)
    return jnp.concatenate([part, zero] if e == 0 else [zero, part], 0)


def attend_blocks(blocks, group, q_ref, k_refs, v_refs, bias_ref, o_ref, lse_ref, qt_ref, ot_ref):
    span = q_ref.shape[0]
    n = blocks * span
    k, v = gather_keys(k_refs, v_refs, blocks)
    vt = v.T
    qt_ref[...] = q_ref[...].T
    factor = HD**-0.5 * LOG2E

    def step(i, carry):
        for e in range(2):
            head = e * group + i
            rows = pl.ds(pl.multiple_of(head * HD, HD), HD)
            scores = nn(k, padded_rows(qt_ref[rows, :], e))
            logits = scores * factor + bias_ref[0, :n, :]
            top = jnp.max(logits, 0, keepdims=True)
            weights = jnp.exp2(logits - top)
            total = jnp.sum(weights, 0, keepdims=True)
            out = nn(vt[e * HD : (e + 1) * HD], weights.astype(bf16))
            ot_ref[rows, :] = out * (1.0 / total)
            lse_ref[0, 0, pl.ds(head, 1), :] = top + jnp.log2(total)
        return carry

    lax.fori_loop(0, group, step, 0)
    o_ref[...] = ot_ref[...].T.astype(bf16)


def attend_kernel(count, group, place, *refs):
    q_ref, k_refs, v_refs = refs[0], refs[1 : 1 + count], refs[1 + count : 1 + 2 * count]
    rest = refs[1 + 2 * count :]
    for blocks in range(1, count + 1):

        @pl.when(place[0] == blocks - 1)
        def _(blocks=blocks):
            attend_blocks(blocks, group, q_ref, k_refs, v_refs, *rest)


def attend(place, queries, pairs, bias, span, group):
    rows, width = queries.shape
    count = len(pairs)
    seqs = rows // span
    kv_width = pairs[0].shape[2]
    tiles = kv_width // LANES
    wide = width // tiles
    in_specs = [pl.BlockSpec((span, wide), lambda b, p, s: (b, p))]
    for part in range(2):
        in_specs += [pl.BlockSpec((1, span, LANES), lambda b, p, s, part=part: (part, b, p))] * count
    in_specs.append(pl.BlockSpec((1, count * span, span), lambda b, p, s: (b, 0, 0)))
    heads = wide // HD
    spec = pltpu.PrefetchScalarGridSpec(
        num_scalar_prefetch=1,
        grid=(seqs, tiles),
        in_specs=in_specs,
        out_specs=[
            pl.BlockSpec((span, wide), lambda b, p, s: (b, p)),
            pl.BlockSpec((1, 1, heads, span), lambda b, p, s: (b, p, 0, 0)),
        ],
        scratch_shapes=[pltpu.VMEM((wide, span), bf16), pltpu.VMEM((wide, span), f32)],
    )
    return call(
        functools.partial(attend_kernel, count, group),
        flops=rows * width * span * count * 8,
        moved=rows * width * 4,
        grid_spec=spec,
        out_shape=[
            jax.ShapeDtypeStruct((rows, width), bf16),
            jax.ShapeDtypeStruct((seqs, tiles, heads, span), f32),
        ],
    )(place, queries, *pairs, *pairs, bias)


def unattend_blocks(
    blocks, count, group, q_ref, g_ref, k_refs, v_refs, bias_ref, lse_ref, cos_ref, sin_ref,
    dq_ref, dkv_ref, qt_ref, gt_ref, dqt_ref, dk_ref, dv_ref,
):
    span = q_ref.shape[0]
    n = blocks * span
    k, v = gather_keys(k_refs, v_refs, blocks)
    kt = k.T
    qt_ref[...] = q_ref[...].T
    gt_ref[...] = g_ref[...].T
    dk_ref[...] = jnp.zeros_like(dk_ref)
    dv_ref[...] = jnp.zeros_like(dv_ref)
    factor = HD**-0.5 * LOG2E
    lane = lax.broadcasted_iota(jnp.int32, (span, LANES), 1)

    def moved(tile, b, e):
        if b != e:
            tile = pltpu.roll(tile, HD, 1)
        return jnp.where((lane < HD) if e == 0 else (lane >= HD), tile, 0.0).astype(bf16)

    def step(i, carry):
        for e in range(2):
            tile_at = pl.ds(pl.multiple_of((e * (group // 2) + i) * LANES, LANES), LANES)
            q_tile = q_ref[:, tile_at].astype(f32)
            g_tile = g_ref[:, tile_at].astype(f32)
            all_ds, all_p = [], []
            for b in range(2):
                head = e * group + 2 * i + b
                rows = pl.ds(pl.multiple_of(head * HD, HD), HD)
                scores = nn(k, padded_rows(qt_ref[rows, :], e))
                lse = lse_ref[0, 0, pl.ds(head, 1), :]
                probs = jnp.exp2(scores * factor + bias_ref[0, :n, :] - lse)
                dp = nn(v, padded_rows(gt_ref[rows, :], e))
                delta = jnp.sum(probs * dp, 0, keepdims=True)
                ds = (probs * (dp - delta)).astype(bf16)
                dqt_ref[rows, :] = nn(kt[e * HD : (e + 1) * HD], ds)
                all_ds.append(ds)
                all_p.append(probs.astype(bf16))
            q_rows = jnp.concatenate([moved(q_tile, b, e) for b in range(2)], 0)
            g_rows = jnp.concatenate([moved(g_tile, b, e) for b in range(2)], 0)
            dk_ref[:n, :] += nn(jnp.concatenate(all_ds, 1), q_rows)
            dv_ref[:n, :] += nn(jnp.concatenate(all_p, 1), g_rows)
        return carry

    lax.fori_loop(0, group // 2, step, 0)
    scale = HD**-0.5
    dq = dqt_ref[...].T * scale
    for t in range(dq.shape[1] // LANES):
        part = dq[:, t * LANES : (t + 1) * LANES]
        dq_ref[:, t * LANES : (t + 1) * LANES] = (
            part * cos_ref[...] - swap_halves(part) * sin_ref[...]
        ).astype(bf16)
    for j in range(count):
        dkv_ref[j, 0] = (dk_ref[j * span : (j + 1) * span, :] * scale).astype(bf16)
        dkv_ref[j, 1] = dv_ref[j * span : (j + 1) * span, :].astype(bf16)


def unattend_kernel(count, group, place, *refs):
    q_ref, g_ref, k_refs, v_refs = refs[0], refs[1], refs[2 : 2 + count], refs[2 + count : 2 + 2 * count]
    rest = refs[2 + 2 * count :]
    for blocks in range(1, count + 1):

        @pl.when(place[0] == blocks - 1)
        def _(blocks=blocks):
            unattend_blocks(blocks, count, group, q_ref, g_ref, k_refs, v_refs, *rest)


def unattend(place, queries, grads, pairs, bias, lse, cos, sin, span, group):
    rows, width = queries.shape
    count = len(pairs)
    seqs = rows // span
    kv_width = pairs[0].shape[2]
    tiles = kv_width // LANES
    wide = width // tiles
    heads = wide // HD
    tall = pl.BlockSpec((span, wide), lambda b, p, s: (b, p))
    table = pl.BlockSpec((span, LANES), lambda b, p, s: (0, 0))
    in_specs = [tall, tall]
    for part in range(2):
        in_specs += [pl.BlockSpec((1, span, LANES), lambda b, p, s, part=part: (part, b, p))] * count
    in_specs += [
        pl.BlockSpec((1, count * span, span), lambda b, p, s: (b, 0, 0)),
        pl.BlockSpec((1, 1, heads, span), lambda b, p, s: (b, p, 0, 0)),
        table,
        table,
    ]
    spec = pltpu.PrefetchScalarGridSpec(
        num_scalar_prefetch=1,
        grid=(seqs, tiles),
        in_specs=in_specs,
        out_specs=[tall, pl.BlockSpec((count, 2, span, LANES), lambda b, p, s: (0, 0, b, p))],
        scratch_shapes=[
            pltpu.VMEM((wide, span), bf16),
            pltpu.VMEM((wide, span), bf16),
            pltpu.VMEM((wide, span), f32),
            pltpu.VMEM((count * span, LANES), f32),
            pltpu.VMEM((count * span, LANES), f32),
        ],
    )
    return call(
        functools.partial(unattend_kernel, count, group),
        flops=rows * width * span * count * 20,
        moved=rows * width * 8,
        grid_spec=spec,
        out_shape=[
            jax.ShapeDtypeStruct((rows, width), bf16),
            jax.ShapeDtypeStruct((count, 2, rows, kv_width), bf16),
        ],
    )(place, queries, grads, *pairs, *pairs, bias, lse, cos, sin)


def turn(y, cos, sin, out_ref, start=0):
    for t in range(y.shape[1] // LANES):
        part = y[:, t * LANES : (t + 1) * LANES]
        out_ref[:, t * LANES : (t + 1) * LANES] = (part * cos + swap_halves(part) * sin).astype(bf16)


def project_pairs(normed, weights, cos, sin, depth):
    rows, width = normed.shape
    parts, shards, _, cols = weights.shape
    half = cols // 2

    def body(x_ref, w_ref, cos_ref, sin_ref, o_ref):
        w = w_ref[:, 0, :depth, :].reshape(parts * depth, cols)
        y = nn(x_ref[...], w)
        k = y[:, :half]
        o_ref[0] = (k * cos_ref[...] + swap_halves(k) * sin_ref[...]).astype(bf16)
        o_ref[1] = y[:, half:].astype(bf16)

    whole = lambda s: (0, 0)
    return call(
        body,
        flops=2 * rows * width * shards * cols,
        moved=weights.size * 2 + normed.size * 2,
        grid=(shards,),
        in_specs=[
            pl.BlockSpec((rows, width), whole),
            pl.BlockSpec((parts, 1, weights.shape[2], cols), lambda s: (0, s, 0, 0)),
            pl.BlockSpec((rows, LANES), whole),
            pl.BlockSpec((rows, LANES), whole),
        ],
        out_specs=pl.BlockSpec((2, rows, half), lambda s: (0, 0, s)),
        out_shape=jax.ShapeDtypeStruct((2, rows, half * shards), bf16),
    )(normed, weights, cos, sin)


def project_queries(normed, weights, cos, sin):
    rows, width = normed.shape
    parts, shards, depth, cols = weights.shape

    def body(x_ref, w_ref, cos_ref, sin_ref, o_ref):
        y = nn(x_ref[...], w_ref[:, 0].reshape(parts * depth, cols))
        turn(y, cos_ref[...], sin_ref[...], o_ref)

    whole = lambda s: (0, 0)
    return call(
        body,
        flops=2 * rows * width * shards * cols,
        moved=weights.size * 2 + normed.size * 2,
        grid=(shards,),
        in_specs=[
            pl.BlockSpec((rows, width), whole),
            pl.BlockSpec((parts, 1, depth, cols), lambda s: (0, s, 0, 0)),
            pl.BlockSpec((rows, LANES), whole),
            pl.BlockSpec((rows, LANES), whole),
        ],
        out_specs=pl.BlockSpec((rows, cols), lambda s: (0, s)),
        out_shape=jax.ShapeDtypeStruct((rows, cols * shards), bf16),
    )(normed, weights, cos, sin)


def project_out(heads_out, weights, tokens):
    rows, width = heads_out.shape
    parts, shards, depth, cols = weights.shape

    def body(x_ref, w_ref, t_ref, o_ref):
        y = nn(x_ref[...], w_ref[0].reshape(shards * depth, cols))
        o_ref[...] = t_ref[...].astype(f32) + y

    tile = pl.BlockSpec((rows, cols), lambda s: (0, s))
    return call(
        body,
        flops=2 * rows * width * parts * cols,
        moved=weights.size * 2 + rows * width * 8,
        grid=(parts,),
        in_specs=[
            pl.BlockSpec((rows, width), lambda s: (0, 0)),
            pl.BlockSpec((1, shards, depth, cols), lambda s: (s, 0, 0, 0)),
            tile,
        ],
        out_specs=tile,
        out_shape=jax.ShapeDtypeStruct((rows, cols * parts), f32),
    )(heads_out, weights, tokens)


def unproject_out(grads, weights):
    rows, width = grads.shape
    parts, shards, depth, cols = weights.shape

    def body(x_ref, w_ref, o_ref):
        w = jnp.concatenate([w_ref[i, 0] for i in range(parts)], 1)
        o_ref[...] = nt(x_ref[...], w).astype(bf16)

    return call(
        body,
        flops=2 * rows * width * shards * depth,
        moved=weights.size * 2 + rows * width * 4,
        grid=(shards,),
        in_specs=[
            pl.BlockSpec((rows, width), lambda s: (0, 0)),
            pl.BlockSpec((parts, 1, depth, cols), lambda s: (0, s, 0, 0)),
        ],
        out_specs=pl.BlockSpec((rows, depth), lambda s: (0, s)),
        out_shape=jax.ShapeDtypeStruct((rows, depth * shards), bf16),
    )(grads, weights)


def unproject_in(dq, dkv, w_q, w_kv):
    rows, width = dq.shape
    parts, shards, depth, cols = w_q.shape
    thin = w_kv.shape[3] // 2

    def body(q_ref, kv_ref, wq_ref, wkv_ref, o_ref):
        total = jnp.zeros((rows, depth), f32)
        for s in range(shards):
            left = jnp.concatenate(
                [
                    q_ref[:, s * cols : (s + 1) * cols],
                    kv_ref[0, :, s * thin : (s + 1) * thin],
                    kv_ref[1, :, s * thin : (s + 1) * thin],
                ],
                1,
            )
            total += nt(left, jnp.concatenate([wq_ref[0, s], wkv_ref[0, s, :depth, :]], 1))
        o_ref[...] = total

    return call(
        body,
        flops=2 * rows * parts * depth * shards * (cols + 2 * thin),
        moved=(w_q.size + w_kv.size) * 2 + rows * width * 6,
        grid=(parts,),
        in_specs=[
            pl.BlockSpec((rows, width), lambda s: (0, 0)),
            pl.BlockSpec(dkv.shape, lambda s: (0, 0, 0)),
            pl.BlockSpec((1, shards, depth, cols), lambda s: (s, 0, 0, 0)),
            pl.BlockSpec((1, shards, w_kv.shape[2], 2 * thin), lambda s: (s, 0, 0, 0)),
        ],
        out_specs=pl.BlockSpec((rows, depth), lambda s: (0, s)),
        out_shape=jax.ShapeDtypeStruct((rows, parts * depth), f32),
    )(dq, dkv, w_q, w_kv)


def query_weight_grad(normed, dq, parts, shards):
    rows, width = normed.shape
    depth, cols = width // parts, dq.shape[1] // shards

    def body(x_ref, y_ref, o_ref):
        total = tn(x_ref[...], y_ref[...])
        for s in range(shards):
            o_ref[0, s] = total[:, s * cols : (s + 1) * cols].astype(bf16)

    return call(
        body,
        flops=2 * rows * width * dq.shape[1],
        moved=rows * width * 4 + width * dq.shape[1] * 2,
        grid=(parts,),
        in_specs=[
            pl.BlockSpec((rows, depth), lambda s: (0, s)),
            pl.BlockSpec(dq.shape, lambda s: (0, 0)),
        ],
        out_specs=pl.BlockSpec((1, shards, depth, cols), lambda s: (s, 0, 0, 0)),
        out_shape=jax.ShapeDtypeStruct((parts, shards, depth, cols), bf16),
    )(normed, dq)


def pair_weight_grad(normed, dkv, gains, parts, shards):
    rows, width = normed.shape
    depth, thin = width // parts, dkv.shape[2] // shards
    extra = gains.shape[1]

    def body(x_ref, y_ref, g_ref, o_ref):
        dk, dv = tn(x_ref[...], y_ref[0]), tn(x_ref[...], y_ref[1])
        for s in range(shards):
            o_ref[0, s, :depth, :thin] = dk[:, s * thin : (s + 1) * thin].astype(bf16)
            o_ref[0, s, :depth, thin:] = dv[:, s * thin : (s + 1) * thin].astype(bf16)
            o_ref[0, s, depth:, :] = g_ref[0].astype(bf16)

    return call(
        body,
        flops=4 * rows * width * dkv.shape[2],
        moved=rows * width * 4 + width * dkv.shape[2] * 4,
        grid=(parts,),
        in_specs=[
            pl.BlockSpec((rows, depth), lambda s: (0, s)),
            pl.BlockSpec(dkv.shape, lambda s: (0, 0, 0)),
            pl.BlockSpec((1, extra, depth), lambda s: (s, 0, 0)),
        ],
        out_specs=pl.BlockSpec((1, shards, depth + extra, 2 * thin), lambda s: (s, 0, 0, 0)),
        out_shape=jax.ShapeDtypeStruct((parts, shards, depth + extra, 2 * thin), bf16),
    )(normed, dkv, gains)


def out_weight_grad(heads_out, grads, parts, shards):
    rows, width = grads.shape
    cols, depth = width // parts, heads_out.shape[1] // shards

    def body(x_ref, y_ref, o_ref):
        total = tn(x_ref[...], y_ref[...])
        for i in range(parts):
            o_ref[i, 0] = total[:, i * cols : (i + 1) * cols].astype(bf16)

    return call(
        body,
        flops=2 * rows * width * heads_out.shape[1],
        moved=rows * width * 4 + width * heads_out.shape[1] * 2,
        grid=(shards,),
        in_specs=[
            pl.BlockSpec((rows, depth), lambda s: (0, s)),
            pl.BlockSpec((rows, width), lambda s: (0, 0)),
        ],
        out_specs=pl.BlockSpec((parts, 1, depth, cols), lambda s: (0, s, 0, 0)),
        out_shape=jax.ShapeDtypeStruct((parts, shards, depth, cols), bf16),
    )(heads_out, grads)


def finish_pairs(own, come, cos, sin):
    _, rows, width = own.shape

    def body(a_ref, b_ref, cos_ref, sin_ref, o_ref):
        total = a_ref[...].astype(f32) + b_ref[...].astype(f32)
        k = total[0]
        o_ref[0] = (k * cos_ref[...] - swap_halves(k) * sin_ref[...]).astype(bf16)
        o_ref[1] = total[1].astype(bf16)

    tile = pl.BlockSpec((2, rows, LANES), lambda s: (0, 0, s))
    table = pl.BlockSpec((rows, LANES), lambda s: (0, 0))
    return call(
        body,
        flops=own.size * 6,
        moved=own.size * 6,
        grid=(width // LANES,),
        in_specs=[tile, tile, table, table],
        out_specs=tile,
        out_shape=jax.ShapeDtypeStruct(own.shape, bf16),
    )(own, come, cos, sin)


def gate_up(x, w_gate, w_up):
    rows, width = x.shape
    shards, _, cols = w_gate.shape
    tall = min(512, rows)

    def body(x_ref, g_ref, u_ref, go_ref, uo_ref, i_ref):
        left = x_ref[...]
        gate, up = nn(left, g_ref[0]), nn(left, u_ref[0])
        go_ref[...] = gate.astype(bf16)
        uo_ref[...] = up.astype(bf16)
        i_ref[...] = (gate / (1.0 + jnp.exp(-gate)) * up).astype(bf16)

    weight = pl.BlockSpec((1, width, cols), lambda s, m: (s, 0, 0))
    tile = pl.BlockSpec((tall, cols), lambda s, m: (m, s))
    shape = jax.ShapeDtypeStruct((rows, shards * cols), bf16)
    return call(
        body,
        flops=4 * rows * width * shards * cols,
        moved=w_gate.size * 4 + rows * width * 10,
        grid=(shards, rows // tall),
        in_specs=[pl.BlockSpec((tall, width), lambda s, m: (m, 0)), weight, weight],
        out_specs=[tile] * 3,
        out_shape=[shape] * 3,
    )(x, w_gate, w_up)


def inner_grads(g, w_down, gate, up):
    rows, width = g.shape
    shards, cols, _ = w_down.shape
    tall = min(512, rows)

    def body(x_ref, w_ref, g_ref, u_ref, dg_ref, du_ref):
        grad = nt(x_ref[...], w_ref[0])
        gate, up = g_ref[...].astype(f32), u_ref[...].astype(f32)
        s = 1.0 / (1.0 + jnp.exp(-gate))
        dg_ref[...] = (grad * up * s * (1.0 + gate * (1.0 - s))).astype(bf16)
        du_ref[...] = (grad * gate * s).astype(bf16)

    tile = pl.BlockSpec((tall, cols), lambda s, m: (m, s))
    shape = jax.ShapeDtypeStruct((rows, shards * cols), bf16)
    return call(
        body,
        flops=2 * rows * width * shards * cols,
        moved=w_down.size * 2 + rows * width * 10,
        grid=(shards, rows // tall),
        in_specs=[
            pl.BlockSpec((tall, width), lambda s, m: (m, 0)),
            pl.BlockSpec((1, cols, width), lambda s, m: (s, 0, 0)),
            tile,
            tile,
        ],
        out_specs=[tile] * 2,
        out_shape=[shape] * 2,
    )(g, w_down, gate, up)


def down(inner, w_down):
    rows, width = inner.shape
    cols = w_down.shape[2]
    wide = 512
    tall = min(512, rows)

    def body(x_ref, w_ref, o_ref):
        o_ref[...] = nn(x_ref[...], w_ref[...]).astype(bf16)

    return call(
        body,
        flops=2 * rows * width * cols,
        moved=w_down.size * 2 + rows * width * 4,
        grid=(cols // wide, rows // tall),
        in_specs=[
            pl.BlockSpec((tall, width), lambda n, m: (m, 0)),
            pl.BlockSpec((width, wide), lambda n, m: (0, n)),
        ],
        out_specs=pl.BlockSpec((tall, wide), lambda n, m: (m, n)),
        out_shape=jax.ShapeDtypeStruct((rows, cols), bf16),
    )(inner, w_down.reshape(width, cols))


def normed_grads(d_gate, d_up, w_gate, w_up):
    rows, width = d_gate.shape
    shards, depth, cols = w_gate.shape
    wide = 512
    tall = min(512, rows)

    def body(g_ref, u_ref, wg_ref, wu_ref, o_ref):
        total = jnp.zeros((tall, wide), f32)
        for d_ref, w_ref in ((g_ref, wg_ref), (u_ref, wu_ref)):
            total += nt(d_ref[...], jnp.concatenate([w_ref[s] for s in range(shards)], 1))
        o_ref[...] = total.astype(bf16)

    weight = pl.BlockSpec((shards, wide, cols), lambda n, m: (0, n, 0))
    left = pl.BlockSpec((tall, width), lambda n, m: (m, 0))
    return call(
        body,
        flops=4 * rows * width * depth,
        moved=w_gate.size * 4 + rows * width * 6,
        grid=(depth // wide, rows // tall),
        in_specs=[left, left, weight, weight],
        out_specs=pl.BlockSpec((tall, wide), lambda n, m: (m, n)),
        out_shape=jax.ShapeDtypeStruct((rows, depth), bf16),
    )(d_gate, d_up, w_gate, w_up)


def column_weight_grad(xs, ys, shards):
    rows, width = xs[0].shape
    cols = ys[0].shape[1] // shards
    depth = width // PLANE // 2
    count = len(xs)

    def body(*refs):
        x_refs, y_refs, o_ref, xt_ref = refs[:count], refs[count : 2 * count], refs[2 * count], refs[-1]

        @pl.when(pl.program_id(1) == 0)
        def _():
            for j in range(count):
                xt_ref[:, j * rows : (j + 1) * rows] = x_refs[j][...].T

        y = jnp.concatenate([r[...] for r in y_refs], 0)
        for core in range(2):
            o_ref[core, 0, 0] = nn(xt_ref[core * depth : (core + 1) * depth, :], y).astype(bf16)

    return call(
        body,
        flops=2 * count * rows * width * shards * cols,
        moved=count * rows * width * 6 + width * shards * cols * 2,
        grid=(PLANE, shards),
        in_specs=[pl.BlockSpec((rows, 2 * depth), lambda q, s: (0, q))] * count
        + [pl.BlockSpec((rows, cols), lambda q, s: (0, s))] * count,
        out_specs=pl.BlockSpec((2, 1, 1, depth, cols), lambda q, s: (0, s, q, 0, 0)),
        out_shape=jax.ShapeDtypeStruct((2, shards, PLANE, depth, cols), bf16),
        scratch_shapes=[pltpu.VMEM((2 * depth, count * rows), bf16)],
    )(*xs, *ys)


def row_weight_grad(xs, ys, shards):
    rows, width = ys[0].shape
    tall = xs[0].shape[1] // shards
    depth = width // PLANE // 2
    count = len(xs)

    def body(*refs):
        x_refs, y_refs, o_ref, xt_ref = refs[:count], refs[count : 2 * count], refs[2 * count], refs[-1]

        @pl.when(pl.program_id(1) == 0)
        def _():
            for j in range(count):
                xt_ref[:, j * rows : (j + 1) * rows] = x_refs[j][...].T

        total = nn(xt_ref[...], jnp.concatenate([r[...] for r in y_refs], 0)).astype(bf16)
        for core in range(2):
            o_ref[core, 0] = total[:, core * depth : (core + 1) * depth]

    return call(
        body,
        flops=2 * count * rows * width * shards * tall,
        moved=count * rows * width * 6 + width * shards * tall * 2,
        grid=(shards, PLANE),
        in_specs=[pl.BlockSpec((rows, tall), lambda s, q: (0, s))] * count
        + [pl.BlockSpec((rows, 2 * depth), lambda s, q: (0, q))] * count,
        out_specs=pl.BlockSpec((2, 1, tall, depth), lambda s, q: (0, s, 0, q)),
        out_shape=jax.ShapeDtypeStruct((2, shards, tall, PLANE * depth), bf16),
        scratch_shapes=[pltpu.VMEM((tall, count * rows), bf16)],
    )(*xs, *ys)


def hop(a, bits):
    n = lax.axis_size("dp")
    return lax.ppermute(a, "dp", [(i, i ^ bits) for i in range(n)])


def climb(a, step):
    n = lax.axis_size("tensor")
    return lax.ppermute(a, "tensor", [(i, i + step) for i in range(n) if 0 <= i + step < n])


def plane_gather(a):
    half = a.shape[0] // 2
    by_x, by_y = hop(a, 2), hop(a, 4)
    far = jnp.concatenate([hop(by_x[:half], 4), hop(by_y[half:], 2)], 0)
    return a, by_x, by_y, far


def added(a, b):
    return (a.astype(f32) + b.astype(f32)).astype(a.dtype)


def plane_scatter(own, to_x, to_y, far):
    half = own.shape[0] // 2
    first, second = hop(far[:half], 2), hop(far[half:], 4)
    to_y = jnp.concatenate([added(to_y[:half], first), to_y[half:]], 0)
    to_x = jnp.concatenate([to_x[:half], added(to_x[half:], second)], 0)
    return own.astype(f32) + hop(to_x, 2).astype(f32) + hop(to_y, 4).astype(f32)


def by_chip(parts, chip):
    a, b, c, d = parts
    odd = (chip & 1) == 1
    a, b, c, d = (
        jnp.where(odd, b, a),
        jnp.where(odd, a, b),
        jnp.where(odd, d, c),
        jnp.where(odd, c, d),
    )
    high = (chip & 2) == 2
    return (
        jnp.where(high, c, a),
        jnp.where(high, d, b),
        jnp.where(high, a, c),
        jnp.where(high, b, d),
    )


def trade(pieces, axis, chip):
    come = []
    for r in range(PLANE):
        piece = lax.dynamic_index_in_dim(pieces, chip ^ r, axis, keepdims=False)
        come.append(piece if r == 0 else hop(piece, 2 * r))
    return by_chip(come, chip)


def sum_all(blocks, chip, core):
    parts, shards = blocks.shape[:2]
    pairs = blocks.reshape((parts // 2, 2) + blocks.shape[1:])
    come = hop(lax.dynamic_index_in_dim(pairs, 1 - core, 1, keepdims=False), 1)
    mine = added(lax.dynamic_index_in_dim(pairs, core, 1, keepdims=False), come)
    own = [lax.dynamic_index_in_dim(mine, chip ^ r, 0, keepdims=False) for r in range(PLANE)]
    total = plane_scatter(*own).astype(bf16)
    return lax.psum_scatter(total, "tensor", scatter_dimension=0, tiled=False)


def rotary_tables(positions):
    half_size = HD // 2
    frequency = THETA ** (-2.0 * jnp.arange(half_size, dtype=f32) / HD)
    angles = positions.astype(f32)[:, None] * frequency[None, :]
    cos, sin = jnp.cos(angles), jnp.sin(angles)
    return (
        jnp.concatenate([cos, cos] * (LANES // HD), -1),
        jnp.concatenate([-sin, sin] * (LANES // HD), -1),
    )


def norm_backward(grad_scaled, unrounded, norm_scale):
    return norm_scale * (grad_scaled - unrounded * jnp.mean(unrounded * grad_scaled, -1, keepdims=True))


def shards(
    tokens, segments, attn_norm, w_query, w_key, w_value, w_out, mlp_norm, w_gate, w_up, w_down, cotangent
):
    dp_count, tp_count = lax.axis_size("dp"), lax.axis_size("tensor")
    groups = dp_count // 8
    place = lax.axis_index("tensor")
    index = lax.axis_index("dp")
    core, chip = index & 1, (index >> 1) & 3
    seqs, span, width = tokens.shape
    rows = seqs * span
    block = width // 8

    group_sets = [[g * 8 + l for g in range(groups)] for l in range(8)]

    def widen(a, axis):
        if groups == 1:
            return a
        return lax.all_gather(a, "dp", axis=axis, tiled=True, axis_index_groups=group_sets)

    def narrow(a, axis):
        if groups == 1:
            return a
        return lax.psum_scatter(
            a.astype(bf16), "dp", scatter_dimension=axis, tiled=True, axis_index_groups=group_sets
        )

    def inward(a):
        if groups == 1:
            return a
        lead = a.shape[:-1]
        return jnp.swapaxes(a.reshape(lead + (groups, 8, -1)), -3, -2).reshape(lead + (-1,))

    def outward(a):
        if groups == 1:
            return a
        lead = a.shape[:-1]
        return jnp.swapaxes(a.reshape(lead + (8, groups, -1)), -3, -2).reshape(lead + (-1,))

    eight = [[g * 8 + l for l in range(8)] for g in range(groups)]

    def everywhere(a):
        near = lax.all_gather(a, "tensor", axis=0, tiled=False)
        if groups == 1:
            return lax.all_gather(near, "dp", axis=0, tiled=False)
        return lax.all_gather(near, "dp", axis=0, tiled=False, axis_index_groups=eight)

    tokens = inward(tokens).reshape(rows, width)
    cotangent = inward(cotangent).reshape(rows, width)
    attn_norm, mlp_norm = widen(attn_norm, 0), widen(mlp_norm, 0)
    w_query, w_key, w_value = widen(w_query, 0), widen(w_key, 0), widen(w_value, 0)
    w_gate, w_up = widen(w_gate, 0), widen(w_up, 0)
    w_out, w_down = widen(w_out, 1), widen(w_down, 1)

    kv_cols = 2 * w_key.shape[1]
    kv_group = w_query.shape[1] // w_key.shape[1]
    gains = jnp.concatenate(
        [
            jnp.pad(attn_norm, (0, kv_cols - block))[None],
            jnp.pad(mlp_norm, (0, kv_cols - block))[None],
            jnp.zeros((14, kv_cols), bf16),
        ],
        0,
    )
    all_kv = everywhere(jnp.concatenate([jnp.concatenate([w_key, w_value], 1), gains], 0))
    all_q = everywhere(w_query)
    all_out = everywhere(w_out)
    gain_one = all_kv[:, 0, block, :block].reshape(width).astype(f32)
    gain_two = all_kv[:, 0, block + 1, :block].reshape(width).astype(f32)

    def columns(w):
        pieces = w.reshape(block, PLANE, -1)
        near = jnp.stack(trade(pieces, 1, chip), 0)
        mine = lax.all_gather(near, "tensor", axis=0, tiled=False)
        other = hop(mine, 1)
        pair = [jnp.where(core == 0, mine, other), jnp.where(core == 0, other, mine)]
        return jnp.stack(pair, 2).reshape(tp_count, width, -1)

    def lines(w):
        pieces = w.reshape(PLANE, -1, block)
        near = jnp.concatenate(trade(pieces, 0, chip), 1)
        mine = lax.all_gather(near, "tensor", axis=0, tiled=False)
        other = hop(mine, 1)
        tall = mine.shape[1]
        mine, other = (a.reshape(tp_count, tall, PLANE, block) for a in (mine, other))
        pair = [jnp.where(core == 0, mine, other), jnp.where(core == 0, other, mine)]
        return jnp.stack(pair, 3).reshape(tp_count, tall, width)

    all_gate, all_up, all_down = columns(w_gate), columns(w_up), lines(w_down)
    chunks = [slice(b * span, (b + 1) * span) for b in range(seqs)]
    cot_full = [jnp.concatenate(plane_gather(cotangent[c]), 0) for c in chunks]

    cos, sin = rotary_tables(place * span + jnp.arange(span, dtype=jnp.int32))
    cos_rows, sin_rows = jnp.tile(cos, (seqs, 1)), jnp.tile(sin, (seqs, 1))
    x = tokens.astype(f32)
    norm_one = lax.rsqrt(jnp.mean(x * x, -1, keepdims=True) + EPS)
    scaled_one = (x * norm_one).astype(bf16)
    normed_one = (scaled_one.astype(f32) * gain_one).astype(bf16)
    pair = project_pairs(normed_one, all_kv, cos_rows, sin_rows, block)
    pairs = [pair]
    for _ in range(tp_count - 1):
        pairs.append(climb(pairs[-1], 1))
    queries = project_queries(normed_one, all_q, cos_rows, sin_rows)

    seg_blocks = segments.reshape(seqs, tp_count, span)
    own_seg = lax.dynamic_index_in_dim(seg_blocks, place, 1, keepdims=False)
    here = jnp.arange(span, dtype=jnp.int32)
    bias = []
    for j in range(tp_count):
        key_seg = lax.dynamic_index_in_dim(seg_blocks, jnp.maximum(place - j, 0), 1, keepdims=False)
        allowed = key_seg[:, :, None] == own_seg[:, None, :]
        if j == 0:
            allowed &= here[None, :, None] <= here[None, None, :]
        bias.append(jnp.where(allowed, 0.0, -1e30).astype(f32))
    bias = jnp.concatenate(bias, 1)
    spot = place.reshape(1).astype(jnp.int32)
    heads_out, lse = attend(spot, queries, pairs, bias, span, kv_group)
    residual = project_out(heads_out, all_out, tokens)

    norm_two = lax.rsqrt(jnp.mean(residual * residual, -1, keepdims=True) + EPS)
    scaled_two = (residual * norm_two).astype(bf16)
    normed_two = (scaled_two.astype(f32) * gain_two).astype(bf16)
    full_two = [jnp.concatenate(plane_gather(normed_two[c]), 0) for c in chunks]
    forward = [gate_up(f, all_gate, all_up) for f in full_two]
    inner = [f[2] for f in forward]

    def quarters(a):
        return [a[r * span : (r + 1) * span] for r in range(PLANE)]

    backward = [inner_grads(g, all_down, f[0], f[1]) for g, f in zip(cot_full, forward)]
    d_gate, d_up = [d[0] for d in backward], [d[1] for d in backward]
    grad_normed_two = jnp.concatenate(
        [plane_scatter(*quarters(normed_grads(a, b, all_gate, all_up))) for a, b in zip(d_gate, d_up)], 0
    )

    def core_sum(a):
        come = hop(lax.dynamic_index_in_dim(a, 1 - core, 0, keepdims=False), 1)
        mine = added(lax.dynamic_index_in_dim(a, core, 0, keepdims=False), come)
        return lax.psum_scatter(mine, "tensor", scatter_dimension=0, tiled=False)

    def columns_back(a):
        return jnp.concatenate(trade(core_sum(a), 0, chip), 1)

    def lines_back(a):
        mine = core_sum(a)
        return jnp.concatenate(trade(mine.reshape(mine.shape[0], PLANE, block), 1, chip), 0)

    grad_down = lines_back(row_weight_grad(inner, cot_full, tp_count))
    grad_gate = columns_back(column_weight_grad(full_two, d_gate, tp_count))
    grad_up = columns_back(column_weight_grad(full_two, d_up, tp_count))

    mixed = [plane_scatter(*quarters(down(i, all_down))) for i in inner]
    mixed = (residual + jnp.concatenate(mixed, 0)).astype(bf16)

    gain_two_terms = jnp.sum(scaled_two.astype(f32) * grad_normed_two, 0)
    unrounded_two = residual * norm_two
    grad_residual = cotangent.astype(f32) + norm_backward(
        grad_normed_two * gain_two, unrounded_two, norm_two
    )

    grad_low = grad_residual.astype(bf16)
    grad_heads = unproject_out(grad_low, all_out)
    grad_out = sum_all(out_weight_grad(heads_out, grad_low, 8, tp_count), chip, core)
    dq, dkv = unattend(spot, queries, grad_heads, pairs, bias, lse, cos, sin, span, kv_group)
    come = climb(dkv[tp_count - 1], -1)
    for j in range(tp_count - 2, 0, -1):
        come = climb(added(dkv[j], come), -1)
    dkv = finish_pairs(dkv[0], come, cos_rows, sin_rows)
    grad_query = sum_all(query_weight_grad(normed_one, dq, 8, tp_count), chip, core)
    grad_normed_one = unproject_in(dq, dkv, all_q, all_kv)
    gain_one_terms = jnp.sum(scaled_one.astype(f32) * grad_normed_one, 0)
    gain_terms = jnp.stack([gain_one_terms.reshape(8, block), gain_two_terms.reshape(8, block)], 1)
    gain_terms = jnp.pad(gain_terms, ((0, 0), (0, 14), (0, kv_cols - block)))
    kv_sum = sum_all(pair_weight_grad(normed_one, dkv, gain_terms, 8, tp_count), chip, core)
    grad_tokens = grad_residual + norm_backward(grad_normed_one * gain_one, x * norm_one, norm_one)
    grad_tokens = grad_tokens.astype(bf16)

    def gain_share(line):
        line = narrow(line, 0)
        share = line.shape[0] // tp_count
        return lax.dynamic_slice_in_dim(line, place * share, share, 0).astype(f32)

    half = kv_cols // 2
    return (
        outward(mixed).reshape(seqs, span, width),
        outward(grad_tokens).reshape(seqs, span, width),
        gain_share(kv_sum[block, :block]),
        narrow(grad_query, 0).astype(f32),
        narrow(kv_sum[:block, :half], 0).astype(f32),
        narrow(kv_sum[:block, half:], 0).astype(f32),
        narrow(grad_out, 1).astype(f32),
        gain_share(kv_sum[block + 1, :block]),
        narrow(grad_gate, 0).astype(f32),
        narrow(grad_up, 0).astype(f32),
        narrow(grad_down, 1).astype(f32),
    )


def solution(mesh):
    placed = (
        P("dp", "tensor", None),
        P("dp", None),
        P("dp"),
        P("dp", "tensor"),
        P("dp", "tensor"),
        P("dp", "tensor"),
        P("tensor", "dp"),
        P("dp"),
        P("dp", "tensor"),
        P("dp", "tensor"),
        P("tensor", "dp"),
        P("dp", "tensor", None),
    )
    return jax.shard_map(
        shards,
        mesh=mesh,
        in_specs=placed,
        out_specs=(
            P("dp", "tensor", None),
            P("dp", "tensor", None),
            P(("dp", "tensor")),
            P("dp", "tensor"),
            P("dp", "tensor"),
            P("dp", "tensor"),
            P("tensor", "dp"),
            P(("dp", "tensor")),
            P("dp", "tensor"),
            P("dp", "tensor"),
            P("tensor", "dp"),
        ),
        check_vma=False,
    )
```

time: 2310 us -> 1590 us (0.69)
  waiting for transfers between devices: 1400 us -> 711 us
  matrix products: 653 us -> 0 us
  Pallas kernels: 0 us -> 415 us
  local copies, waits for them, and re-layouts: 35.9 us -> 166 us
  starting transfers between devices: 0.81 us -> 111 us
  blocking collectives: 73.2 us -> 19.7 us
  other arithmetic: 92.7 us -> 135 us
  loops' own time: 25.7 us -> 0 us
    dot_general x43 -> x0, matrix products: 653 us -> none  [the longest x4 105 us: attend_backward(): jnp.einsum('gjqk,qgjd->kgd', grad_scores, query_block, preferred_element_...]
    reduce_scatter x11 -> x6, waiting for transfers between devices: 778 us -> 138 us  [the longest x3 138 us: core_sum(): return lax.psum_scatter(mine, 'tensor', scatter_dimension=0, tiled=False)]
    all_gather x9 -> x8, waiting for transfers between devices: 621 us -> 204 us  [the longest x2 88 us: columns(): mine = lax.all_gather(near, 'tensor', axis=0, tiled=False)]
    pallas_call x0 -> x22, Pallas kernels: none -> 415 us  [the longest x2 64 us: column_weight_grad(): call(body, flops=2 * count * rows * width * shards * cols, moved=count *...]
    ppermute x0 -> x77, waiting for transfers between devices: none -> 367 us  [the longest x71 232 us: hop(): return lax.ppermute(a, 'dp', [(i, i ^ bits) for i in range(n)])]
    ppermute x0 -> x77, starting transfers between devices: none -> 110 us  [the longest x71 73.7 us: hop(): return lax.ppermute(a, 'dp', [(i, i ^ bits) for i in range(n)])]
    another operation x0 -> x6, local copies, waits for them, and re-layouts: none -> 45.8 us  [the longest x1 21.5 us: lines(): return jnp.stack(pair, 3).reshape(tp_count, tall, width)]
    another operation x5 -> x11, other arithmetic: 7.5 us -> 40.5 us  [the longest x4 27.8 us: columns(): return jnp.stack(pair, 2).reshape(tp_count, width, -1)]
  transfers between devices with their start and end apart: 20 -> 91, of which waited for: 13 -> 44; matrix products, arithmetic and copies ran while one was open for 29% -> 18% of each run, Pallas kernels for 0% -> 24%
where the time goes in v1:
time: 1590 us; the launch traced here: 1570 us
  waiting for transfers between devices  711 us (45%)
  Pallas kernels  415 us (26%)
  local copies, waits for them, and re-layouts  166 us (10%)
  other arithmetic  135 us (8%)
  starting transfers between devices  111 us (7%)
  blocking collectives  19.7 us (1%)
    ppermute x71, waiting for transfers between devices, hop(): return lax.ppermute(a, 'dp', [(i, i ^ bits) for i in range(n)])  232 us
    reduce_scatter x3, waiting for transfers between devices, core_sum(): return lax.psum_scatter(mine, 'tensor', scatter_dimension=0, tiled=False)  138 us
    ppermute x6, waiting for transfers between devices, climb(): lax.ppermute(a, 'tensor', [(i, i + step) for i in range(n) if 0 <= i + st...  135 us
    all_gather x2, waiting for transfers between devices, columns(): mine = lax.all_gather(near, 'tensor', axis=0, tiled=False)  88 us
    all_gather x1, waiting for transfers between devices, lines(): mine = lax.all_gather(near, 'tensor', axis=0, tiled=False)  78.2 us
    ppermute x71, starting transfers between devices, hop(): return lax.ppermute(a, 'dp', [(i, i ^ bits) for i in range(n)])  73.7 us
    pallas_call x2, Pallas kernels, column_weight_grad(): call(body, flops=2 * count * rows * width * shards * cols, moved=count *...  64 us
    pallas_call x2, Pallas kernels, normed_grads(): call(body, flops=4 * rows * width * depth, moved=w_gate.size * 4 + rows *...  55.9 us
  transfers between devices with their start and end apart: 91, of which 44 were waited for; matrix products, arithmetic and copies ran while one was open for 18% of the time, Pallas kernels for 24%

profile of v1, /device:TPU:0, one launch (start us, length us, event | category | flops | bytes accessed | tf_op | source)
XLA Modules:
  0.0 1573.8 jit_solution(943144370506960010)
XLA Ops:
  90.2 67.8 %all-gather.28.cloned.1.call-done = bf16[16,256,512]{2,1,0:T(8,128)(2,1)} async-done(((bf16[4,256,512]{2,1,0:T(8,128)(2,1)}), bf16[16,256,512]{2,1,0:T(8,128)(2,1)}) %all-gather.28.cloned.1.call-update) | async-done | bytes 4194320 | tf_op jit(solution)/shard_map/all_gather | solution.py:792
  161.2 78.2 %all-gather.32.cloned.1.call-done = bf16[2048,1024]{1,0:T(8,128)(2,1)} async-done(((bf16[512,1024]{1,0:T(8,128)(2,1)}), bf16[2048,1024]{1,0:T(8,128)(2,1)}) %all-gather.32.cloned.1.call-update) | async-done | bytes 4194320 | tf_op jit(solution)/shard_map/all_gather | solution.py:800
  239.7 37.8 %all-gather.18.cloned.1.call-done = bf16[32,272,256]{2,1,0:T(8,128)(2,1)} async-done(((bf16[4,272,256]{2,1,0:T(8,128)(2,1)}), bf16[32,272,256]{2,1,0:T(8,128)(2,1)}) %all-gather.18.cloned.1.call-update) | async-done | bytes 4456464 | tf_op jit(solution)/shard_map/all_gather | solution.py:763
  316.4 20.1 %collective-permute-done.refs_2_.refs_6_.refs_3_.refs_7_ = bf16[2,512,512]{2,1,0:T(8,128)(2,1)S(1)} collective-permute-done((bf16[2,512,512]{2,1,0:T(8,128)(2,1)}, bf16[2,512,512]{2,1,0:T(8,128)(2,1)S(1)}, u32[]{:S(2)}, u32[]{:S(2)}) %collective-permute-start) | collective-permute-done | bytes 1048608 | tf_op jit(solution)/shard_map/ppermute | solution.py:647
  336.5 23.0 %collective-permute-start.1 = (bf16[2,512,512]{2,1,0:T(8,128)(2,1)S(1)}, bf16[2,512,512]{2,1,0:T(8,128)(2,1)S(1)}, u32[]{:S(2)}, u32[]{:S(2)}) collective-permute-start(bf16[2,512,512]{2,1,0:T(8,128)(2,1)S(1)} %collective-permute-done.refs_2_.refs_6_.refs_3_.refs_7_), channel_id=1, source_target_pairs={{0,1},{1,2},{2,3},{4,5},{5,6},{6,7},{8,9},{9,10},{10,11},{12,13},{... | collective-permute-start | bytes 3145736 | tf_op jit(solution)/shard_map/ppermute | solution.py:647
  377.1 20.2 %all-gather.30.cloned.1.call-done = bf16[16,256,512]{2,1,0:T(8,128)(2,1)} async-done(((bf16[4,256,512]{2,1,0:T(8,128)(2,1)}), bf16[16,256,512]{2,1,0:T(8,128)(2,1)}) %all-gather.30.cloned.1.call-update) | async-done | bytes 4194320 | tf_op jit(solution)/shard_map/all_gather | solution.py:792
  439.3 21.5 %copy.110 = bf16[4,512,4,2,256]{4,3,2,1,0:T(2,128)(2,1)} copy(bf16[4,512,4,2,256]{1,4,2,0,3:T(8,128)(2,1)} %pad_maximum_fusion.2) | data formatting | bytes 16777216 | tf_op jit(solution)/shard_map/stack | solution.py:805
  516.2 26.4 %shard_map.205 = (bf16[512,2048]{1,0:T(8,128)(2,1)}, f32[2,4,8,256]{3,2,1,0:T(8,128)S(1)}) custom-call(s32[1]{0:T(128)} %bitcast.place, bf16[512,2048]{1,0:T(8,128)(2,1)} %copy-done.10, bf16[2,512,512]{2,1,0:T(8,128)(2,1)} %shard_map.204.refs_1_.refs_5_.refs_2_.refs_6_, bf16[2,512,512]{2,1,0:T(8,128)(2,1)S(1)} %collective-permute-done.refs_2_.refs_6_.refs_3_.refs_7_, ...), custom_call_target="tpu_custom_call" | custom-call | flops 8589934592 | bytes 4194304 | tf_op jit(solution)/shard_map/pallas_call | solution.py:115
  632.4 26.3 %shard_map.209 = (bf16[1024,2048]{1,0:T(8,128)(2,1)}, bf16[1024,2048]{1,0:T(8,128)(2,1)}, bf16[1024,2048]{1,0:T(8,128)(2,1)}) custom-call(bf16[1024,2048]{1,0:T(8,128)(2,1)} %constant_dynamic-update-slice_fusion.5.x_ref.refs_1_, bf16[4,2048,512]{2,1,0:T(8,128)(2,1)} %bitcast.322, bf16[4,2048,512]{2,1,0:T(8,128)(2,1)} %bitcast.328), custom_call_target="tpu_custom_call" | custom-call | flops 17179869184 | bytes 37748736 | tf_op jit(solution)/shard_map/pallas_call | solution.py:489
  658.7 21.4 %shard_map.213 = (bf16[1024,2048]{1,0:T(8,128)(2,1)}, bf16[1024,2048]{1,0:T(8,128)(2,1)}) custom-call(bf16[1024,2048]{1,0:T(8,128)(2,1)} %constant_dynamic-update-slice_fusion.15.x_ref.refs_3_, bf16[4,512,2048]{2,1,0:T(8,128)(2,1)} %reshape.288.w_ref, bf16[1024,2048]{1,0:T(8,128)(2,1)} %get-tuple-element.32.g_ref, bf16[1024,2048]{1,0:T(8,128)(2,1)} %get-tuple-element.33.u_ref), custom_call_target="tpu_custom_call" | custom-call | flops 8589934592 | bytes 29360128 | tf_op jit(solution)/shard_map/pallas_call | solution.py:514
  680.1 27.8 %shard_map.214 = bf16[1024,2048]{1,0:T(8,128)(2,1)} custom-call(bf16[1024,2048]{1,0:T(8,128)(2,1)} %get-tuple-element.34.g_ref.refs_3_, bf16[1024,2048]{1,0:T(8,128)(2,1)} %get-tuple-element.35.u_ref.refs_3_, bf16[4,2048,512]{2,1,0:T(8,128)(2,1)} %bitcast.323, bf16[4,2048,512]{2,1,0:T(8,128)(2,1)} %bitcast.329), custom_call_target="tpu_custom_call" | custom-call | flops 17179869184 | bytes 29360128 | tf_op jit(solution)/shard_map/pallas_call | solution.py:567
  735.2 26.3 %shard_map.207 = (bf16[1024,2048]{1,0:T(8,128)(2,1)}, bf16[1024,2048]{1,0:T(8,128)(2,1)}, bf16[1024,2048]{1,0:T(8,128)(2,1)}) custom-call(bf16[1024,2048]{1,0:T(8,128)(2,1)} %constant_dynamic-update-slice_fusion.x_ref.refs_0_, bf16[4,2048,512]{2,1,0:T(8,128)(2,1)} %bitcast.324, bf16[4,2048,512]{2,1,0:T(8,128)(2,1)} %bitcast.330), custom_call_target="tpu_custom_call" | custom-call | flops 17179869184 | bytes 37748736 | tf_op jit(solution)/shard_map/pallas_call | solution.py:489
  778.7 21.5 %shard_map.211 = (bf16[1024,2048]{1,0:T(8,128)(2,1)}, bf16[1024,2048]{1,0:T(8,128)(2,1)}) custom-call(bf16[1024,2048]{1,0:T(8,128)(2,1)} %constant_dynamic-update-slice_fusion.10.x_ref.refs_2_, bf16[4,512,2048]{2,1,0:T(8,128)(2,1)} %reshape.288.w_ref, bf16[1024,2048]{1,0:T(8,128)(2,1)} %get-tuple-element.28.g_ref, bf16[1024,2048]{1,0:T(8,128)(2,1)} %get-tuple-element.29.u_ref), custom_call_target="tpu_custom_call" | custom-call | flops 8589934592 | bytes 29360128 | tf_op jit(solution)/shard_map/pallas_call | solution.py:514
  800.2 28.1 %shard_map.212 = bf16[1024,2048]{1,0:T(8,128)(2,1)} custom-call(bf16[1024,2048]{1,0:T(8,128)(2,1)} %get-tuple-element.30.g_ref.refs_2_, bf16[1024,2048]{1,0:T(8,128)(2,1)} %get-tuple-element.31.u_ref.refs_2_, bf16[4,2048,512]{2,1,0:T(8,128)(2,1)} %bitcast.325, bf16[4,2048,512]{2,1,0:T(8,128)(2,1)} %bitcast.331), custom_call_target="tpu_custom_call" | custom-call | flops 17179869184 | bytes 29360128 | tf_op jit(solution)/shard_map/pallas_call | solution.py:567
  882.7 42.7 %collective-permute-done.38 = bf16[256,2048]{1,0:T(8,128)(2,1)S(1)} collective-permute-done((bf16[256,2048]{1,0:T(8,128)(2,1)S(1)}, bf16[256,2048]{1,0:T(8,128)(2,1)S(1)}, u32[]{:S(2)}, u32[]{:S(2)}) %collective-permute-start.38) | collective-permute-done | bytes 1048608 | tf_op jit(solution)/shard_map/ppermute | solution.py:642
  958.7 33.6 %shard_map.216 = (bf16[512,2048]{1,0:T(8,128)(2,1)}, bf16[4,2,512,512]{3,2,1,0:T(8,128)(2,1)}) custom-call(s32[1]{0:T(128)} %bitcast.place, bf16[512,2048]{1,0:T(8,128)(2,1)} %copy-done.10, bf16[512,2048]{1,0:T(8,128)(2,1)} %copy-done.12, bf16[2,512,512]{2,1,0:T(8,128)(2,1)} %shard_map.204.refs_1_.refs_5_.refs_2_.refs_6_, ...), custom_call_target="tpu_custom_call" | custom-call | flops 21474836480 | bytes 8388608 | tf_op jit(solution)/shard_map/pallas_call | solution.py:226
  995.8 39.9 %collective-permute-done.47 = bf16[2,512,512]{2,1,0:T(8,128)(2,1)S(1)} collective-permute-done((bf16[2,512,512]{2,1,0:T(8,128)(2,1)S(1)}, bf16[2,512,512]{2,1,0:T(8,128)(2,1)S(1)}, u32[]{:S(2)}, u32[]{:S(2)}) %collective-permute-start.47) | collective-permute-done | bytes 1048608 | tf_op jit(solution)/shard_map/ppermute | solution.py:647
  1037.3 43.0 %collective-permute-done.48 = bf16[2,512,512]{2,1,0:T(8,128)(2,1)S(1)} collective-permute-done((bf16[2,512,512]{2,1,0:T(8,128)(2,1)S(1)}, bf16[2,512,512]{2,1,0:T(8,128)(2,1)S(1)}, u32[]{:S(2)}, u32[]{:S(2)}) %collective-permute-start.48) | collective-permute-done | bytes 1048608 | tf_op jit(solution)/shard_map/ppermute | solution.py:647
  1097.0 28.4 %collective-permute-done.49.b_ref = bf16[2,512,512]{2,1,0:T(8,128)(2,1)} collective-permute-done((bf16[2,512,512]{2,1,0:T(8,128)(2,1)}, bf16[2,512,512]{2,1,0:T(8,128)(2,1)}, u32[]{:S(2)}, u32[]{:S(2)}) %collective-permute-start.49) | collective-permute-done | bytes 1048608 | tf_op jit(solution)/shard_map/ppermute | solution.py:647
  1181.6 31.9 %shard_map.224 = bf16[2,4,512,1024]{3,2,1,0:T(8,128)(2,1)} custom-call(bf16[1024,2048]{1,0:T(8,128)(2,1)} %get-tuple-element.26.x_ref.refs_0_, bf16[1024,2048]{1,0:T(8,128)(2,1)} %get-tuple-element.27.x_ref.refs_1_, bf16[1024,2048]{1,0:T(8,128)(2,1)} %constant_dynamic-update-slice_fusion.10.x_ref.refs_2_, ...), custom_call_target="tpu_custom_call" | custom-call | flops 17179869184 | bytes 33554432 | tf_op jit(solution)/shard_map/pallas_call | solution.py:627
  1287.1 31.9 %shard_map.223 = bf16[2,4,4,256,512]{4,3,2,1,0:T(8,128)(2,1)} custom-call(bf16[1024,2048]{1,0:T(8,128)(2,1)} %constant_dynamic-update-slice_fusion.x_ref.refs_0_, bf16[1024,2048]{1,0:T(8,128)(2,1)} %constant_dynamic-update-slice_fusion.5.x_ref.refs_1_, bf16[1024,2048]{1,0:T(8,128)(2,1)} %get-tuple-element.31.u_ref.refs_2_, ...), custom_call_target="tpu_custom_call" | custom-call | flops 17179869184 | bytes 33554432 | tf_op jit(solution)/shard_map/pallas_call | solution.py:596
  1332.8 32.0 %shard_map.222 = bf16[2,4,4,256,512]{4,3,2,1,0:T(8,128)(2,1)} custom-call(bf16[1024,2048]{1,0:T(8,128)(2,1)} %constant_dynamic-update-slice_fusion.x_ref.refs_0_, bf16[1024,2048]{1,0:T(8,128)(2,1)} %constant_dynamic-update-slice_fusion.5.x_ref.refs_1_, bf16[1024,2048]{1,0:T(8,128)(2,1)} %get-tuple-element.30.g_ref.refs_2_, ...), custom_call_target="tpu_custom_call" | custom-call | flops 17179869184 | bytes 33554432 | tf_op jit(solution)/shard_map/pallas_call | solution.py:596
  1400.7 62.5 %reduce-scatter.15.cloned.1.call-done = bf16[1,4,256,512]{3,2,1,0:T(8,128)(2,1)} async-done(((bf16[4,4,256,512]{3,2,1,0:T(8,128)(2,1)}), bf16[1,4,256,512]{3,2,1,0:T(8,128)(2,1)}) %reduce-scatter.15.cloned.1.call-update) | async-done | bytes 1048592 | tf_op jit(solution)/shard_map/reduce_scatter | solution.py:857
  1467.4 75.4 %reduce-scatter.13.cloned.1.call-done = bf16[1,4,256,512]{3,2,1,0:T(8,128)(2,1)} async-done(((bf16[4,4,256,512]{3,2,1,0:T(8,128)(2,1)}), bf16[1,4,256,512]{3,2,1,0:T(8,128)(2,1)}) %reduce-scatter.13.cloned.1.call-update) | async-done | bytes 1048592 | tf_op jit(solution)/shard_map/reduce_scatter | solution.py:857
  (448 shorter events, 690.6 us)
Async XLA Ops:
  8.7 149.3 %all-gather.28.cloned.1.call-start = ((), (), s32[]{:S(2)}) async-start(), calls=%async_computation.17 | async-start | bytes 5242880 | tf_op jit(solution)/shard_map/all_gather | solution.py:792
  43.3 196.0 %all-gather.32.cloned.1.call-start = ((), (), s32[]{:S(2)}) async-start(), calls=%async_computation.19 | async-start | bytes 5242880 | tf_op jit(solution)/shard_map/all_gather | solution.py:800
  59.6 217.8 %all-gather.18.cloned.1.call-start = ((), (), s32[]{:S(2)}) async-start(), calls=%async_computation.12 | async-start | bytes 5013504 | tf_op jit(solution)/shard_map/all_gather | solution.py:763
  79.7 317.7 %all-gather.30.cloned.1.call-start = ((), (), s32[]{:S(2)}) async-start(), calls=%async_computation.18 | async-start | bytes 5242880 | tf_op jit(solution)/shard_map/all_gather | solution.py:792
  80.9 424.6 %all-gather.22.cloned.1.call-start = ((), (), s32[]{:S(2)}) async-start(), calls=%async_computation.14 | async-start | bytes 9437184 | tf_op jit(solution)/shard_map/all_gather | solution.py:763
  81.6 460.9 %all-gather.26.cloned.1.call-start = ((), (), s32[]{:S(2)}) async-start(), calls=%async_computation.16 | async-start | bytes 9437184 | tf_op jit(solution)/shard_map/all_gather | solution.py:763
  82.4 1303.5 %reduce-scatter.7.cloned.1.call-start = ((), (), s32[]{:S(2)}) async-start(), calls=%async_computation.6 | async-start | bytes 696320 | tf_op jit(solution)/shard_map/reduce_scatter | solution.py:702
  85.7 192.7 %collective-permute-start.32 = (bf16[256,2048]{1,0:T(8,128)(2,1)}, bf16[256,2048]{1,0:T(8,128)(2,1)}, u32[]{:S(2)}, u32[]{:S(2)}) collective-permute-start(bf16[256,2048]{1,0:T(8,128)(2,1)} %get-tuple-element.110), channel_id=1, source_target_pairs={{0,16},{4,20},{8,24},{12,28},{16,0},{20,4},{24,8},{28,12},{1,17},{... | collective-permute-start | bytes 3145736 | tf_op jit(solution)/shard_map/ppermute | solution.py:642
  87.1 200.1 %collective-permute-start.31 = (bf16[256,2048]{1,0:T(8,128)(2,1)}, bf16[256,2048]{1,0:T(8,128)(2,1)}, u32[]{:S(2)}, u32[]{:S(2)}) collective-permute-start(bf16[256,2048]{1,0:T(8,128)(2,1)} %get-tuple-element.110), channel_id=1, source_target_pairs={{0,8},{4,12},{8,0},{12,4},{16,24},{20,28},{24,16},{28,20},{1,9},{5... | collective-permute-start | bytes 3145736 | tf_op jit(solution)/shard_map/ppermute | solution.py:642
  88.6 207.1 %collective-permute-start.40 = (bf16[256,2048]{1,0:T(8,128)(2,1)}, bf16[256,2048]{1,0:T(8,128)(2,1)}, u32[]{:S(2)}, u32[]{:S(2)}) collective-permute-start(bf16[256,2048]{1,0:T(8,128)(2,1)} %get-tuple-element.111), channel_id=1, source_target_pairs={{0,16},{4,20},{8,24},{12,28},{16,0},{20,4},{24,8},{28,12},{1,17},{... | collective-permute-start | bytes 3145736 | tf_op jit(solution)/shard_map/ppermute | solution.py:642
  158.0 248.2 %collective-permute-start.10 = (bf16[4,4,256,512]{3,2,1,0:T(8,128)(2,1)}, bf16[4,4,256,512]{3,2,1,0:T(8,128)(2,1)}, u32[]{:S(2)}, u32[]{:S(2)}) collective-permute-start(bf16[4,4,256,512]{3,2,1,0:T(8,128)(2,1)} %bitcast.339), channel_id=1, source_target_pairs={{0,4},{4,0},{8,12},{12,8},{16,20},{20,16},{24,28},{28,24},{1,5},{5... | collective-permute-start | bytes 12582920 | tf_op jit(solution)/shard_map/ppermute | solution.py:642
  239.3 174.1 %collective-permute-start.18 = (bf16[4,512,1024]{2,1,0:T(8,128)(2,1)}, bf16[4,512,1024]{2,1,0:T(8,128)(2,1)}, u32[]{:S(2)}, u32[]{:S(2)}) collective-permute-start(bf16[4,512,1024]{2,1,0:T(8,128)(2,1)} %bitcast.343), channel_id=1, source_target_pairs={{0,4},{4,0},{8,12},{12,8},{16,20},{20,16},{24,28},{28,24},{1,5},{5... | collective-permute-start | bytes 12582920 | tf_op jit(solution)/shard_map/ppermute | solution.py:642
  397.3 167.5 %collective-permute-start.14 = (bf16[4,4,256,512]{3,2,1,0:T(8,128)(2,1)}, bf16[4,4,256,512]{3,2,1,0:T(8,128)(2,1)}, u32[]{:S(2)}, u32[]{:S(2)}) collective-permute-start(bf16[4,4,256,512]{3,2,1,0:T(8,128)(2,1)} %bitcast.341), channel_id=1, source_target_pairs={{0,4},{4,0},{8,12},{12,8},{16,20},{20,16},{24,28},{28,24},{1,5},{5... | collective-permute-start | bytes 12582920 | tf_op jit(solution)/shard_map/ppermute | solution.py:642
  587.1 147.3 %collective-permute-start.6 = (bf16[128,2048]{1,0:T(8,128)(2,1)S(1)}, bf16[128,2048]{1,0:T(8,128)(2,1)S(1)}, u32[]{:S(2)}, u32[]{:S(2)}) collective-permute-start(bf16[128,2048]{1,0:T(8,128)(2,1)S(1)} %slice.376), channel_id=1, source_target_pairs={{0,8},{4,12},{8,0},{12,4},{16,24},{20,28},{24,16},{28,20},{1,9},{5... | collective-permute-start | bytes 1572872 | tf_op jit(solution)/shard_map/ppermute | solution.py:642
  588.8 143.8 %collective-permute-start.5 = (bf16[128,2048]{1,0:T(8,128)(2,1)S(1)}, bf16[128,2048]{1,0:T(8,128)(2,1)S(1)}, u32[]{:S(2)}, u32[]{:S(2)}) collective-permute-start(bf16[128,2048]{1,0:T(8,128)(2,1)S(1)} %slice.375), channel_id=1, source_target_pairs={{0,16},{4,20},{8,24},{12,28},{16,0},{20,4},{24,8},{28,12},{1,17},{... | collective-permute-start | bytes 1572872 | tf_op jit(solution)/shard_map/ppermute | solution.py:642
  709.5 122.3 %collective-permute-start.45 = (bf16[128,2048]{1,0:T(8,128)(2,1)S(1)}, bf16[128,2048]{1,0:T(8,128)(2,1)S(1)}, u32[]{:S(2)}, u32[]{:S(2)}) collective-permute-start(bf16[128,2048]{1,0:T(8,128)(2,1)S(1)} %get-tuple-element.88), channel_id=1, source_target_pairs={{0,8},{4,12},{8,0},{12,4},{16,24},{20,28},{24,16},{28,20},{1,9},{5... | collective-permute-start | bytes 1572872 | tf_op jit(solution)/shard_map/ppermute | solution.py:642
  711.0 122.0 %collective-permute-start.43 = (bf16[128,2048]{1,0:T(8,128)(2,1)S(1)}, bf16[128,2048]{1,0:T(8,128)(2,1)S(1)}, u32[]{:S(2)}, u32[]{:S(2)}) collective-permute-start(bf16[128,2048]{1,0:T(8,128)(2,1)S(1)} %get-tuple-element.89), channel_id=1, source_target_pairs={{0,16},{4,20},{8,24},{12,28},{16,0},{20,4},{24,8},{28,12},{1,17},{... | collective-permute-start | bytes 1572872 | tf_op jit(solution)/shard_map/ppermute | solution.py:642
  1219.8 169.6 %reduce-scatter.9.cloned.1.call-start = ((), (), s32[]{:S(2)}) async-start(), calls=%async_computation.7 | async-start | bytes 1310720 | tf_op jit(solution)/shard_map/reduce_scatter | solution.py:702
  1246.0 145.1 %reduce-scatter.11.cloned.1.call-start = ((), (), s32[]{:S(2)}) async-start(), calls=%async_computation.8 | async-start | bytes 1310720 | tf_op jit(solution)/shard_map/reduce_scatter | solution.py:702
  1287.1 176.1 %reduce-scatter.15.cloned.1.call-start = ((), (), s32[]{:S(2)}) async-start(), calls=%async_computation.10 | async-start | bytes 5242880 | tf_op jit(solution)/shard_map/reduce_scatter | solution.py:857
  1332.5 210.2 %reduce-scatter.13.cloned.1.call-start = ((), (), s32[]{:S(2)}) async-start(), calls=%async_computation.9 | async-start | bytes 5242880 | tf_op jit(solution)/shard_map/reduce_scatter | solution.py:857
  1397.2 146.8 %collective-permute-start.74 = (bf16[512,256]{1,0:T(8,128)(2,1)S(1)}, bf16[512,256]{1,0:T(8,128)(2,1)S(1)}, u32[]{:S(2)}, u32[]{:S(2)}) collective-permute-start(bf16[512,256]{1,0:T(8,128)(2,1)S(1)} %bitcast.354), channel_id=1, source_target_pairs={{0,24},{4,28},{8,16},{12,20},{16,8},{20,12},{24,0},{28,4},{1,25},{... | collective-permute-start | bytes 786440 | tf_op jit(solution)/shard_map/ppermute | solution.py:642
  1398.9 147.5 %collective-permute-start.75 = (bf16[512,256]{1,0:T(8,128)(2,1)S(1)}, bf16[512,256]{1,0:T(8,128)(2,1)S(1)}, u32[]{:S(2)}, u32[]{:S(2)}) collective-permute-start(bf16[512,256]{1,0:T(8,128)(2,1)S(1)} %bitcast.353), channel_id=1, source_target_pairs={{0,16},{4,20},{8,24},{12,28},{16,0},{20,4},{24,8},{28,12},{1,17},{... | collective-permute-start | bytes 786440 | tf_op jit(solution)/shard_map/ppermute | solution.py:642
  1400.1 146.9 %collective-permute-start.76 = (bf16[512,256]{1,0:T(8,128)(2,1)S(1)}, bf16[512,256]{1,0:T(8,128)(2,1)S(1)}, u32[]{:S(2)}, u32[]{:S(2)}) collective-permute-start(bf16[512,256]{1,0:T(8,128)(2,1)S(1)} %bitcast.352), channel_id=1, source_target_pairs={{0,8},{4,12},{8,0},{12,4},{16,24},{20,28},{24,16},{28,20},{1,9},{5... | collective-permute-start | bytes 786440 | tf_op jit(solution)/shard_map/ppermute | solution.py:642
  (113 other events, 3790.6 us)
Sparse Core Ops, SparseCore 0:
  9.6 30.6 all-gather.19
  41.8 32.3 all-gather.23
  76.4 81.5 all-gather.27
  160.0 79.2 all-gather.31
  241.1 36.3 all-gather.17
  279.4 117.8 all-gather.29
  399.2 55.0 all-gather.21
  456.2 54.3 all-gather.25
  1219.9 20.3 reduce-scatter.6
  1246.2 26.5 reduce-scatter.8
  1279.4 26.4 reduce-scatter.10
  1308.2 75.4 reduce-scatter.16
  1385.9 77.2 reduce-scatter.14
  1465.5 77.2 reduce-scatter.12

commit v2 on v1

v2 whole, which is shorter than its diff:
```python
import functools

import jax
import jax.numpy as jnp
from jax import lax
from jax.experimental import pallas as pl
from jax.experimental.pallas import tpu as pltpu
from jax.sharding import PartitionSpec as P

HD = 64
EPS = 1e-05
THETA = 500000.0
LOG2E = 1.4426950408889634
LANES = 128
PLANE = 4
f32 = jnp.float32
bf16 = jnp.bfloat16


def call(body, flops, moved, vmem=50, **kw):
    return pl.pallas_call(
        body,
        compiler_params=pltpu.CompilerParams(vmem_limit_bytes=vmem * 2**20),
        cost_estimate=pl.CostEstimate(flops=flops, bytes_accessed=moved, transcendentals=0),
        **kw,
    )


def nn(a, b):
    return jnp.dot(a, b, preferred_element_type=f32)


def nt(a, b):
    return lax.dot_general(a, b, (((1,), (1,)), ((), ())), preferred_element_type=f32)


def tn(a, b):
    return lax.dot_general(a, b, (((0,), (0,)), ((), ())), preferred_element_type=f32)


def swap_halves(x):
    lane = lax.broadcasted_iota(jnp.int32, x.shape, 1)
    return jnp.where(lane % HD < HD // 2, pltpu.roll(x, LANES - HD // 2, 1), pltpu.roll(x, HD // 2, 1))


def gather_keys(k_refs, v_refs, blocks):
    k = jnp.concatenate([k_refs[j][0, 0] for j in range(blocks)], 0)
    v = jnp.concatenate([v_refs[j][0, 0] for j in range(blocks)], 0)
    return k, v


def padded_rows(part, e):
    zero = jnp.zeros_like(part)
    return jnp.concatenate([part, zero] if e == 0 else [zero, part], 0)


def attend_blocks(blocks, group, q_ref, k_refs, v_refs, bias_ref, o_ref, lse_ref, qt_ref, ot_ref):
    span = q_ref.shape[0]
    n = blocks * span
    k, v = gather_keys(k_refs, v_refs, blocks)
    vt = v.T
    qt_ref[...] = q_ref[...].T
    factor = HD**-0.5 * LOG2E

    def step(i, carry):
        for e in range(2):
            head = e * group + i
            rows = pl.ds(pl.multiple_of(head * HD, HD), HD)
            scores = nn(k, padded_rows(qt_ref[rows, :], e))
            logits = scores * factor + bias_ref[0, :n, :]
            top = jnp.max(logits, 0, keepdims=True)
            weights = jnp.exp2(logits - top)
            total = jnp.sum(weights, 0, keepdims=True)
            out = nn(vt[e * HD : (e + 1) * HD], weights.astype(bf16))
            ot_ref[rows, :] = out * (1.0 / total)
            lse_ref[0, 0, pl.ds(head, 1), :] = top + jnp.log2(total)
        return carry

    lax.fori_loop(0, group, step, 0)
    o_ref[...] = ot_ref[...].T.astype(bf16)


def attend_kernel(count, group, place, *refs):
    q_ref, k_refs, v_refs = refs[0], refs[1 : 1 + count], refs[1 + count : 1 + 2 * count]
    rest = refs[1 + 2 * count :]
    for blocks in range(1, count + 1):

        @pl.when(place[0] == blocks - 1)
        def _(blocks=blocks):
            attend_blocks(blocks, group, q_ref, k_refs, v_refs, *rest)


def key_specs(count, span):
    return [
        pl.BlockSpec(
            (1, 1, span, LANES), lambda b, p, s, part=part, j=j: (jnp.maximum(s[0] - j, 0), part, b, p)
        )
        for part in range(2)
        for j in range(count)
    ]


def attend(place, queries, pairs, bias, span, group):
    rows, width = queries.shape
    count = pairs.shape[0]
    seqs = rows // span
    kv_width = pairs.shape[3]
    tiles = kv_width // LANES
    wide = width // tiles
    in_specs = [pl.BlockSpec((span, wide), lambda b, p, s: (b, p))] + key_specs(count, span)
    in_specs.append(pl.BlockSpec((1, count * span, span), lambda b, p, s: (b, 0, 0)))
    heads = wide // HD
    spec = pltpu.PrefetchScalarGridSpec(
        num_scalar_prefetch=1,
        grid=(seqs, tiles),
        in_specs=in_specs,
        out_specs=[
            pl.BlockSpec((span, wide), lambda b, p, s: (b, p)),
            pl.BlockSpec((1, 1, heads, span), lambda b, p, s: (b, p, 0, 0)),
        ],
        scratch_shapes=[pltpu.VMEM((wide, span), bf16), pltpu.VMEM((wide, span), f32)],
    )
    return call(
        functools.partial(attend_kernel, count, group),
        flops=rows * width * span * count * 8,
        moved=rows * width * 4,
        grid_spec=spec,
        out_shape=[
            jax.ShapeDtypeStruct((rows, width), bf16),
            jax.ShapeDtypeStruct((seqs, tiles, heads, span), f32),
        ],
    )(place, queries, *([pairs] * (2 * count)), bias)


def unattend_blocks(
    blocks, count, group, q_ref, g_ref, k_refs, v_refs, bias_ref, lse_ref, cos_ref, sin_ref,
    dq_ref, dkv_ref, qt_ref, gt_ref, dqt_ref, dk_ref, dv_ref,
):
    span = q_ref.shape[0]
    n = blocks * span
    k, v = gather_keys(k_refs, v_refs, blocks)
    kt = k.T
    qt_ref[...] = q_ref[...].T
    gt_ref[...] = g_ref[...].T
    dk_ref[...] = jnp.zeros_like(dk_ref)
    dv_ref[...] = jnp.zeros_like(dv_ref)
    factor = HD**-0.5 * LOG2E
    lane = lax.broadcasted_iota(jnp.int32, (span, LANES), 1)

    def moved(tile, b, e):
        if b != e:
            tile = pltpu.roll(tile, HD, 1)
        return jnp.where((lane < HD) if e == 0 else (lane >= HD), tile, 0.0).astype(bf16)

    def step(i, carry):
        for e in range(2):
            tile_at = pl.ds(pl.multiple_of((e * (group // 2) + i) * LANES, LANES), LANES)
            q_tile = q_ref[:, tile_at].astype(f32)
            g_tile = g_ref[:, tile_at].astype(f32)
            all_ds, all_p = [], []
            for b in range(2):
                head = e * group + 2 * i + b
                rows = pl.ds(pl.multiple_of(head * HD, HD), HD)
                scores = nn(k, padded_rows(qt_ref[rows, :], e))
                lse = lse_ref[0, 0, pl.ds(head, 1), :]
                probs = jnp.exp2(scores * factor + bias_ref[0, :n, :] - lse)
                dp = nn(v, padded_rows(gt_ref[rows, :], e))
                delta = jnp.sum(probs * dp, 0, keepdims=True)
                ds = (probs * (dp - delta)).astype(bf16)
                dqt_ref[rows, :] = nn(kt[e * HD : (e + 1) * HD], ds)
                all_ds.append(ds)
                all_p.append(probs.astype(bf16))
            q_rows = jnp.concatenate([moved(q_tile, b, e) for b in range(2)], 0)
            g_rows = jnp.concatenate([moved(g_tile, b, e) for b in range(2)], 0)
            dk_ref[:n, :] += nn(jnp.concatenate(all_ds, 1), q_rows)
            dv_ref[:n, :] += nn(jnp.concatenate(all_p, 1), g_rows)
        return carry

    lax.fori_loop(0, group // 2, step, 0)
    scale = HD**-0.5
    dq = dqt_ref[...].T * scale
    for t in range(dq.shape[1] // LANES):
        part = dq[:, t * LANES : (t + 1) * LANES]
        dq_ref[:, t * LANES : (t + 1) * LANES] = (
            part * cos_ref[...] - swap_halves(part) * sin_ref[...]
        ).astype(bf16)
    for n in range(count):
        j = blocks - 1 - n if n < blocks else n
        dkv_ref[n, 0] = (dk_ref[j * span : (j + 1) * span, :] * scale).astype(bf16)
        dkv_ref[n, 1] = dv_ref[j * span : (j + 1) * span, :].astype(bf16)


def unattend_kernel(count, group, skip, place, *refs):
    refs = refs[skip:]
    q_ref, g_ref, k_refs, v_refs = refs[0], refs[1], refs[2 : 2 + count], refs[2 + count : 2 + 2 * count]
    rest = refs[2 + 2 * count :]
    for blocks in range(1, count + 1):

        @pl.when(place[0] == blocks - 1)
        def _(blocks=blocks):
            unattend_blocks(blocks, count, group, q_ref, g_ref, k_refs, v_refs, *rest)


def unattend(place, queries, grads, pairs, bias, lse, cos, sin, span, group, deps=()):
    rows, width = queries.shape
    count = pairs.shape[0]
    seqs = rows // span
    kv_width = pairs.shape[3]
    tiles = kv_width // LANES
    wide = width // tiles
    heads = wide // HD
    tall = pl.BlockSpec((span, wide), lambda b, p, s: (b, p))
    table = pl.BlockSpec((span, LANES), lambda b, p, s: (0, 0))
    deps = jax.tree.leaves(deps)
    in_specs = [pl.BlockSpec(memory_space=pl.ANY)] * len(deps) + [tall, tall] + key_specs(count, span)
    in_specs += [
        pl.BlockSpec((1, count * span, span), lambda b, p, s: (b, 0, 0)),
        pl.BlockSpec((1, 1, heads, span), lambda b, p, s: (b, p, 0, 0)),
        table,
        table,
    ]
    spec = pltpu.PrefetchScalarGridSpec(
        num_scalar_prefetch=1,
        grid=(seqs, tiles),
        in_specs=in_specs,
        out_specs=[tall, pl.BlockSpec((count, 2, span, LANES), lambda b, p, s: (0, 0, b, p))],
        scratch_shapes=[
            pltpu.VMEM((wide, span), bf16),
            pltpu.VMEM((wide, span), bf16),
            pltpu.VMEM((wide, span), f32),
            pltpu.VMEM((count * span, LANES), f32),
            pltpu.VMEM((count * span, LANES), f32),
        ],
    )
    return call(
        functools.partial(unattend_kernel, count, group, len(deps)),
        flops=rows * width * span * count * 20,
        moved=rows * width * 8,
        grid_spec=spec,
        out_shape=[
            jax.ShapeDtypeStruct((rows, width), bf16),
            jax.ShapeDtypeStruct((count, 2, rows, kv_width), bf16),
        ],
    )(place, *deps, queries, grads, *([pairs] * (2 * count)), bias, lse, cos, sin)


def turn(y, cos, sin, out_ref, start=0):
    for t in range(y.shape[1] // LANES):
        part = y[:, t * LANES : (t + 1) * LANES]
        out_ref[:, t * LANES : (t + 1) * LANES] = (part * cos + swap_halves(part) * sin).astype(bf16)


def block_home(spot, half, r):
    core = spot[1] if half == 0 else 1 - spot[1]
    return 2 * (spot[2] ^ r) + core


def lanes_at(ref, at, size):
    return ref[:, pl.ds(pl.multiple_of(at * size, size), size)]


def by_block(ref, spot, size):
    return jnp.concatenate(
        [lanes_at(ref, block_home(spot, half, r), size) for half in range(2) for r in range(PLANE)], 1
    )


def by_slot(ref, spot, shards, size):
    return jnp.concatenate([lanes_at(ref, slot_home(spot, s, shards), size) for s in range(shards)], 1)


def slot_home(spot, s, shards):
    return lax.rem(spot[0] + shards - s, shards)


def grid_call(body, grid, in_specs, out_specs, out_shape, flops, moved, scratch=(), deps=()):
    deps = jax.tree.leaves(deps)

    def late(spot, *refs):
        body(spot, *refs[len(deps) :])

    run = call(
        late,
        flops=flops,
        moved=moved,
        grid_spec=pltpu.PrefetchScalarGridSpec(
            num_scalar_prefetch=1,
            grid=grid,
            in_specs=[pl.BlockSpec(memory_space=pl.ANY)] * len(deps) + list(in_specs),
            out_specs=out_specs,
            scratch_shapes=list(scratch),
        ),
        out_shape=out_shape,
    )
    return lambda spot, *arrays: run(spot, *deps, *arrays)


def project_pairs(spot, normed, weights, cos, sin, depth, deps=()):
    rows, width = normed.shape
    parts, shards, _, cols = weights.shape
    half = cols // 2

    def body(spot, x_ref, w_ref, cos_ref, sin_ref, o_ref):
        w = w_ref[:, 0, :depth, :].reshape(parts * depth, cols)
        y = nn(x_ref[...], w)
        k = y[:, :half]
        o_ref[0] = (k * cos_ref[...] + swap_halves(k) * sin_ref[...]).astype(bf16)
        o_ref[1] = y[:, half:].astype(bf16)

    whole = lambda s, _: (0, 0)
    return grid_call(
        body,
        (shards,),
        [
            pl.BlockSpec((rows, width), whole),
            pl.BlockSpec((parts, 1, weights.shape[2], cols), lambda s, _: (0, s, 0, 0)),
            pl.BlockSpec((rows, LANES), whole),
            pl.BlockSpec((rows, LANES), whole),
        ],
        pl.BlockSpec((2, rows, half), lambda s, spot: (0, 0, slot_home(spot, s, shards))),
        jax.ShapeDtypeStruct((2, rows, half * shards), bf16),
        2 * rows * width * shards * cols,
        weights.size * 2 + normed.size * 2,
        deps=deps,
    )(spot, normed, weights, cos, sin)


def project_queries(spot, normed, weights, cos, sin):
    rows, width = normed.shape
    shards, depth, cols = weights[0].shape
    count = len(weights)

    def body(spot, *refs):
        x_ref, w_refs, cos_ref, sin_ref, o_ref, xs_ref = refs[0], refs[1 : 1 + count], *refs[1 + count :]

        @pl.when(pl.program_id(0) == 0)
        def _():
            xs_ref[...] = by_block(x_ref, spot, depth)

        y = nn(xs_ref[...], jnp.concatenate([w[0] for w in w_refs], 0))
        turn(y, cos_ref[...], sin_ref[...], o_ref)

    whole = lambda s, _: (0, 0)
    return grid_call(
        body,
        (shards,),
        [pl.BlockSpec((rows, width), whole)]
        + [pl.BlockSpec((1, depth, cols), lambda s, _: (s, 0, 0))] * count
        + [pl.BlockSpec((rows, LANES), whole)] * 2,
        pl.BlockSpec((rows, cols), lambda s, spot: (0, slot_home(spot, s, shards))),
        jax.ShapeDtypeStruct((rows, cols * shards), bf16),
        2 * rows * width * shards * cols,
        width * shards * cols * 2 + normed.size * 4,
        [pltpu.VMEM((rows, width), bf16)],
    )(spot, normed, *weights, cos, sin)


def folded(w):
    half = w.shape[0] // 2
    return jnp.concatenate([w[:half], w[half:]], 1)


def unfolded(w):
    half = w.shape[1] // 2
    return jnp.concatenate([w[:, :half], w[:, half:]], 0)


def project_out(spot, heads_out, weights, tokens, deps=()):
    rows, width = heads_out.shape
    shards, depth, cols = weights[0].shape
    depth, cols = 2 * depth, cols // 2
    count = len(weights)
    tall = min(256, rows)

    def body(spot, *refs):
        x_ref, w_refs, t_ref, o_ref = refs[0], refs[1 : 1 + count], *refs[1 + count :]
        x = by_slot(x_ref, spot, shards, depth)
        for n, w_ref in enumerate(w_refs):
            at = block_home(spot, n // PLANE, n % PLANE)
            y = nn(x, jnp.concatenate([unfolded(w_ref[s]) for s in range(shards)], 0))
            o_ref[:, pl.ds(pl.multiple_of(at * cols, cols), cols)] = lanes_at(t_ref, at, cols).astype(f32) + y

    tile = pl.BlockSpec((tall, width), lambda m, _: (m, 0))
    return grid_call(
        body,
        (rows // tall,),
        [tile] + [pl.BlockSpec(w.shape, lambda m, _: (0, 0, 0)) for w in weights] + [tile],
        tile,
        jax.ShapeDtypeStruct((rows, cols * count), f32),
        2 * rows * width * count * cols,
        width * cols * count * 2 + rows * width * 8,
        deps=deps,
    )(spot, heads_out, *weights, tokens)


def unproject_out(spot, grads, weights, deps=()):
    rows, width = grads.shape
    shards, depth, cols = weights[0].shape
    depth, cols = 2 * depth, cols // 2
    count = len(weights)

    def body(spot, *refs):
        x_ref, w_refs, o_ref, xs_ref = refs[0], refs[1 : 1 + count], *refs[1 + count :]

        @pl.when(pl.program_id(0) == 0)
        def _():
            xs_ref[...] = by_block(x_ref, spot, cols)

        w = jnp.concatenate([unfolded(w_ref[0]) for w_ref in w_refs], 1)
        o_ref[...] = nt(xs_ref[...], w).astype(bf16)

    return grid_call(
        body,
        (shards,),
        [pl.BlockSpec((rows, width), lambda s, _: (0, 0))]
        + [pl.BlockSpec((1, depth // 2, 2 * cols), lambda s, _: (s, 0, 0))] * count,
        pl.BlockSpec((rows, depth), lambda s, spot: (0, slot_home(spot, s, shards))),
        jax.ShapeDtypeStruct((rows, depth * shards), bf16),
        2 * rows * width * shards * depth,
        width * shards * depth * 2 + rows * width * 6,
        [pltpu.VMEM((rows, width), bf16)],
        deps=deps,
    )(spot, grads, *weights)


def unproject_in(spot, dq, dkv, w_q, w_kv):
    rows, width = dq.shape
    shards, depth, cols = w_q[0].shape
    thin = w_kv.shape[3] // 2
    count = len(w_q)
    tall = min(256, rows)

    def body(spot, *refs):
        q_ref, kv_ref, wq_refs, wkv_ref, o_ref = *refs[:2], refs[2 : 2 + count], *refs[2 + count :]
        left = by_slot(q_ref, spot, shards, cols)
        thin_left = jnp.concatenate(
            [
                kv_ref[n, :, pl.ds(pl.multiple_of(slot_home(spot, s, shards) * thin, thin), thin)]
                for s in range(shards)
                for n in range(2)
            ],
            1,
        )
        for n, w_ref in enumerate(wq_refs):
            at = block_home(spot, n // PLANE, n % PLANE)
            y = nt(left, jnp.concatenate([w_ref[s] for s in range(shards)], 1))
            y += nt(thin_left, jnp.concatenate([wkv_ref[at, s, :depth, :] for s in range(shards)], 1))
            o_ref[:, pl.ds(pl.multiple_of(at * depth, depth), depth)] = y

    tile = pl.BlockSpec((tall, width), lambda m, _: (m, 0))
    return grid_call(
        body,
        (rows // tall,),
        [tile, pl.BlockSpec((2, tall, dkv.shape[2]), lambda m, _: (0, m, 0))]
        + [pl.BlockSpec(w.shape, lambda m, _: (0, 0, 0)) for w in w_q]
        + [pl.BlockSpec(w_kv.shape, lambda m, _: (0, 0, 0, 0))],
        pl.BlockSpec((tall, count * depth), lambda m, _: (m, 0)),
        jax.ShapeDtypeStruct((rows, count * depth), f32),
        2 * rows * count * depth * shards * (cols + 2 * thin),
        count * depth * shards * cols * 2 + w_kv.size * 2 + rows * width * 6,
    )(spot, dq, dkv, *w_q, w_kv)


def of_core(ref, core, depth):
    return ref[:, pl.ds(pl.multiple_of(core * depth, depth), depth)]


def in_blocks_grad(spot, normed, dq, dkv, gains, shards):
    rows, width = normed.shape
    depth = width // PLANE // 2
    y = dq if dkv is None else dkv
    cols = (dq.shape[1] if dkv is None else 2 * dkv.shape[2]) // shards
    extra = 0 if gains is None else gains.shape[1]

    def body(spot, x_ref, y_ref, *refs):
        for n, core in ((0, spot[1]), (1, 1 - spot[1])):
            x, o_ref = of_core(x_ref, core, depth), refs[-2 + n]
            totals = [tn(x, y_ref[...])] if dkv is None else [tn(x, y_ref[0]), tn(x, y_ref[1])]
            thin = cols // len(totals)
            for s in range(shards):
                for m, total in enumerate(totals):
                    o_ref[0, s, :depth, m * thin : (m + 1) * thin] = total[:, s * thin : (s + 1) * thin].astype(bf16)
                if extra:
                    o_ref[0, s, depth:, :] = refs[0][core].astype(bf16)

    whole = pl.BlockSpec(y.shape, (lambda q, _: (0, 0)) if dkv is None else (lambda q, _: (0, 0, 0)))
    more = [] if gains is None else [pl.BlockSpec((2, extra, gains.shape[2]), lambda q, _: (q, 0, 0))]
    shape = jax.ShapeDtypeStruct((PLANE, shards, depth + extra, cols), bf16)
    return grid_call(
        body,
        (PLANE,),
        [pl.BlockSpec((rows, 2 * depth), lambda q, _: (0, q)), whole] + more,
        [pl.BlockSpec((1, shards, depth + extra, cols), lambda q, _: (q, 0, 0, 0))] * 2,
        [shape] * 2,
        2 * rows * width * shards * cols,
        rows * width * 4 + width * shards * cols * 2,
    )(spot, normed, y, *([] if gains is None else [gains]))


def out_blocks_grad(spot, heads_out, grads, shards):
    rows, width = grads.shape
    cols, depth = width // PLANE // 2, heads_out.shape[1] // shards

    def body(spot, x_ref, y_ref, *o_refs):
        for n, core in ((0, spot[1]), (1, 1 - spot[1])):
            total = tn(x_ref[...], of_core(y_ref, core, cols)).astype(bf16)
            for s in range(shards):
                o_refs[n][0, s] = folded(total[s * depth : (s + 1) * depth])

    shape = jax.ShapeDtypeStruct((PLANE, shards, depth // 2, 2 * cols), bf16)
    return grid_call(
        body,
        (PLANE,),
        [
            pl.BlockSpec((rows, heads_out.shape[1]), lambda q, _: (0, 0)),
            pl.BlockSpec((rows, 2 * cols), lambda q, _: (0, q)),
        ],
        [pl.BlockSpec((1, shards, depth // 2, 2 * cols), lambda q, _: (q, 0, 0, 0))] * 2,
        [shape] * 2,
        2 * rows * width * heads_out.shape[1],
        rows * width * 4 + width * heads_out.shape[1] * 2,
    )(spot, heads_out, grads)


def finish_pairs(spot, own, cos, sin, deps=()):
    _, rows, width = own.shape

    def body(spot, a_ref, cos_ref, sin_ref, o_ref):
        k = a_ref[0].astype(f32)
        o_ref[0] = (k * cos_ref[...] - swap_halves(k) * sin_ref[...]).astype(bf16)
        o_ref[1] = a_ref[1]

    tile = pl.BlockSpec((2, rows, LANES), lambda s, _: (0, 0, s))
    table = pl.BlockSpec((rows, LANES), lambda s, _: (0, 0))
    return grid_call(
        body,
        (width // LANES,),
        [tile, table, table],
        tile,
        jax.ShapeDtypeStruct(own.shape, bf16),
        own.size * 6,
        own.size * 4,
        deps=deps,
    )(spot, own, cos, sin)


def lanes_of(x_refs, core, depth):
    return jnp.concatenate(
        [
            jnp.concatenate([lanes_at(x, 2 * q + core, depth) for q in range(PLANE)], 1)
            for x in x_refs
        ],
        0,
    )


def gate_up(spot, xs, own, other):
    span, width = xs[0].shape
    rows = span * len(xs)
    shards, half, cols = own[0].shape
    depth = half // PLANE
    count = len(xs)

    def body(spot, *refs):
        x_refs, (og_ref, ou_ref, tg_ref, tu_ref, go_ref, uo_ref, i_ref) = refs[:count], refs[count:]
        core = spot[1]
        left, right = lanes_of(x_refs, core, depth), lanes_of(x_refs, 1 - core, depth)
        gate = nn(left, og_ref[0]) + nn(right, tg_ref[0])
        up = nn(left, ou_ref[0]) + nn(right, tu_ref[0])
        go_ref[...] = gate.astype(bf16)
        uo_ref[...] = up.astype(bf16)
        i_ref[...] = (gate / (1.0 + jnp.exp(-gate)) * up).astype(bf16)

    weight = pl.BlockSpec((1, half, cols), lambda s, _: (s, 0, 0))
    tile = pl.BlockSpec((rows, cols), lambda s, _: (0, s))
    shape = jax.ShapeDtypeStruct((rows, shards * cols), bf16)
    return grid_call(
        body,
        (shards,),
        [pl.BlockSpec((span, width), lambda s, _: (0, 0))] * count + [weight] * 4,
        [tile] * 3,
        [shape] * 3,
        4 * rows * width * shards * cols,
        own[0].size * 8 + rows * width * 10,
    )(spot, *xs, *own, *other)


def inner_grads(spot, gs, own, other, gate, up, deps=()):
    span, width = gs[0].shape
    rows = span * len(gs)
    shards, _, deep, cols = own.shape
    depth, cols = cols // 2, 2 * deep
    count = len(gs)

    def body(spot, *refs):
        x_refs, (own_ref, other_ref, g_ref, u_ref, dg_ref, du_ref) = refs[:count], refs[count:]
        core = spot[1]
        grad = jnp.zeros((rows, cols), f32)
        for w_ref, at in ((own_ref, core), (other_ref, 1 - core)):
            w = jnp.concatenate([unfolded(w_ref[0, q]) for q in range(PLANE)], 1)
            grad += nt(lanes_of(x_refs, at, depth), w)
        gate, up = g_ref[...].astype(f32), u_ref[...].astype(f32)
        s = 1.0 / (1.0 + jnp.exp(-gate))
        dg_ref[...] = (grad * up * s * (1.0 + gate * (1.0 - s))).astype(bf16)
        du_ref[...] = (grad * gate * s).astype(bf16)

    tile = pl.BlockSpec((rows, cols), lambda s, _: (0, s))
    weight = pl.BlockSpec((1, PLANE, deep, 2 * depth), lambda s, _: (s, 0, 0, 0))
    shape = jax.ShapeDtypeStruct((rows, shards * cols), bf16)
    return grid_call(
        body,
        (shards,),
        [pl.BlockSpec((span, width), lambda s, _: (0, 0))] * count + [weight, weight, tile, tile],
        [tile] * 2,
        [shape] * 2,
        2 * rows * width * shards * cols,
        own.size * 4 + rows * width * 10,
        deps=deps,
    )(spot, *gs, own, other, gate, up)


def split_rows(total, o_refs, at, depth):
    span = total.shape[0] // len(o_refs)
    for r, o_ref in enumerate(o_refs):
        o_ref[:, pl.ds(pl.multiple_of(at * depth, depth), depth)] = total[r * span : (r + 1) * span].astype(bf16)


def down(spot, inner, own, other, deps=()):
    rows, width = inner.shape
    shards, _, deep, cols = own.shape
    depth = cols // 2
    span = rows // PLANE

    def body(spot, x_ref, own_ref, other_ref, *o_refs):
        core = spot[1]
        for w_ref, at in ((own_ref, core), (other_ref, 1 - core)):
            w = jnp.concatenate([unfolded(w_ref[s, 0]) for s in range(shards)], 0)
            split_rows(nn(x_ref[...], w), o_refs, at, depth)

    weight = pl.BlockSpec((shards, 1, deep, cols), lambda q, _: (0, q, 0, 0))
    return grid_call(
        body,
        (PLANE,),
        [pl.BlockSpec((rows, width), lambda q, _: (0, 0)), weight, weight],
        [pl.BlockSpec((span, 2 * depth), lambda q, _: (0, q))] * PLANE,
        [jax.ShapeDtypeStruct((span, 2 * PLANE * depth), bf16)] * PLANE,
        4 * rows * width * PLANE * depth,
        own.size * 4 + rows * width * 4,
        deps=deps,
    )(spot, inner, own, other)


def normed_grads(spot, d_gate, d_up, own, other):
    rows, width = d_gate.shape
    shards, half, cols = own[0].shape
    depth = half // PLANE
    span = rows // PLANE

    def body(spot, g_ref, u_ref, og_ref, ou_ref, tg_ref, tu_ref, *o_refs):
        core = spot[1]
        for gate_ref, up_ref, at in ((og_ref, ou_ref, core), (tg_ref, tu_ref, 1 - core)):
            total = nt(g_ref[...], jnp.concatenate([gate_ref[s] for s in range(shards)], 1))
            total += nt(u_ref[...], jnp.concatenate([up_ref[s] for s in range(shards)], 1))
            split_rows(total, o_refs, at, depth)

    weight = pl.BlockSpec((shards, depth, cols), lambda q, _: (0, q, 0))
    left = pl.BlockSpec((rows, width), lambda q, _: (0, 0))
    return grid_call(
        body,
        (PLANE,),
        [left, left] + [weight] * 4,
        [pl.BlockSpec((span, 2 * depth), lambda q, _: (0, q))] * PLANE,
        [jax.ShapeDtypeStruct((span, 2 * half), bf16)] * PLANE,
        8 * rows * width * half,
        own[0].size * 8 + rows * width * 6,
    )(spot, d_gate, d_up, *own, *other)


def turned(x_refs, xt_ref):
    at = 0
    for x_ref in x_refs:
        xt_ref[:, at : at + x_ref.shape[0]] = x_ref[...].T
        at += x_ref.shape[0]


def summed(xt_ref, ys):
    total, at = None, 0
    for y in ys:
        part = nn(xt_ref[:, at : at + y.shape[0]], y)
        total, at = (part if total is None else total + part), at + y.shape[0]
    return total


def column_weight_grad(spot, xs, ys, shards, deps=()):
    span, width = xs[0].shape
    rows = span * len(xs)
    cols = ys[0].shape[1] // shards
    depth = width // PLANE // 2
    count = len(xs)
    pair = 2

    def body(spot, *refs):
        x_refs, y_refs, o_refs, xt_ref = refs[:count], refs[count:-3], refs[-3:-1], refs[-1]

        @pl.when(pl.program_id(1) == 0)
        def _():
            turned(x_refs, xt_ref)

        total = summed(xt_ref, [r[...] for r in y_refs]).astype(bf16)
        first = spot[1] == 0
        for q in range(pair):
            a = total[2 * q * depth : (2 * q + 1) * depth]
            b = total[(2 * q + 1) * depth : (2 * q + 2) * depth]
            o_refs[0][0, q] = jnp.where(first, a, b)
            o_refs[1][0, q] = jnp.where(first, b, a)

    shape = jax.ShapeDtypeStruct((shards, PLANE, depth, cols), bf16)
    return grid_call(
        body,
        (PLANE // pair, shards),
        [pl.BlockSpec((span, 2 * pair * depth), lambda q, s, _: (0, q))] * count
        + [pl.BlockSpec((y.shape[0], cols), lambda q, s, _: (0, s)) for y in ys],
        [pl.BlockSpec((1, pair, depth, cols), lambda q, s, _: (s, q, 0, 0))] * 2,
        [shape] * 2,
        2 * rows * width * shards * cols,
        rows * width * 6 + width * shards * cols * 2,
        [pltpu.VMEM((2 * pair * depth, rows), bf16)],
        deps=deps,
    )(spot, *xs, *ys)


def row_weight_grad(spot, xs, ys, shards):
    span, width = ys[0].shape
    rows = span * len(ys)
    tall = xs[0].shape[1] // shards
    depth = width // PLANE // 2
    count = len(xs)
    pair = 2 if shards % 2 == 0 else 1

    def body(spot, *refs):
        x_refs, y_refs, o_refs, xt_ref = refs[:count], refs[count:-3], refs[-3:-1], refs[-1]

        @pl.when(pl.program_id(1) == 0)
        def _():
            turned(x_refs, xt_ref)

        y = jnp.concatenate([r[...] for r in y_refs], 0)
        total = nn(xt_ref[...], y).astype(bf16)
        first = spot[1] == 0
        for s in range(pair):
            part = total[s * tall : (s + 1) * tall]
            a, b = folded(part[:, :depth]), folded(part[:, depth:])
            o_refs[0][s, 0] = jnp.where(first, a, b)
            o_refs[1][s, 0] = jnp.where(first, b, a)

    shape = jax.ShapeDtypeStruct((shards, PLANE, tall // 2, 2 * depth), bf16)
    return grid_call(
        body,
        (shards // pair, PLANE),
        [pl.BlockSpec((x.shape[0], pair * tall), lambda s, q, _: (0, s)) for x in xs]
        + [pl.BlockSpec((span, 2 * depth), lambda s, q, _: (0, q))] * len(ys),
        [pl.BlockSpec((pair, 1, tall // 2, 2 * depth), lambda s, q, _: (s, q, 0, 0))] * 2,
        [shape] * 2,
        2 * rows * width * shards * tall,
        rows * width * 6 + width * shards * tall * 2,
        [pltpu.VMEM((pair * tall, rows), bf16)],
    )(spot, *xs, *ys)


def hop(a, bits):
    n = lax.axis_size("dp")
    return lax.ppermute(a, "dp", [(i, i ^ bits) for i in range(n)])


def added(a, b):
    return (a.astype(f32) + b.astype(f32)).astype(a.dtype)


def plane_gather(a):
    return [a] + [hop(a, 2 * r) for r in range(1, PLANE)]


def plane_scatter(blocks):
    total = blocks[0].astype(f32)
    for r in range(1, PLANE):
        total += hop(blocks[r], 2 * r).astype(f32)
    return total


def shift(a, step):
    n = lax.axis_size("tensor")
    return lax.ppermute(a, "tensor", [(i, (i + step) % n) for i in range(n)])


def line_gather(a):
    return [a] + [shift(a, s) for s in range(1, lax.axis_size("tensor"))]


def line_scatter(blocks):
    n, place = lax.axis_size("tensor"), lax.axis_index("tensor")
    total = lax.dynamic_index_in_dim(blocks, place, 0, keepdims=False).astype(f32)
    for step in range(1, n):
        mine = lax.dynamic_index_in_dim(blocks, lax.rem(place + step, n), 0, keepdims=False)
        total += shift(mine, step).astype(f32)
    return total


def after(a, *others):
    others = jax.tree.leaves(others)
    place = pl.BlockSpec(memory_space=pl.ANY)
    return pl.pallas_call(
        lambda *refs: None,
        in_specs=[place] * (1 + len(others)),
        out_specs=place,
        out_shape=jax.ShapeDtypeStruct(a.shape, a.dtype),
        input_output_aliases={0: 0},
        cost_estimate=pl.CostEstimate(flops=1, bytes_accessed=1, transcendentals=0),
    )(a, *others)


def by_chip(parts, chip):
    a, b, c, d = parts
    odd = (chip & 1) == 1
    a, b, c, d = (
        jnp.where(odd, b, a),
        jnp.where(odd, a, b),
        jnp.where(odd, d, c),
        jnp.where(odd, c, d),
    )
    high = (chip & 2) == 2
    return (
        jnp.where(high, c, a),
        jnp.where(high, d, b),
        jnp.where(high, a, c),
        jnp.where(high, b, d),
    )


def trade(pieces, axis, chip):
    come = []
    for r in range(PLANE):
        piece = lax.dynamic_index_in_dim(pieces, chip ^ r, axis, keepdims=False)
        come.append(piece if r == 0 else hop(piece, 2 * r))
    return by_chip(come, chip)


def sum_all(pair, chip):
    mine = added(pair[0], hop(pair[1], 1))
    own = [lax.dynamic_index_in_dim(mine, chip ^ r, 0, keepdims=False) for r in range(PLANE)]
    return line_scatter(plane_scatter(own).astype(bf16))


def rotary_tables(positions):
    half_size = HD // 2
    frequency = THETA ** (-2.0 * jnp.arange(half_size, dtype=f32) / HD)
    angles = positions.astype(f32)[:, None] * frequency[None, :]
    cos, sin = jnp.cos(angles), jnp.sin(angles)
    return (
        jnp.concatenate([cos, cos] * (LANES // HD), -1),
        jnp.concatenate([-sin, sin] * (LANES // HD), -1),
    )


def norm_backward(grad_scaled, unrounded, norm_scale):
    return norm_scale * (grad_scaled - unrounded * jnp.mean(unrounded * grad_scaled, -1, keepdims=True))


def shards(
    tokens, segments, attn_norm, w_query, w_key, w_value, w_out, mlp_norm, w_gate, w_up, w_down, cotangent
):
    dp_count, tp_count = lax.axis_size("dp"), lax.axis_size("tensor")
    groups = dp_count // 8
    place = lax.axis_index("tensor")
    index = lax.axis_index("dp")
    core, chip = index & 1, (index >> 1) & 3
    seqs, span, width = tokens.shape
    rows = seqs * span
    block = width // 8

    group_sets = [[g * 8 + l for g in range(groups)] for l in range(8)]

    def widen(a, axis):
        if groups == 1:
            return a
        return lax.all_gather(a, "dp", axis=axis, tiled=True, axis_index_groups=group_sets)

    def narrow(a, axis):
        if groups == 1:
            return a
        return lax.psum_scatter(
            a.astype(bf16), "dp", scatter_dimension=axis, tiled=True, axis_index_groups=group_sets
        )

    def inward(a):
        if groups == 1:
            return a
        lead = a.shape[:-1]
        return jnp.swapaxes(a.reshape(lead + (groups, 8, -1)), -3, -2).reshape(lead + (-1,))

    def outward(a):
        if groups == 1:
            return a
        lead = a.shape[:-1]
        return jnp.swapaxes(a.reshape(lead + (8, groups, -1)), -3, -2).reshape(lead + (-1,))

    eight = [[g * 8 + l for l in range(8)] for g in range(groups)]

    def along(a):
        return lax.all_gather(a, "tensor", axis=0, tiled=False)

    def in_plane(a):
        if groups == 1:
            return lax.all_gather(a, "dp", axis=0, tiled=False)
        return lax.all_gather(a, "dp", axis=0, tiled=False, axis_index_groups=eight)

    tokens = inward(tokens).reshape(rows, width)
    cotangent = inward(cotangent).reshape(rows, width)
    attn_norm, mlp_norm = widen(attn_norm, 0), widen(mlp_norm, 0)
    w_query, w_key, w_value = widen(w_query, 0), widen(w_key, 0), widen(w_value, 0)
    w_gate, w_up = widen(w_gate, 0), widen(w_up, 0)
    w_out, w_down = widen(w_out, 1), widen(w_down, 1)

    kv_cols = 2 * w_key.shape[1]
    kv_group = w_query.shape[1] // w_key.shape[1]
    gains = jnp.concatenate(
        [
            jnp.pad(attn_norm, (0, kv_cols - block))[None],
            jnp.pad(mlp_norm, (0, kv_cols - block))[None],
            jnp.zeros((14, kv_cols), bf16),
        ],
        0,
    )
    near_kv = line_gather(jnp.concatenate([jnp.concatenate([w_key, w_value], 1), gains], 0))
    lines = w_down.reshape(PLANE, 2, -1, block)
    pieces = jnp.stack(
        [
            jnp.swapaxes(w_gate.reshape(block, PLANE, -1), 0, 1),
            jnp.swapaxes(w_up.reshape(block, PLANE, -1), 0, 1),
            jnp.concatenate([lines[:, 0], lines[:, 1]], 2),
        ],
        1,
    )
    all_kv = in_plane(jnp.stack(near_kv, 0))
    near = jnp.stack(trade(after(pieces, all_kv), 0, chip), 1)
    gain_one = all_kv[:, 0, block, :block].reshape(width).astype(f32)
    gain_two = all_kv[:, 0, block + 1, :block].reshape(width).astype(f32)
    lined = line_gather(after(jnp.stack([w_query, folded(w_out)], 0), near_kv[1:]))
    lined_q, lined_out = (jnp.stack([a[n] for a in lined], 0) for n in range(2))
    chunks = [slice(b * span, (b + 1) * span) for b in range(seqs)]

    spot = jnp.stack([place, core, chip]).astype(jnp.int32)
    cos, sin = rotary_tables(place * span + jnp.arange(span, dtype=jnp.int32))
    cos_rows, sin_rows = jnp.tile(cos, (seqs, 1)), jnp.tile(sin, (seqs, 1))
    x = tokens.astype(f32)
    norm_one = lax.rsqrt(jnp.mean(x * x, -1, keepdims=True) + EPS)
    scaled_one = (x * norm_one).astype(bf16)
    normed_one = (scaled_one.astype(f32) * gain_one).astype(bf16)
    pair = project_pairs(spot, normed_one, all_kv, cos_rows, sin_rows, block, deps=lined[1:])
    pairs = along(pair)
    tall = near.shape[1] * near.shape[2]
    own_gate, own_up = along(after(near[0].reshape(tall, -1), pair)), along(after(near[1].reshape(tall, -1), pair))

    def both_cores(blocks):
        return blocks + [hop(b, 1) for b in blocks]

    all_q = plane_gather(after(lined_q, pair))
    all_out = plane_gather(after(lined_out, all_q[1:]))
    late = after(cotangent, all_q[1:])
    cot_full = [plane_gather(late[c]) for c in chunks]
    all_q, all_out = both_cores(all_q), both_cores(all_out)
    queries = project_queries(spot, normed_one, all_q, cos_rows, sin_rows)

    seg_blocks = segments.reshape(seqs, tp_count, span)
    own_seg = lax.dynamic_index_in_dim(seg_blocks, place, 1, keepdims=False)
    here = jnp.arange(span, dtype=jnp.int32)
    bias = []
    for j in range(tp_count):
        key_seg = lax.dynamic_index_in_dim(seg_blocks, jnp.maximum(place - j, 0), 1, keepdims=False)
        allowed = key_seg[:, :, None] == own_seg[:, None, :]
        if j == 0:
            allowed &= here[None, :, None] <= here[None, None, :]
        bias.append(jnp.where(allowed, 0.0, -1e30).astype(f32))
    bias = jnp.concatenate(bias, 1)
    heads_out, lse = attend(spot, queries, pairs, bias, span, kv_group)
    residual = project_out(spot, heads_out, all_out, tokens, deps=cot_full)

    norm_two = lax.rsqrt(jnp.mean(residual * residual, -1, keepdims=True) + EPS)
    scaled_two = (residual * norm_two).astype(bf16)
    normed_two = (scaled_two.astype(f32) * gain_two).astype(bf16)
    full_two = []
    for c in chunks:
        full_two.append(plane_gather(after(normed_two[c], full_two[-1][1:] if full_two else ())))
    own_gate, own_up = after(own_gate, normed_two), after(own_up, normed_two)
    own_in = (own_gate, own_up)
    other_in = (hop(own_gate, 1), hop(own_up, 1))
    own_down = along(after(near[2], residual))
    other_down = hop(own_down, 1)
    forward = [gate_up(spot, f, own_in, other_in) for f in full_two]
    inner = [f[2] for f in forward]

    def core_sum(pair):
        return added(pair[0], hop(pair[1], 1))

    def line_sum(a):
        return lax.psum_scatter(a, "tensor", scatter_dimension=0, tiled=False)

    down_parts = row_weight_grad(spot, inner, sum(cot_full, []), tp_count)
    down_pair = core_sum(down_parts)
    down_sum = line_sum(down_pair)
    d_gate, d_up, to_plane = [], [], []
    for b, (g, f) in enumerate(zip(cot_full, forward)):
        deps = down_parts if b == 0 else [down_pair, to_plane[-1]]
        dg, du = inner_grads(spot, g, own_down, other_down, f[0], f[1], deps=deps)
        d_gate.append(dg)
        d_up.append(du)
        to_plane.append(normed_grads(spot, dg, du, own_in, other_in))
    grad_normed_two = jnp.concatenate([plane_scatter(p) for p in to_plane], 0)
    tokens_two = sum(full_two, [])
    gate_parts = column_weight_grad(spot, tokens_two, d_gate, tp_count, deps=to_plane[-1])
    gate_pair = core_sum(gate_parts)
    up_parts = column_weight_grad(spot, tokens_two, d_up, tp_count, deps=gate_parts)
    up_pair = core_sum(up_parts)
    gate_sum = line_sum(gate_pair)

    gain_two_terms = jnp.sum(scaled_two.astype(f32) * grad_normed_two, 0)
    unrounded_two = residual * norm_two
    grad_residual = cotangent.astype(f32) + norm_backward(
        grad_normed_two * gain_two, unrounded_two, norm_two
    )

    grad_low = grad_residual.astype(bf16)
    grad_heads = unproject_out(spot, grad_low, all_out, deps=up_parts)
    out_parts = out_blocks_grad(spot, heads_out, grad_low, tp_count)
    deps = [out_parts, gate_pair, up_pair, down_sum]
    dq, dkv = unattend(spot, queries, grad_heads, pairs, bias, lse, cos, sin, span, kv_group, deps=deps)
    dkv = line_sum(after(dkv, gate_sum))
    grad_out = unfolded(sum_all((out_parts[0], after(out_parts[1], dq)), chip))
    query_parts = in_blocks_grad(spot, normed_one, dq, None, None, tp_count)
    grad_query = sum_all(query_parts, chip)
    to_rows = [down(spot, i, own_down, other_down, deps=query_parts) for i in inner]
    mixed = (residual + jnp.concatenate([plane_scatter(r) for r in to_rows], 0)).astype(bf16)
    up_sum = line_sum(after(up_pair, dkv))

    dkv = finish_pairs(spot, dkv, cos_rows, sin_rows, deps=[grad_out, grad_query])
    grad_normed_one = unproject_in(spot, dq, dkv, all_q, all_kv)
    gain_one_terms = jnp.sum(scaled_one.astype(f32) * grad_normed_one, 0)
    gain_terms = jnp.stack([gain_one_terms.reshape(8, block), gain_two_terms.reshape(8, block)], 1)
    gain_terms = jnp.pad(gain_terms, ((0, 0), (0, 14), (0, kv_cols - block)))
    kv_parts = in_blocks_grad(spot, normed_one, dq, dkv, gain_terms, tp_count)
    kv_sum = sum_all(kv_parts, chip)
    grad_tokens = grad_residual + norm_backward(grad_normed_one * gain_one, x * norm_one, norm_one)
    grad_tokens = grad_tokens.astype(bf16)
    sums = jnp.stack([down_sum, gate_sum, up_sum], 1)
    come = trade(sums, 0, chip)
    grad_down = jnp.concatenate([jnp.concatenate([c[0, :, :block], c[0, :, block:]], 0) for c in come], 0)
    grad_gate, grad_up = (jnp.concatenate([c[n] for c in come], 1) for n in (1, 2))

    def gain_share(line):
        line = narrow(line, 0)
        share = line.shape[0] // tp_count
        return lax.dynamic_slice_in_dim(line, place * share, share, 0).astype(f32)

    half = kv_cols // 2
    return (
        outward(mixed).reshape(seqs, span, width),
        outward(grad_tokens).reshape(seqs, span, width),
        gain_share(kv_sum[block, :block]),
        narrow(grad_query, 0).astype(f32),
        narrow(kv_sum[:block, :half], 0).astype(f32),
        narrow(kv_sum[:block, half:], 0).astype(f32),
        narrow(grad_out, 1).astype(f32),
        gain_share(kv_sum[block + 1, :block]),
        narrow(grad_gate, 0).astype(f32),
        narrow(grad_up, 0).astype(f32),
        narrow(grad_down, 1).astype(f32),
    )


def solution(mesh):
    placed = (
        P("dp", "tensor", None),
        P("dp", None),
        P("dp"),
        P("dp", "tensor"),
        P("dp", "tensor"),
        P("dp", "tensor"),
        P("tensor", "dp"),
        P("dp"),
        P("dp", "tensor"),
        P("dp", "tensor"),
        P("tensor", "dp"),
        P("dp", "tensor", None),
    )
    return jax.shard_map(
        shards,
        mesh=mesh,
        in_specs=placed,
        out_specs=(
            P("dp", "tensor", None),
            P("dp", "tensor", None),
            P(("dp", "tensor")),
            P("dp", "tensor"),
            P("dp", "tensor"),
            P("dp", "tensor"),
            P("tensor", "dp"),
            P(("dp", "tensor")),
            P("dp", "tensor"),
            P("dp", "tensor"),
            P("tensor", "dp"),
        ),
        check_vma=False,
    )
```

time: 1590 us -> 1250 us (0.79)
  waiting for transfers between devices: 711 us -> 595 us
  local copies, waits for them, and re-layouts: 166 us -> 53.3 us
  other arithmetic: 135 us -> 83.7 us
  Pallas kernels: 415 us -> 378 us
  blocking collectives: 19.7 us -> 0 us
    all_gather x8 -> x5, waiting for transfers between devices: 204 us -> 30.6 us  [the longest x1 30.6 us: in_plane(): return lax.all_gather(a, 'dp', axis=0, tiled=False)]
    ppermute x71 -> x62, waiting for transfers between devices: 232 us -> 399 us  [hop(): return lax.ppermute(a, 'dp', [(i, i ^ bits) for i in range(n)])]
    ppermute x6 -> x15, waiting for transfers between devices: 135 us -> 58.8 us  [shift(): return lax.ppermute(a, 'tensor', [(i, (i + step) % n) for i in range(n)])]
    another operation x4 -> x0, local copies, waits for them, and re-layouts: 45.7 us -> none  [the longest x1 21.5 us: lines(): return jnp.stack(pair, 3).reshape(tp_count, tall, width)]
    pallas_call x21 -> x36, Pallas kernels: 388 us -> 351 us  [the longest x20 316 us: grid_call(): return lambda spot, *arrays: run(spot, *deps, *arrays)]
    reduce_scatter x6 -> x4, waiting for transfers between devices: 138 us -> 106 us  [line_sum(): return lax.psum_scatter(a, 'tensor', scatter_dimension=0, tiled=False)]
    another operation x10 -> x12, other arithmetic: 40.4 us -> 12.5 us  [the longest x2 3.41 us: shards(): lined_q, lined_out = (jnp.stack([a[n] for a in lined], 0) for n in range(2))]
    ppermute x6 -> x15, starting transfers between devices: 36.3 us -> 57.2 us  [shift(): return lax.ppermute(a, 'tensor', [(i, (i + step) % n) for i in range(n)])]
  transfers between devices with their start and end apart: 91 -> 86, of which waited for: 44 -> 34; matrix products, arithmetic and copies ran while one was open for 18% -> 9% of each run, Pallas kernels for 24% -> 30%
where the time goes in v2:
time: 1250 us; the launch traced here: 1240 us
  waiting for transfers between devices  595 us (48%)
  Pallas kernels  378 us (30%)
  starting transfers between devices  117 us (9%)
  other arithmetic  83.7 us (7%)
  local copies, waits for them, and re-layouts  53.3 us (4%)
  between operations  15.7 us (1%)
    ppermute x62, waiting for transfers between devices, hop(): return lax.ppermute(a, 'dp', [(i, i ^ bits) for i in range(n)])  399 us
    pallas_call x20, Pallas kernels, grid_call(): return lambda spot, *arrays: run(spot, *deps, *arrays)  316 us
    reduce_scatter x4, waiting for transfers between devices, line_sum(): return lax.psum_scatter(a, 'tensor', scatter_dimension=0, tiled=False)  106 us
    ppermute x15, waiting for transfers between devices, shift(): return lax.ppermute(a, 'tensor', [(i, (i + step) % n) for i in range(n)])  58.8 us
    ppermute x62, starting transfers between devices, hop(): return lax.ppermute(a, 'dp', [(i, i ^ bits) for i in range(n)])  58.5 us
    ppermute x15, starting transfers between devices, shift(): return lax.ppermute(a, 'tensor', [(i, (i + step) % n) for i in range(n)])  57.2 us
    pallas_call x1, Pallas kernels, unattend(): call(functools.partial(unattend_kernel, count, group, len(deps)), flops=r...  34.6 us
    all_gather x1, waiting for transfers between devices, in_plane(): return lax.all_gather(a, 'dp', axis=0, tiled=False)  30.6 us
  transfers between devices with their start and end apart: 86, of which 34 were waited for; matrix products, arithmetic and copies ran while one was open for 9% of the time, Pallas kernels for 30%

profile of v2, /device:TPU:0, one launch (start us, length us, event | category | flops | bytes accessed | tf_op | source)
XLA Modules:
  0.0 1242.0 jit_solution(13361031237262116769)
XLA Ops:
  35.1 30.6 %all-gather.11.cloned.1.call-done = bf16[32,272,256]{2,1,0:T(8,128)(2,1)} async-done(((bf16[4,272,256]{2,1,0:T(8,128)(2,1)}), bf16[32,272,256]{2,1,0:T(8,128)(2,1)}) %all-gather.11.cloned.1.call-update) | async-done | bytes 4456464 | tf_op jit(solution)/shard_map/all_gather | solution.py:913
  144.1 19.9 %collective-permute-done.6.refs_1_.refs_2_.refs_3_ = bf16[4,256,512]{2,1,0:T(8,128)(2,1)S(1)} collective-permute-done((bf16[4,256,512]{2,1,0:T(8,128)(2,1)}, bf16[4,256,512]{2,1,0:T(8,128)(2,1)S(1)}, u32[]{:S(2)}, u32[]{:S(2)}) %collective-permute-start.6) | collective-permute-done | bytes 1048608 | tf_op jit(solution)/shard_map/ppermute | solution.py:772
  164.0 22.7 %collective-permute-done.7.refs_2_.refs_3_.refs_4_ = bf16[4,256,512]{2,1,0:T(8,128)(2,1)S(1)} collective-permute-done((bf16[4,256,512]{2,1,0:T(8,128)(2,1)}, bf16[4,256,512]{2,1,0:T(8,128)(2,1)S(1)}, u32[]{:S(2)}, u32[]{:S(2)}) %collective-permute-start.7) | collective-permute-done | bytes 1048608 | tf_op jit(solution)/shard_map/ppermute | solution.py:772
  191.7 22.3 %collective-permute-done.19.refs_10_.refs_4_ = bf16[4,256,512]{2,1,0:T(8,128)(2,1)S(1)} collective-permute-done((bf16[4,256,512]{2,1,0:T(8,128)(2,1)}, bf16[4,256,512]{2,1,0:T(8,128)(2,1)S(1)}, u32[]{:S(2)}, u32[]{:S(2)}) %collective-permute-start.19) | collective-permute-done | bytes 1048608 | tf_op jit(solution)/shard_map/ppermute | solution.py:772
  242.9 53.5 %collective-permute-done.10.refs_2_.refs_4_ = bf16[256,2048]{1,0:T(8,128)(2,1)S(1)} collective-permute-done((bf16[256,2048]{1,0:T(8,128)(2,1)}, bf16[256,2048]{1,0:T(8,128)(2,1)S(1)}, u32[]{:S(2)}, u32[]{:S(2)}) %collective-permute-start.10) | collective-permute-done | bytes 1048608 | tf_op jit(solution)/shard_map/ppermute | solution.py:772
  303.2 20.4 %collective-permute-done.13.refs_6_.refs_8_.refs_7_ = bf16[256,2048]{1,0:T(8,128)(2,1)S(1)} collective-permute-done((bf16[256,2048]{1,0:T(8,128)(2,1)}, bf16[256,2048]{1,0:T(8,128)(2,1)S(1)}, u32[]{:S(2)}, u32[]{:S(2)}) %collective-permute-start.13) | collective-permute-done | bytes 1048608 | tf_op jit(solution)/shard_map/ppermute | solution.py:772
  335.6 27.1 %shard_map.208 = (bf16[512,2048]{1,0:T(8,128)(2,1)S(1)}, f32[2,4,8,256]{3,2,1,0:T(8,128)S(1)}) custom-call(s32[3]{0:T(128)S(1)} %pad_add_fusion.spot.place, bf16[512,2048]{1,0:T(8,128)(2,1)} %shard_map.207.refs_0_.refs_5_, bf16[4,2,512,512]{3,2,1,0:T(8,128)(2,1)} %bitcast.239, bf16[4,2,512,512]{3,2,1,0:T(8,128)(2,1)} %bitcast.240, ...), custom_call_target="tpu_custom_call" | custom-call | flops 8589934592 | bytes 4194304 | tf_op jit(solution)/shard_map/pallas_call | solution.py:123
  387.2 22.5 %collective-permute-done.26.refs_1_.refs_5_.refs_3_ = bf16[256,2048]{1,0:T(8,128)(2,1)S(1)} collective-permute-done((bf16[256,2048]{1,0:T(8,128)(2,1)}, bf16[256,2048]{1,0:T(8,128)(2,1)S(1)}, u32[]{:S(2)}, u32[]{:S(2)}) %collective-permute-start.26) | collective-permute-done | bytes 1048608 | tf_op jit(solution)/shard_map/ppermute | solution.py:772
  409.7 21.0 %collective-permute-done.27.refs_2_.refs_6_.refs_4_ = bf16[256,2048]{1,0:T(8,128)(2,1)} collective-permute-done((bf16[256,2048]{1,0:T(8,128)(2,1)}, bf16[256,2048]{1,0:T(8,128)(2,1)}, u32[]{:S(2)}, u32[]{:S(2)}) %collective-permute-start.27) | collective-permute-done | bytes 1048608 | tf_op jit(solution)/shard_map/ppermute | solution.py:772
  437.2 23.4 %shard_map.217 = (bf16[1024,2048]{1,0:T(8,128)(2,1)}, bf16[1024,2048]{1,0:T(8,128)(2,1)}, bf16[1024,2048]{1,0:T(8,128)(2,1)}) custom-call(s32[3]{0:T(128)S(1)} %pad_add_fusion.spot.place, bf16[256,2048]{1,0:T(8,128)(2,1)S(1)} %copy-done.14, bf16[256,2048]{1,0:T(8,128)(2,1)S(1)} %copy-done.28, ...), custom_call_target="tpu_custom_call" | custom-call | flops 17179869184 | bytes 37748736 | tf_op jit(solution)/shard_map/pallas_call | solution.py:295
  480.6 23.5 %shard_map.219 = (bf16[1024,2048]{1,0:T(8,128)(2,1)}, bf16[1024,2048]{1,0:T(8,128)(2,1)}, bf16[1024,2048]{1,0:T(8,128)(2,1)}) custom-call(s32[3]{0:T(128)S(1)} %pad_add_fusion.spot.place, bf16[256,2048]{1,0:T(8,128)(2,1)S(1)} %copy-done.13, bf16[256,2048]{1,0:T(8,128)(2,1)S(1)} %collective-permute-done.34.refs_1_.refs_9_.refs_7_, ...), custom_call_target="tpu_custom_call" | custom-call | flops 17179869184 | bytes 37748736 | tf_op jit(solution)/shard_map/pallas_call | solution.py:295
  504.1 26.6 %shard_map.220 = (bf16[4,4,256,512]{3,2,1,0:T(8,128)(2,1)}, bf16[4,4,256,512]{3,2,1,0:T(8,128)(2,1)}) custom-call(s32[3]{0:T(128)S(1)} %pad_add_fusion.spot.place, bf16[1024,2048]{1,0:T(8,128)(2,1)} %get-tuple-element.54.refs_0_.refs_2_, bf16[1024,2048]{1,0:T(8,128)(2,1)} %get-tuple-element.55.refs_1_.refs_2_, ...), custom_call_target="tpu_custom_call" | custom-call | flops 17179869184 | bytes 33554432 | tf_op jit(solution)/shard_map/pallas_call | solution.py:295
  563.4 24.5 %shard_map.223 = (bf16[256,2048]{1,0:T(8,128)(2,1)S(1)}, bf16[256,2048]{1,0:T(8,128)(2,1)S(1)}, bf16[256,2048]{1,0:T(8,128)(2,1)S(1)}, bf16[256,2048]{1,0:T(8,128)(2,1)}) custom-call(s32[3]{0:T(128)S(1)} %pad_add_fusion.spot.place, bf16[1024,2048]{1,0:T(8,128)(2,1)} %get-tuple-element.60.refs_0_.refs_12_, ...), custom_call_target="tpu_custom_call" | custom-call | flops 17179869184 | bytes 29360128 | tf_op jit(solution)/shard_map/pallas_call | solution.py:295
  606.8 24.5 %shard_map.225 = (bf16[256,2048]{1,0:T(8,128)(2,1)S(1)}, bf16[256,2048]{1,0:T(8,128)(2,1)S(1)}, bf16[256,2048]{1,0:T(8,128)(2,1)S(1)}, bf16[256,2048]{1,0:T(8,128)(2,1)}) custom-call(s32[3]{0:T(128)S(1)} %pad_add_fusion.spot.place, bf16[1024,2048]{1,0:T(8,128)(2,1)} %get-tuple-element.68.refs_0_.refs_13_, ...), custom_call_target="tpu_custom_call" | custom-call | flops 17179869184 | bytes 29360128 | tf_op jit(solution)/shard_map/pallas_call | solution.py:295
  631.4 27.4 %shard_map.227 = (bf16[4,4,256,512]{3,2,1,0:T(8,128)(2,1)}, bf16[4,4,256,512]{3,2,1,0:T(8,128)(2,1)}) custom-call(s32[3]{0:T(128)S(1)} %pad_add_fusion.spot.place, bf16[256,2048]{1,0:T(8,128)(2,1)S(1)} %get-tuple-element.70.refs_0_, bf16[256,2048]{1,0:T(8,128)(2,1)S(1)} %get-tuple-element.71.refs_1_, bf16[256,2048]{1,0:T(8,128)(2,1)S(1)} %get-tuple-element.72.refs_2_, ...), custom_call_target="tpu_custom_call" | custom-call | flops 17179869184 | bytes 33554432 | tf_op jit(solution)/shard_map/pallas_call | solution.py:295
  675.3 26.5 %shard_map.228 = (bf16[4,4,256,512]{3,2,1,0:T(8,128)(2,1)}, bf16[4,4,256,512]{3,2,1,0:T(8,128)(2,1)}) custom-call(s32[3]{0:T(128)S(1)} %pad_add_fusion.spot.place, bf16[4,4,256,512]{3,2,1,0:T(8,128)(2,1)} %get-tuple-element.76.refs_0_, bf16[4,4,256,512]{3,2,1,0:T(8,128)(2,1)} %get-tuple-element.77.refs_1_, bf16[256,2048]{1,0:T(8,128)(2,1)S(1)} %copy-done.15, ...), custom_call_target="tpu_custom_call" | custom-call | flops 17179869184 | bytes 33554432 | tf_op jit(solution)/shard_map/pallas_call | solution.py:295
  722.0 21.0 %collective-permute-done.42 = bf16[256,2048]{1,0:T(8,128)(2,1)S(1)} collective-permute-done((bf16[256,2048]{1,0:T(8,128)(2,1)S(1)}, bf16[256,2048]{1,0:T(8,128)(2,1)S(1)}, u32[]{:S(2)}, u32[]{:S(2)}) %collective-permute-start.42) | collective-permute-done | bytes 1048608 | tf_op jit(solution)/shard_map/ppermute | solution.py:772
  743.0 22.8 %collective-permute-done.43 = bf16[256,2048]{1,0:T(8,128)(2,1)S(1)} collective-permute-done((bf16[256,2048]{1,0:T(8,128)(2,1)S(1)}, bf16[256,2048]{1,0:T(8,128)(2,1)S(1)}, u32[]{:S(2)}, u32[]{:S(2)}) %collective-permute-start.43) | collective-permute-done | bytes 1048608 | tf_op jit(solution)/shard_map/ppermute | solution.py:772
  797.7 34.6 %shard_map.230 = (bf16[512,2048]{1,0:T(8,128)(2,1)S(1)}, bf16[4,2,512,512]{3,2,1,0:T(8,128)(2,1)}) custom-call(s32[3]{0:T(128)S(1)} %pad_add_fusion.spot.place, bf16[4,4,256,512]{3,2,1,0:T(8,128)(2,1)} %get-tuple-element.74.refs_0_, bf16[4,4,256,512]{3,2,1,0:T(8,128)(2,1)} %get-tuple-element.75.refs_1_.refs_0_, ...), custom_call_target="tpu_custom_call" | custom-call | flops 21474836480 | bytes 8388608 | tf_op jit(solution)/shard_map/pallas_call | solution.py:235
  872.0 105.6 %reduce-scatter.9.cloned.1.call-done = bf16[1,2,512,512]{3,2,1,0:T(8,128)(2,1)} async-done(((bf16[4,2,512,512]{3,2,1,0:T(8,128)(2,1)}), bf16[1,2,512,512]{3,2,1,0:T(8,128)(2,1)}) %reduce-scatter.9.cloned.1.call-update) | async-done | bytes 1048592 | tf_op jit(solution)/shard_map/reduce_scatter | solution.py:1005
  1012.9 22.5 %collective-permute-done.62 = bf16[4,256,512]{2,1,0:T(8,128)(2,1)S(1)} collective-permute-done((bf16[4,256,512]{2,1,0:T(8,128)(2,1)}, bf16[4,256,512]{2,1,0:T(8,128)(2,1)S(1)}, u32[]{:S(2)}, u32[]{:S(2)}) %collective-permute-start.62) | collective-permute-done | bytes 1048608 | tf_op jit(solution)/shard_map/ppermute | solution.py:772
  1042.3 24.2 %collective-permute-done.58 = bf16[256,512]{1,0:T(8,128)(2,1)S(1)} collective-permute-done((bf16[256,512]{1,0:T(8,128)(2,1)S(1)}, bf16[256,512]{1,0:T(8,128)(2,1)S(1)}, u32[]{:S(2)}, u32[]{:S(2)}) %collective-permute-start.58) | collective-permute-done | bytes 262176 | tf_op jit(solution)/shard_map/ppermute | solution.py:792
  1075.0 24.1 %collective-permute-done.65 = bf16[256,512]{1,0:T(8,128)(2,1)S(1)} collective-permute-done((bf16[256,512]{1,0:T(8,128)(2,1)S(1)}, bf16[256,512]{1,0:T(8,128)(2,1)S(1)}, u32[]{:S(2)}, u32[]{:S(2)}) %collective-permute-start.65) | collective-permute-done | bytes 262176 | tf_op jit(solution)/shard_map/ppermute | solution.py:792
  1163.2 29.3 %collective-permute-start.71 = (bf16[272,256]{1,0:T(8,128)(2,1)S(1)}, bf16[272,256]{1,0:T(8,128)(2,1)S(1)}, u32[]{:S(2)}, u32[]{:S(2)}) collective-permute-start(bf16[272,256]{1,0:T(8,128)(2,1)S(1)} %get-tuple-element.149), channel_id=1, source_target_pairs={{0,1},{1,2},{2,3},{3,0},{4,5},{5,6},{6,7},{7,4},{8,9},{9,10},{10,1... | collective-permute-start | bytes 417800 | tf_op jit(solution)/shard_map/ppermute | solution.py:792
  (487 shorter events, 525.8 us)
Async XLA Ops:
  27.7 307.9 %all-gather.13.cloned.1.call-start = ((), (), s32[]{:S(2)}) async-start(), calls=%async_computation.9 | async-start | bytes 5242880 | tf_op jit(solution)/shard_map/all_gather | solution.py:909
  77.9 302.1 %all-gather.17.cloned.1.call-start = ((), (), s32[]{:S(2)}) async-start(), calls=%async_computation.11 | async-start | bytes 5242880 | tf_op jit(solution)/shard_map/all_gather | solution.py:909
  132.7 247.8 %all-gather.15.cloned.1.call-start = ((), (), s32[]{:S(2)}) async-start(), calls=%async_computation.10 | async-start | bytes 5242880 | tf_op jit(solution)/shard_map/all_gather | solution.py:909
  141.3 389.4 %all-gather.19.cloned.1.call-start = ((), (), s32[]{:S(2)}) async-start(), calls=%async_computation.12 | async-start | bytes 5242880 | tf_op jit(solution)/shard_map/all_gather | solution.py:909
  233.7 62.7 %collective-permute-start.10 = (bf16[256,2048]{1,0:T(8,128)(2,1)}, bf16[256,2048]{1,0:T(8,128)(2,1)S(1)}, u32[]{:S(2)}, u32[]{:S(2)}) collective-permute-start(bf16[256,2048]{1,0:T(8,128)(2,1)} %get-tuple-element.132.refs_0_.refs_2_), channel_id=1, source_target_pairs={{0,16},{4,20},{8,24},{12,28},{16,0},{20,4},{24,8},{28,12},{1,17},{... | collective-permute-start | bytes 3145736 | tf_op jit(solution)/shard_map/ppermute | solution.py:772
  235.5 66.5 %collective-permute-start.11 = (bf16[256,2048]{1,0:T(8,128)(2,1)}, bf16[256,2048]{1,0:T(8,128)(2,1)S(1)}, u32[]{:S(2)}, u32[]{:S(2)}) collective-permute-start(bf16[256,2048]{1,0:T(8,128)(2,1)} %get-tuple-element.132.refs_0_.refs_2_), channel_id=1, source_target_pairs={{0,24},{4,28},{8,16},{12,20},{16,8},{20,12},{24,0},{28,4},{1,25},{... | collective-permute-start | bytes 3145736 | tf_op jit(solution)/shard_map/ppermute | solution.py:772
  236.5 65.6 %collective-permute-start.12 = (bf16[256,2048]{1,0:T(8,128)(2,1)}, bf16[256,2048]{1,0:T(8,128)(2,1)S(1)}, u32[]{:S(2)}, u32[]{:S(2)}) collective-permute-start(bf16[256,2048]{1,0:T(8,128)(2,1)} %get-tuple-element.131.refs_4_.refs_6_.refs_5_), channel_id=1, source_target_pairs={{0,8},{4,12},{8,0},{12,4},{16,24},{20,28},{24,16},{28,20},{1,9},{5... | collective-permute-start | bytes 3145736 | tf_op jit(solution)/shard_map/ppermute | solution.py:772
  237.2 86.3 %collective-permute-start.13 = (bf16[256,2048]{1,0:T(8,128)(2,1)}, bf16[256,2048]{1,0:T(8,128)(2,1)S(1)}, u32[]{:S(2)}, u32[]{:S(2)}) collective-permute-start(bf16[256,2048]{1,0:T(8,128)(2,1)} %get-tuple-element.131.refs_4_.refs_6_.refs_5_), channel_id=1, source_target_pairs={{0,16},{4,20},{8,24},{12,28},{16,0},{20,4},{24,8},{28,12},{1,17},{... | collective-permute-start | bytes 3145736 | tf_op jit(solution)/shard_map/ppermute | solution.py:772
  241.9 122.0 %collective-permute-start.14 = (bf16[256,2048]{1,0:T(8,128)(2,1)}, bf16[256,2048]{1,0:T(8,128)(2,1)}, u32[]{:S(2)}, u32[]{:S(2)}) collective-permute-start(bf16[256,2048]{1,0:T(8,128)(2,1)} %get-tuple-element.131.refs_4_.refs_6_.refs_5_), channel_id=1, source_target_pairs={{0,24},{4,28},{8,16},{12,20},{16,8},{20,12},{24,0},{28,4},{1,25},{... | collective-permute-start | bytes 3145736 | tf_op jit(solution)/shard_map/ppermute | solution.py:772
  297.5 66.5 %collective-permute-start.9 = (bf16[256,2048]{1,0:T(8,128)(2,1)}, bf16[256,2048]{1,0:T(8,128)(2,1)}, u32[]{:S(2)}, u32[]{:S(2)}) collective-permute-start(bf16[256,2048]{1,0:T(8,128)(2,1)} %get-tuple-element.132.refs_0_.refs_2_), channel_id=1, source_target_pairs={{0,8},{4,12},{8,0},{12,4},{16,24},{20,28},{24,16},{28,20},{1,9},{5... | collective-permute-start | bytes 3145736 | tf_op jit(solution)/shard_map/ppermute | solution.py:772
  302.1 61.9 %collective-permute-start.23 = (bf16[4,256,512]{2,1,0:T(8,128)(2,1)S(1)}, bf16[4,256,512]{2,1,0:T(8,128)(2,1)}, u32[]{:S(2)}, u32[]{:S(2)}) collective-permute-start(bf16[4,256,512]{2,1,0:T(8,128)(2,1)S(1)} %collective-permute-done.19.refs_10_.refs_4_), channel_id=1, source_target_pairs={{0,4},{4,0},{8,12},{12,8},{16,20},{20,16},{24,28},{28,24},{1,5},{5... | collective-permute-start | bytes 3145736 | tf_op jit(solution)/shard_map/ppermute | solution.py:772
  302.2 61.8 %collective-permute-start.24 = (bf16[4,256,512]{2,1,0:T(8,128)(2,1)S(1)}, bf16[4,256,512]{2,1,0:T(8,128)(2,1)}, u32[]{:S(2)}, u32[]{:S(2)}) collective-permute-start(bf16[4,256,512]{2,1,0:T(8,128)(2,1)S(1)} %collective-permute-done.20.refs_11_.refs_5_), channel_id=1, source_target_pairs={{0,4},{4,0},{8,12},{12,8},{16,20},{20,16},{24,28},{28,24},{1,5},{5... | collective-permute-start | bytes 3145736 | tf_op jit(solution)/shard_map/ppermute | solution.py:772
  387.0 409.4 %reduce-scatter.5.cloned.1.call-start = ((), (), s32[]{:S(2)}) async-start(), calls=%async_computation.4 | async-start | bytes 5242880 | tf_op jit(solution)/shard_map/reduce_scatter | solution.py:1005
  545.0 288.6 %reduce-scatter.7.cloned.1.call-start = ((), (), s32[]{:S(2)}) async-start(), calls=%async_computation.5 | async-start | bytes 5242880 | tf_op jit(solution)/shard_map/reduce_scatter | solution.py:1005
  671.7 306.0 %reduce-scatter.9.cloned.1.call-start = ((), (), s32[]{:S(2)}) async-start(), calls=%async_computation.6 | async-start | bytes 5242880 | tf_op jit(solution)/shard_map/reduce_scatter | solution.py:1005
  701.8 89.1 %collective-permute-start.46 = (bf16[4,4,256,512]{3,2,1,0:T(8,128)(2,1)}, bf16[4,4,256,512]{3,2,1,0:T(8,128)(2,1)}, u32[]{:S(2)}, u32[]{:S(2)}) collective-permute-start(bf16[4,4,256,512]{3,2,1,0:T(8,128)(2,1)} %get-tuple-element.79.refs_1_), channel_id=1, source_target_pairs={{0,4},{4,0},{8,12},{12,8},{16,20},{20,16},{24,28},{28,24},{1,5},{5... | collective-permute-start | bytes 12582920 | tf_op jit(solution)/shard_map/ppermute | solution.py:772
  703.4 62.4 %collective-permute-start.43 = (bf16[256,2048]{1,0:T(8,128)(2,1)S(1)}, bf16[256,2048]{1,0:T(8,128)(2,1)S(1)}, u32[]{:S(2)}, u32[]{:S(2)}) collective-permute-start(bf16[256,2048]{1,0:T(8,128)(2,1)S(1)} %copy-done.50), channel_id=1, source_target_pairs={{0,16},{4,20},{8,24},{12,28},{16,0},{20,4},{24,8},{28,12},{1,17},{... | collective-permute-start | bytes 3145736 | tf_op jit(solution)/shard_map/ppermute | solution.py:772
  833.6 364.0 %reduce-scatter.11.cloned.1.call-start = ((), (), s32[]{:S(2)}) async-start(), calls=%async_computation.7 | async-start | bytes 5242880 | tf_op jit(solution)/shard_map/reduce_scatter | solution.py:1005
  843.9 133.8 %collective-permute-start.60 = (bf16[4,4,256,512]{3,2,1,0:T(8,128)(2,1)}, bf16[4,4,256,512]{3,2,1,0:T(8,128)(2,1)}, u32[]{:S(2)}, u32[]{:S(2)}) collective-permute-start(bf16[4,4,256,512]{3,2,1,0:T(8,128)(2,1)} %get-tuple-element.83.refs_1_), channel_id=1, source_target_pairs={{0,4},{4,0},{8,12},{12,8},{16,20},{20,16},{24,28},{28,24},{1,5},{5... | collective-permute-start | bytes 12582920 | tf_op jit(solution)/shard_map/ppermute | solution.py:772
  851.8 136.3 %collective-permute-start.54 = (bf16[4,256,512]{2,1,0:T(8,128)(2,1)}, bf16[4,256,512]{2,1,0:T(8,128)(2,1)}, u32[]{:S(2)}, u32[]{:S(2)}) collective-permute-start(bf16[4,256,512]{2,1,0:T(8,128)(2,1)} %get-tuple-element.114), channel_id=1, source_target_pairs={{0,8},{4,12},{8,0},{12,4},{16,24},{20,28},{24,16},{28,20},{1,9},{5... | collective-permute-start | bytes 3145736 | tf_op jit(solution)/shard_map/ppermute | solution.py:772
  869.2 133.3 %collective-permute-start.55 = (bf16[4,256,512]{2,1,0:T(8,128)(2,1)}, bf16[4,256,512]{2,1,0:T(8,128)(2,1)}, u32[]{:S(2)}, u32[]{:S(2)}) collective-permute-start(bf16[4,256,512]{2,1,0:T(8,128)(2,1)} %get-tuple-element.116), channel_id=1, source_target_pairs={{0,16},{4,20},{8,24},{12,28},{16,0},{20,4},{24,8},{28,12},{1,17},{... | collective-permute-start | bytes 3145736 | tf_op jit(solution)/shard_map/ppermute | solution.py:772
  870.4 133.6 %collective-permute-start.56 = (bf16[4,256,512]{2,1,0:T(8,128)(2,1)}, bf16[4,256,512]{2,1,0:T(8,128)(2,1)}, u32[]{:S(2)}, u32[]{:S(2)}) collective-permute-start(bf16[4,256,512]{2,1,0:T(8,128)(2,1)} %get-tuple-element.115), channel_id=1, source_target_pairs={{0,24},{4,28},{8,16},{12,20},{16,8},{20,12},{24,0},{28,4},{1,25},{... | collective-permute-start | bytes 3145736 | tf_op jit(solution)/shard_map/ppermute | solution.py:772
  1002.5 118.2 %collective-permute-start.47 = (bf16[256,2048]{1,0:T(8,128)(2,1)S(1)}, bf16[256,2048]{1,0:T(8,128)(2,1)S(1)}, u32[]{:S(2)}, u32[]{:S(2)}) collective-permute-start(bf16[256,2048]{1,0:T(8,128)(2,1)S(1)} %copy-done.46), channel_id=1, source_target_pairs={{0,8},{4,12},{8,0},{12,4},{16,24},{20,28},{24,16},{28,20},{1,9},{5... | collective-permute-start | bytes 3145736 | tf_op jit(solution)/shard_map/ppermute | solution.py:772
  1004.0 121.9 %collective-permute-start.48 = (bf16[256,2048]{1,0:T(8,128)(2,1)S(1)}, bf16[256,2048]{1,0:T(8,128)(2,1)}, u32[]{:S(2)}, u32[]{:S(2)}) collective-permute-start(bf16[256,2048]{1,0:T(8,128)(2,1)S(1)} %copy-done.44), channel_id=1, source_target_pairs={{0,16},{4,20},{8,24},{12,28},{16,0},{20,4},{24,8},{28,12},{1,17},{... | collective-permute-start | bytes 3145736 | tf_op jit(solution)/shard_map/ppermute | solution.py:772
  (155 other events, 4333.2 us)
Sparse Core Ops, SparseCore 0:
  27.8 37.8 all-gather.10
  78.0 88.1 all-gather.12
  167.8 79.2 all-gather.16
  248.6 79.2 all-gather.14
  387.1 109.1 all-gather.18
  545.1 105.0 reduce-scatter.4
  671.8 105.0 reduce-scatter.6
  833.8 143.8 reduce-scatter.8
  980.1 107.6 reduce-scatter.10

commit v3 on v2

--- a/solution.py
+++ b/solution.py
@@ -465,7 +465,7 @@
     return ref[:, pl.ds(pl.multiple_of(core * depth, depth), depth)]
 
 
-def in_blocks_grad(spot, normed, dq, dkv, gains, shards):
+def in_blocks_grad(spot, normed, dq, dkv, gains, shards, deps=()):
     rows, width = normed.shape
     depth = width // PLANE // 2
     y = dq if dkv is None else dkv
@@ -494,7 +494,8 @@
         [shape] * 2,
         2 * rows * width * shards * cols,
         rows * width * 4 + width * shards * cols * 2,
-    )(spot, normed, y, *([] if gains is None else [gains]))
+    deps=deps,
+        )(spot, normed, y, *([] if gains is None else [gains]))
 
 
 def out_blocks_grad(spot, heads_out, grads, shards):
@@ -554,7 +555,11 @@
     )
 
 
-def gate_up(spot, xs, own, other):
+def still(shape, index):
+    return pl.BlockSpec(shape, index, pipeline_mode=pl.Buffered(1))
+
+
+def gate_up(spot, xs, own, other, deps=()):
     span, width = xs[0].shape
     rows = span * len(xs)
     shards, half, cols = own[0].shape
@@ -564,12 +569,15 @@
     def body(spot, *refs):
         x_refs, (og_ref, ou_ref, tg_ref, tu_ref, go_ref, uo_ref, i_ref) = refs[:count], refs[count:]
         core = spot[1]
-        left, right = lanes_of(x_refs, core, depth), lanes_of(x_refs, 1 - core, depth)
-        gate = nn(left, og_ref[0]) + nn(right, tg_ref[0])
-        up = nn(left, ou_ref[0]) + nn(right, tu_ref[0])
-        go_ref[...] = gate.astype(bf16)
-        uo_ref[...] = up.astype(bf16)
-        i_ref[...] = (gate / (1.0 + jnp.exp(-gate)) * up).astype(bf16)
+        for at in range(0, count, PLANE):
+            part = x_refs[at : at + PLANE]
+            left, right = lanes_of(part, core, depth), lanes_of(part, 1 - core, depth)
+            gate = nn(left, og_ref[0]) + nn(right, tg_ref[0])
+            up = nn(left, ou_ref[0]) + nn(right, tu_ref[0])
+            here = slice(at * span, (at + PLANE) * span)
+            go_ref[here, :] = gate.astype(bf16)
+            uo_ref[here, :] = up.astype(bf16)
+            i_ref[here, :] = (gate / (1.0 + jnp.exp(-gate)) * up).astype(bf16)
 
     weight = pl.BlockSpec((1, half, cols), lambda s, _: (s, 0, 0))
     tile = pl.BlockSpec((rows, cols), lambda s, _: (0, s))
@@ -577,46 +585,13 @@
     return grid_call(
         body,
         (shards,),
-        [pl.BlockSpec((span, width), lambda s, _: (0, 0))] * count + [weight] * 4,
+        [still((span, width), lambda s, _: (0, 0))] * count + [weight] * 4,
         [tile] * 3,
         [shape] * 3,
         4 * rows * width * shards * cols,
         own[0].size * 8 + rows * width * 10,
+        deps=deps,
     )(spot, *xs, *own, *other)
-
-
-def inner_grads(spot, gs, own, other, gate, up, deps=()):
-    span, width = gs[0].shape
-    rows = span * len(gs)
-    shards, _, deep, cols = own.shape
-    depth, cols = cols // 2, 2 * deep
-    count = len(gs)
-
-    def body(spot, *refs):
-        x_refs, (own_ref, other_ref, g_ref, u_ref, dg_ref, du_ref) = refs[:count], refs[count:]
-        core = spot[1]
-        grad = jnp.zeros((rows, cols), f32)
-        for w_ref, at in ((own_ref, core), (other_ref, 1 - core)):
-            w = jnp.concatenate([unfolded(w_ref[0, q]) for q in range(PLANE)], 1)
-            grad += nt(lanes_of(x_refs, at, depth), w)
-        gate, up = g_ref[...].astype(f32), u_ref[...].astype(f32)
-        s = 1.0 / (1.0 + jnp.exp(-gate))
-        dg_ref[...] = (grad * up * s * (1.0 + gate * (1.0 - s))).astype(bf16)
-        du_ref[...] = (grad * gate * s).astype(bf16)
-
-    tile = pl.BlockSpec((rows, cols), lambda s, _: (0, s))
-    weight = pl.BlockSpec((1, PLANE, deep, 2 * depth), lambda s, _: (s, 0, 0, 0))
-    shape = jax.ShapeDtypeStruct((rows, shards * cols), bf16)
-    return grid_call(
-        body,
-        (shards,),
-        [pl.BlockSpec((span, width), lambda s, _: (0, 0))] * count + [weight, weight, tile, tile],
-        [tile] * 2,
-        [shape] * 2,
-        2 * rows * width * shards * cols,
-        own.size * 4 + rows * width * 10,
-        deps=deps,
-    )(spot, *gs, own, other, gate, up)
 
 
 def split_rows(total, o_refs, at, depth):
@@ -625,55 +600,154 @@
         o_ref[:, pl.ds(pl.multiple_of(at * depth, depth), depth)] = total[r * span : (r + 1) * span].astype(bf16)
 
 
-def down(spot, inner, own, other, deps=()):
+def down(spot, inner, own, other, seqs, deps=()):
     rows, width = inner.shape
     shards, _, deep, cols = own.shape
     depth = cols // 2
-    span = rows // PLANE
+    tall = rows // seqs
+    span = tall // PLANE
 
     def body(spot, x_ref, own_ref, other_ref, *o_refs):
         core = spot[1]
         for w_ref, at in ((own_ref, core), (other_ref, 1 - core)):
             w = jnp.concatenate([unfolded(w_ref[s, 0]) for s in range(shards)], 0)
-            split_rows(nn(x_ref[...], w), o_refs, at, depth)
+            lanes = pl.ds(pl.multiple_of(at * depth, depth), depth)
+            for b in range(seqs):
+                total = nn(x_ref[b * tall : (b + 1) * tall, :], w).astype(bf16)
+                for r, o_ref in enumerate(o_refs):
+                    o_ref[b * span : (b + 1) * span, lanes] = total[r * span : (r + 1) * span]
 
     weight = pl.BlockSpec((shards, 1, deep, cols), lambda q, _: (0, q, 0, 0))
     return grid_call(
         body,
         (PLANE,),
-        [pl.BlockSpec((rows, width), lambda q, _: (0, 0)), weight, weight],
-        [pl.BlockSpec((span, 2 * depth), lambda q, _: (0, q))] * PLANE,
-        [jax.ShapeDtypeStruct((span, 2 * PLANE * depth), bf16)] * PLANE,
+        [still((rows, width), lambda q, _: (0, 0)), weight, weight],
+        [pl.BlockSpec((seqs * span, 2 * depth), lambda q, _: (0, q))] * PLANE,
+        [jax.ShapeDtypeStruct((seqs * span, 2 * PLANE * depth), bf16)] * PLANE,
         4 * rows * width * PLANE * depth,
         own.size * 4 + rows * width * 4,
         deps=deps,
     )(spot, inner, own, other)
 
 
-def normed_grads(spot, d_gate, d_up, own, other):
-    rows, width = d_gate.shape
-    shards, half, cols = own[0].shape
-    depth = half // PLANE
-    span = rows // PLANE
-
-    def body(spot, g_ref, u_ref, og_ref, ou_ref, tg_ref, tu_ref, *o_refs):
-        core = spot[1]
-        for gate_ref, up_ref, at in ((og_ref, ou_ref, core), (tg_ref, tu_ref, 1 - core)):
-            total = nt(g_ref[...], jnp.concatenate([gate_ref[s] for s in range(shards)], 1))
-            total += nt(u_ref[...], jnp.concatenate([up_ref[s] for s in range(shards)], 1))
-            split_rows(total, o_refs, at, depth)
-
-    weight = pl.BlockSpec((shards, depth, cols), lambda q, _: (0, q, 0))
-    left = pl.BlockSpec((rows, width), lambda q, _: (0, 0))
+def backward_chunk(spot, chunk, span, gs, own_down, other_down, gate, up, own, other, deps=()):
+    width = gs[0].shape[1]
+    rows = span * len(gs)
+    shards, _, deep, cols = own_down.shape
+    depth, cols = cols // 2, 2 * deep
+    count = len(gs)
+    half = own[0].shape[1]
+
+    def body(spot, *refs):
+        x_refs, refs = refs[:count], refs[count:]
+        own_ref, other_ref, g_ref, u_ref, og_ref, ou_ref, tg_ref, tu_ref, dg_ref, du_ref = refs[:10]
+        o_refs, (gs_ref, us_ref) = refs[10:-2], refs[-2:]
+        core, step = spot[1], pl.program_id(0)
+
+        @pl.when(step < shards)
+        def _():
+            grad = None
+            for w_ref, at in ((own_ref, core), (other_ref, 1 - core)):
+                w = jnp.concatenate([unfolded(w_ref[0, q]) for q in range(PLANE)], 1)
+                part = nt(lanes_of(x_refs, at, depth), w)
+                grad = part if grad is None else grad + part
+            gate, up = g_ref[...].astype(f32), u_ref[...].astype(f32)
+            s = 1.0 / (1.0 + jnp.exp(-gate))
+            dg = (grad * up * s * (1.0 + gate * (1.0 - s))).astype(bf16)
+            du = (grad * gate * s).astype(bf16)
+            dg_ref[...] = dg
+            du_ref[...] = du
+            gs_ref[step] = dg
+            us_ref[step] = du
+
+        @pl.when(step >= shards)
+        def _():
+            for gate_ref, up_ref, at in ((og_ref, ou_ref, core), (tg_ref, tu_ref, 1 - core)):
+                total = None
+                for d_ref, w_ref in ((gs_ref, gate_ref), (us_ref, up_ref)):
+                    left = jnp.concatenate([d_ref[s] for s in range(shards)], 1)
+                    part = nt(left, jnp.concatenate([w_ref[s] for s in range(shards)], 1))
+                    total = part if total is None else total + part
+                split_rows(total, o_refs, at, depth)
+
+    def early(t):
+        return jnp.minimum(t, shards - 1)
+
+    def late(t):
+        return jnp.maximum(t - shards, 0)
+
+    tile = pl.BlockSpec((rows, cols), lambda t, _: (0, early(t)))
+    given = pl.BlockSpec((rows, cols), lambda t, _: (chunk, early(t)))
+    first = pl.BlockSpec((1, PLANE, deep, 2 * depth), lambda t, _: (early(t), 0, 0, 0))
+    second = pl.BlockSpec((shards, depth, cols), lambda t, _: (0, late(t), 0))
+    shape = jax.ShapeDtypeStruct((rows, shards * cols), bf16)
+    outs = grid_call(
+        body,
+        (shards + PLANE,),
+        [still((span, width), lambda t, _: (chunk, 0))] * count + [first] * 2 + [given] * 2 + [second] * 4,
+        [tile] * 2 + [pl.BlockSpec((span, 2 * depth), lambda t, _: (0, late(t)))] * PLANE,
+        [shape] * 2 + [jax.ShapeDtypeStruct((span, 2 * half), bf16)] * PLANE,
+        6 * rows * width * shards * cols,
+        own_down.size * 12 + rows * width * 16,
+        [pltpu.VMEM((shards, rows, cols), bf16)] * 2,
+        deps=deps,
+    )(spot, *gs, own_down, other_down, gate, up, *own, *other)
+    return outs[0], outs[1], outs[2:]
+
+
+def norm_backward(grad_scaled, unrounded, norm_scale):
+    return norm_scale * (grad_scaled - unrounded * jnp.mean(unrounded * grad_scaled, -1, keepdims=True))
+
+
+def residual_grads(spot, parts, residual, cotangent, gain, deps=()):
+    rows, width = residual.shape
+    tall = 128
+    count, each = len(parts), len(parts[0])
+    per = rows // tall // count
+
+    def body(spot, *refs):
+        p_refs = refs[: count * each]
+        r_ref, c_ref, g_ref, o_ref, low_ref, sum_ref = refs[count * each :]
+        m = pl.program_id(0)
+
+        @pl.when(m == 0)
+        def _():
+            sum_ref[...] = jnp.zeros_like(sum_ref)
+
+        residual = r_ref[...]
+        scale = lax.rsqrt(jnp.mean(residual * residual, -1, keepdims=True) + EPS)
+        unrounded = residual * scale
+        for b in range(count):
+
+            @pl.when(m // per == b)
+            def _(b=b):
+                grad = total_of([ref[...] for ref in p_refs[b * each : (b + 1) * each]])
+                terms = unrounded.astype(bf16).astype(f32) * grad
+                sum_ref[0:1, :] += jnp.sum(terms, 0, keepdims=True)
+                out = c_ref[...].astype(f32) + norm_backward(grad * g_ref[...], unrounded, scale)
+                o_ref[...] = out
+                low_ref[...] = out.astype(bf16)
+
+    def place_of(b):
+        return lambda m, _: (jnp.clip(m - b * per, 0, per - 1), 0)
+
+    tile = pl.BlockSpec((tall, width), lambda m, _: (m, 0))
+    fixed = lambda m, _: (0, 0)
     return grid_call(
         body,
-        (PLANE,),
-        [left, left] + [weight] * 4,
-        [pl.BlockSpec((span, 2 * depth), lambda q, _: (0, q))] * PLANE,
-        [jax.ShapeDtypeStruct((span, 2 * half), bf16)] * PLANE,
-        8 * rows * width * half,
-        own[0].size * 8 + rows * width * 6,
-    )(spot, d_gate, d_up, *own, *other)
+        (rows // tall,),
+        [pl.BlockSpec((tall, width), place_of(b)) for b in range(count) for _ in range(each)]
+        + [tile, tile, pl.BlockSpec((1, width), fixed)],
+        [tile, tile, pl.BlockSpec((8, width), fixed)],
+        [
+            jax.ShapeDtypeStruct((rows, width), f32),
+            jax.ShapeDtypeStruct((rows, width), bf16),
+            jax.ShapeDtypeStruct((8, width), f32),
+        ],
+        rows * width * 20,
+        rows * width * 20,
+        deps=deps,
+    )(spot, *sum(parts, []), residual, cotangent, gain)
 
 
 def turned(x_refs, xt_ref):
@@ -691,47 +765,65 @@
     return total
 
 
-def column_weight_grad(spot, xs, ys, shards, deps=()):
+def column_weight_grads(spot, xs, ys, shards, deps=()):
     span, width = xs[0].shape
     rows = span * len(xs)
-    cols = ys[0].shape[1] // shards
+    cols = ys[0][0].shape[1] // shards
     depth = width // PLANE // 2
-    count = len(xs)
+    count, lists, pieces = len(xs), len(ys), len(ys[0])
     pair = 2
 
     def body(spot, *refs):
-        x_refs, y_refs, o_refs, xt_ref = refs[:count], refs[count:-3], refs[-3:-1], refs[-1]
-
-        @pl.when(pl.program_id(1) == 0)
+        x_refs, y_refs, o_refs, xt_ref = refs[:count], refs[count : -1 - 2 * lists], refs[-1 - 2 * lists : -1], refs[-1]
+        m, s = pl.program_id(1), pl.program_id(2)
+
+        @pl.when((m == 0) & (s == 0))
         def _():
             turned(x_refs, xt_ref)
 
-        total = summed(xt_ref, [r[...] for r in y_refs]).astype(bf16)
-        first = spot[1] == 0
-        for q in range(pair):
-            a = total[2 * q * depth : (2 * q + 1) * depth]
-            b = total[(2 * q + 1) * depth : (2 * q + 2) * depth]
-            o_refs[0][0, q] = jnp.where(first, a, b)
-            o_refs[1][0, q] = jnp.where(first, b, a)
+        for n in range(lists):
+
+            @pl.when(m == n)
+            def _(n=n):
+                mine = y_refs[n * pieces : (n + 1) * pieces]
+                total = summed(xt_ref, [r[...] for r in mine]).astype(bf16)
+                first = spot[1] == 0
+                for q in range(pair):
+                    a = total[2 * q * depth : (2 * q + 1) * depth]
+                    b = total[(2 * q + 1) * depth : (2 * q + 2) * depth]
+                    o_refs[2 * n][0, q] = jnp.where(first, a, b)
+                    o_refs[2 * n + 1][0, q] = jnp.where(first, b, a)
+
+    def column(n, m, s):
+        return jnp.where(m == n, s, jnp.where(m < n, 0, shards - 1))
 
     shape = jax.ShapeDtypeStruct((shards, PLANE, depth, cols), bf16)
-    return grid_call(
-        body,
-        (PLANE // pair, shards),
-        [pl.BlockSpec((span, 2 * pair * depth), lambda q, s, _: (0, q))] * count
-        + [pl.BlockSpec((y.shape[0], cols), lambda q, s, _: (0, s)) for y in ys],
-        [pl.BlockSpec((1, pair, depth, cols), lambda q, s, _: (s, q, 0, 0))] * 2,
-        [shape] * 2,
-        2 * rows * width * shards * cols,
-        rows * width * 6 + width * shards * cols * 2,
+    y_specs, o_specs = [], []
+    for n in range(lists):
+        y_specs += [
+            pl.BlockSpec((y.shape[0], cols), lambda q, m, s, _, n=n: (0, column(n, m, s))) for y in ys[n]
+        ]
+        o_specs += [
+            pl.BlockSpec((1, pair, depth, cols), lambda q, m, s, _, n=n: (column(n, m, s), q, 0, 0))
+        ] * 2
+    outs = grid_call(
+        body,
+        (PLANE // pair, lists, shards),
+        [pl.BlockSpec((span, 2 * pair * depth), lambda q, m, s, _: (0, q))] * count + y_specs,
+        o_specs,
+        [shape] * (2 * lists),
+        2 * lists * rows * width * shards * cols,
+        lists * rows * width * 6 + lists * width * shards * cols * 2,
         [pltpu.VMEM((2 * pair * depth, rows), bf16)],
         deps=deps,
-    )(spot, *xs, *ys)
-
-
-def row_weight_grad(spot, xs, ys, shards):
-    span, width = ys[0].shape
-    rows = span * len(ys)
+    )(spot, *xs, *sum(ys, []))
+    return [outs[2 * n : 2 * n + 2] for n in range(lists)]
+
+
+def row_weight_grad(spot, xs, ys, span, shards, deps=()):
+    width = ys[0].shape[1]
+    rows = sum(y.shape[0] for y in ys)
+    seqs = ys[0].shape[0] // span
     tall = xs[0].shape[1] // shards
     depth = width // PLANE // 2
     count = len(xs)
@@ -758,13 +850,37 @@
         body,
         (shards // pair, PLANE),
         [pl.BlockSpec((x.shape[0], pair * tall), lambda s, q, _: (0, s)) for x in xs]
-        + [pl.BlockSpec((span, 2 * depth), lambda s, q, _: (0, q))] * len(ys),
+        + [pl.BlockSpec((span, 2 * depth), lambda s, q, _, b=b: (b, q)) for b in range(seqs) for _ in ys],
         [pl.BlockSpec((pair, 1, tall // 2, 2 * depth), lambda s, q, _: (s, q, 0, 0))] * 2,
         [shape] * 2,
         2 * rows * width * shards * tall,
         rows * width * 6 + width * shards * tall * 2,
         [pltpu.VMEM((pair * tall, rows), bf16)],
-    )(spot, *xs, *ys)
+    deps=deps,
+        )(spot, *xs, *(list(ys) * seqs))
+
+
+def finish_mixed(spot, residual, blocks, deps=()):
+    rows, width = residual.shape
+    tall = min(128, rows)
+
+    def body(spot, r_ref, *refs):
+        total = r_ref[...]
+        for ref in refs[:-1]:
+            total += ref[...].astype(f32)
+        refs[-1][...] = total.astype(bf16)
+
+    tile = pl.BlockSpec((tall, width), lambda m, _: (m, 0))
+    return grid_call(
+        body,
+        (rows // tall,),
+        [tile] * (1 + len(blocks)),
+        tile,
+        jax.ShapeDtypeStruct((rows, width), bf16),
+        rows * width * 5,
+        rows * width * 14,
+        deps=deps,
+    )(spot, residual, *blocks)
 
 
 def hop(a, bits):
@@ -780,11 +896,19 @@
     return [a] + [hop(a, 2 * r) for r in range(1, PLANE)]
 
 
+def plane_trade(blocks):
+    return [blocks[0]] + [hop(blocks[r], 2 * r) for r in range(1, PLANE)]
+
+
+def total_of(blocks):
+    total = blocks[0].astype(f32)
+    for b in blocks[1:]:
+        total += b.astype(f32)
+    return total
+
+
 def plane_scatter(blocks):
-    total = blocks[0].astype(f32)
-    for r in range(1, PLANE):
-        total += hop(blocks[r], 2 * r).astype(f32)
-    return total
+    return total_of(plane_trade(blocks))
 
 
 def shift(a, step):
@@ -818,6 +942,25 @@
     )(a, *others)
 
 
+def token(*arrays, steps=2):
+    arrays = jax.tree.leaves(arrays)
+    place = pl.BlockSpec(memory_space=pl.ANY)
+
+    def body(*refs):
+        refs[-1][...] = jnp.zeros_like(refs[-1])
+
+    for _ in range(steps):
+        arrays = [
+            pl.pallas_call(
+                body,
+                in_specs=[place] * len(arrays),
+                out_specs=pl.BlockSpec(memory_space=pltpu.VMEM),
+                out_shape=jax.ShapeDtypeStruct((8, LANES), f32),
+            )(*arrays)
+        ]
+    return arrays[0]
+
+
 def by_chip(parts, chip):
     a, b, c, d = parts
     odd = (chip & 1) == 1
@@ -836,18 +979,21 @@
     )
 
 
-def trade(pieces, axis, chip):
+def trade(pieces, axis, chip, hold=lambda a: a):
     come = []
     for r in range(PLANE):
         piece = lax.dynamic_index_in_dim(pieces, chip ^ r, axis, keepdims=False)
-        come.append(piece if r == 0 else hop(piece, 2 * r))
+        come.append(hold(piece) if r == 0 else hop(piece, 2 * r))
     return by_chip(come, chip)
 
 
-def sum_all(pair, chip):
-    mine = added(pair[0], hop(pair[1], 1))
-    own = [lax.dynamic_index_in_dim(mine, chip ^ r, 0, keepdims=False) for r in range(PLANE)]
-    return line_scatter(plane_scatter(own).astype(bf16))
+def core_sum(pair, *others):
+    return added(after(pair[0], others) if others else pair[0], hop(pair[1], 1))
+
+
+def plane_sum(blocks, chip):
+    mine = [lax.dynamic_index_in_dim(blocks, chip ^ r, 0, keepdims=False) for r in range(PLANE)]
+    return plane_scatter(mine).astype(bf16)
 
 
 def rotary_tables(positions):
@@ -859,10 +1005,6 @@
         jnp.concatenate([cos, cos] * (LANES // HD), -1),
         jnp.concatenate([-sin, sin] * (LANES // HD), -1),
     )
-
-
-def norm_backward(grad_scaled, unrounded, norm_scale):
-    return norm_scale * (grad_scaled - unrounded * jnp.mean(unrounded * grad_scaled, -1, keepdims=True))
 
 
 def shards(
@@ -941,7 +1083,6 @@
         1,
     )
     all_kv = in_plane(jnp.stack(near_kv, 0))
-    near = jnp.stack(trade(after(pieces, all_kv), 0, chip), 1)
     gain_one = all_kv[:, 0, block, :block].reshape(width).astype(f32)
     gain_two = all_kv[:, 0, block + 1, :block].reshape(width).astype(f32)
     lined = line_gather(after(jnp.stack([w_query, folded(w_out)], 0), near_kv[1:]))
@@ -957,18 +1098,19 @@
     normed_one = (scaled_one.astype(f32) * gain_one).astype(bf16)
     pair = project_pairs(spot, normed_one, all_kv, cos_rows, sin_rows, block, deps=lined[1:])
     pairs = along(pair)
+    def both_cores(blocks, *others):
+        if others:
+            blocks = [after(b, others) for b in blocks]
+        return blocks + [hop(b, 1) for b in blocks]
+
+    all_q = plane_gather(after(lined_q, pair))
+    sent = after(pieces, all_q[1:])
+    all_q = both_cores(all_q)
+    queries = project_queries(spot, normed_one, all_q, cos_rows, sin_rows)
+    near = jnp.stack(trade(sent, 0, chip, lambda own: after(own, queries)), 1)
     tall = near.shape[1] * near.shape[2]
-    own_gate, own_up = along(after(near[0].reshape(tall, -1), pair)), along(after(near[1].reshape(tall, -1), pair))
-
-    def both_cores(blocks):
-        return blocks + [hop(b, 1) for b in blocks]
-
-    all_q = plane_gather(after(lined_q, pair))
-    all_out = plane_gather(after(lined_out, all_q[1:]))
-    late = after(cotangent, all_q[1:])
-    cot_full = [plane_gather(late[c]) for c in chunks]
-    all_q, all_out = both_cores(all_q), both_cores(all_out)
-    queries = project_queries(spot, normed_one, all_q, cos_rows, sin_rows)
+    own_gate, own_up = (along(after(near[n].reshape(tall, -1), pair)) for n in range(2))
+    all_out = plane_gather(after(lined_out, all_q[1:], near))
 
     seg_blocks = segments.reshape(seqs, tp_count, span)
     own_seg = lax.dynamic_index_in_dim(seg_blocks, place, 1, keepdims=False)
@@ -982,79 +1124,76 @@
         bias.append(jnp.where(allowed, 0.0, -1e30).astype(f32))
     bias = jnp.concatenate(bias, 1)
     heads_out, lse = attend(spot, queries, pairs, bias, span, kv_group)
-    residual = project_out(spot, heads_out, all_out, tokens, deps=cot_full)
+    all_out = both_cores(all_out, heads_out)
+    residual = project_out(spot, heads_out, all_out, tokens)
 
     norm_two = lax.rsqrt(jnp.mean(residual * residual, -1, keepdims=True) + EPS)
     scaled_two = (residual * norm_two).astype(bf16)
     normed_two = (scaled_two.astype(f32) * gain_two).astype(bf16)
     full_two = []
     for c in chunks:
-        full_two.append(plane_gather(after(normed_two[c], full_two[-1][1:] if full_two else ())))
-    own_gate, own_up = after(own_gate, normed_two), after(own_up, normed_two)
+        full_two.append(plane_gather(after(normed_two[c], full_two[-1][1:]) if full_two else normed_two[c]))
+    cot_full = plane_gather(after(cotangent, full_two[-1][1:]))
+    own_gate, own_up = after(own_gate, full_two[0][1:]), after(own_up, full_two[-1][1:])
     own_in = (own_gate, own_up)
     other_in = (hop(own_gate, 1), hop(own_up, 1))
     own_down = along(after(near[2], residual))
+    tokens_two = sum(full_two, [])
+    gate, up, inner = gate_up(spot, tokens_two, own_in, other_in)
     other_down = hop(own_down, 1)
-    forward = [gate_up(spot, f, own_in, other_in) for f in full_two]
-    inner = [f[2] for f in forward]
-
-    def core_sum(pair):
-        return added(pair[0], hop(pair[1], 1))
 
     def line_sum(a):
         return lax.psum_scatter(a, "tensor", scatter_dimension=0, tiled=False)
 
-    down_parts = row_weight_grad(spot, inner, sum(cot_full, []), tp_count)
-    down_pair = core_sum(down_parts)
-    down_sum = line_sum(down_pair)
-    d_gate, d_up, to_plane = [], [], []
-    for b, (g, f) in enumerate(zip(cot_full, forward)):
-        deps = down_parts if b == 0 else [down_pair, to_plane[-1]]
-        dg, du = inner_grads(spot, g, own_down, other_down, f[0], f[1], deps=deps)
+    down_parts = row_weight_grad(spot, [inner], cot_full, span, tp_count)
+    d_gate, d_up, from_plane, deps = [], [], [], down_parts
+    for n in range(seqs):
+        weights = (own_down, other_down, gate, up, own_in, other_in)
+        dg, du, to_plane = backward_chunk(spot, n, span, cot_full, *weights, deps=deps)
         d_gate.append(dg)
         d_up.append(du)
-        to_plane.append(normed_grads(spot, dg, du, own_in, other_in))
-    grad_normed_two = jnp.concatenate([plane_scatter(p) for p in to_plane], 0)
-    tokens_two = sum(full_two, [])
-    gate_parts = column_weight_grad(spot, tokens_two, d_gate, tp_count, deps=to_plane[-1])
-    gate_pair = core_sum(gate_parts)
-    up_parts = column_weight_grad(spot, tokens_two, d_up, tp_count, deps=gate_parts)
-    up_pair = core_sum(up_parts)
+        deps = to_plane
+        from_plane.append(plane_trade(list(to_plane)))
+    down_pair = core_sum(down_parts, d_gate[0])
+    down_sum = line_sum(down_pair)
+    deps = [down_pair, to_plane, [f[1:] for f in from_plane[:-1]]]
+    gate_parts, up_parts = column_weight_grads(spot, tokens_two, [d_gate, d_up], tp_count, deps=deps)
+    grad_residual, grad_low, gain_two_terms = residual_grads(
+        spot, from_plane, residual, cotangent, gain_two[None], deps=[up_parts[0], down_sum]
+    )
+    gain_two_terms = gain_two_terms[0]
+    gate_parts, up_parts = ((p[0], after(p[1], grad_low)) for p in (gate_parts, up_parts))
+    shares = down(spot, inner, own_down, other_down, seqs, deps=grad_low)
+    gate_pair, up_pair = core_sum(gate_parts, shares[0]), core_sum(up_parts, shares[0])
     gate_sum = line_sum(gate_pair)
-
-    gain_two_terms = jnp.sum(scaled_two.astype(f32) * grad_normed_two, 0)
-    unrounded_two = residual * norm_two
-    grad_residual = cotangent.astype(f32) + norm_backward(
-        grad_normed_two * gain_two, unrounded_two, norm_two
-    )
-
-    grad_low = grad_residual.astype(bf16)
-    grad_heads = unproject_out(spot, grad_low, all_out, deps=up_parts)
+    mixed = plane_trade(list(shares))
+
     out_parts = out_blocks_grad(spot, heads_out, grad_low, tp_count)
-    deps = [out_parts, gate_pair, up_pair, down_sum]
+    grad_heads = unproject_out(spot, grad_low, all_out, deps=[up_parts[0], out_parts])
+    deps = [out_parts, up_pair, gate_pair]
     dq, dkv = unattend(spot, queries, grad_heads, pairs, bias, lse, cos, sin, span, kv_group, deps=deps)
-    dkv = line_sum(after(dkv, gate_sum))
-    grad_out = unfolded(sum_all((out_parts[0], after(out_parts[1], dq)), chip))
-    query_parts = in_blocks_grad(spot, normed_one, dq, None, None, tp_count)
-    grad_query = sum_all(query_parts, chip)
-    to_rows = [down(spot, i, own_down, other_down, deps=query_parts) for i in inner]
-    mixed = (residual + jnp.concatenate([plane_scatter(r) for r in to_rows], 0)).astype(bf16)
-    up_sum = line_sum(after(up_pair, dkv))
-
-    dkv = finish_pairs(spot, dkv, cos_rows, sin_rows, deps=[grad_out, grad_query])
+    gate_here = token(dq, mixed[1:], gate_sum, steps=1)
+    dkv = line_sum(after(dkv, gate_here))
+    up_sum = line_sum(up_pair)
+    out_near = plane_sum(core_sum((out_parts[0], after(out_parts[1], gate_here))), chip)
+    query_parts = in_blocks_grad(spot, normed_one, dq, None, None, tp_count, deps=gate_here)
+    grad_out = unfolded(line_scatter(after(out_near, dkv)))
+    query_near = plane_sum(core_sum(query_parts), chip)
+    grad_query = line_scatter(after(query_near, dkv))
+    mixed = finish_mixed(spot, residual, mixed, deps=query_parts)
+    come = trade(after(jnp.stack([down_sum, gate_sum, up_sum], 1), out_near, query_near), 0, chip)
+    grad_down = jnp.concatenate([jnp.concatenate([c[0, :, :block], c[0, :, block:]], 0) for c in come], 0)
+    grad_gate, grad_up = (jnp.concatenate([c[n] for c in come], 1) for n in (1, 2))
+
+    dkv = finish_pairs(spot, dkv, cos_rows, sin_rows, deps=[out_near, query_near])
     grad_normed_one = unproject_in(spot, dq, dkv, all_q, all_kv)
     gain_one_terms = jnp.sum(scaled_one.astype(f32) * grad_normed_one, 0)
     gain_terms = jnp.stack([gain_one_terms.reshape(8, block), gain_two_terms.reshape(8, block)], 1)
     gain_terms = jnp.pad(gain_terms, ((0, 0), (0, 14), (0, kv_cols - block)))
     kv_parts = in_blocks_grad(spot, normed_one, dq, dkv, gain_terms, tp_count)
-    kv_sum = sum_all(kv_parts, chip)
+    kv_sum = line_scatter(plane_sum(core_sum(kv_parts), chip))
     grad_tokens = grad_residual + norm_backward(grad_normed_one * gain_one, x * norm_one, norm_one)
     grad_tokens = grad_tokens.astype(bf16)
-    sums = jnp.stack([down_sum, gate_sum, up_sum], 1)
-    come = trade(sums, 0, chip)
-    grad_down = jnp.concatenate([jnp.concatenate([c[0, :, :block], c[0, :, block:]], 0) for c in come], 0)
-    grad_gate, grad_up = (jnp.concatenate([c[n] for c in come], 1) for n in (1, 2))
-
     def gain_share(line):
         line = narrow(line, 0)
         share = line.shape[0] // tp_count

time: 1250 us -> 1110 us (0.89)
  waiting for transfers between devices: 595 us -> 491 us
  starting transfers between devices: 117 us -> 71.1 us
  local copies, waits for them, and re-layouts: 53.3 us -> 67.3 us
    reduce_scatter x4, waiting for transfers between devices: 106 us -> 0.01 us  [line_sum(): return lax.psum_scatter(a, 'tensor', scatter_dimension=0, tiled=False)]
    all_gather x4, waiting for transfers between devices: 0.03 us -> 93.7 us  [along(): return lax.all_gather(a, 'tensor', axis=0, tiled=False)]
    ppermute x62 -> x56, waiting for transfers between devices: 399 us -> 308 us  [hop(): return lax.ppermute(a, 'dp', [(i, i ^ bits) for i in range(n)])]
    ppermute x15, starting transfers between devices: 57.2 us -> 23.3 us  [shift(): return lax.ppermute(a, 'tensor', [(i, (i + step) % n) for i in range(n)])]
    ppermute x62 -> x56, starting transfers between devices: 58.5 us -> 46.9 us  [hop(): return lax.ppermute(a, 'dp', [(i, i ^ bits) for i in range(n)])]
    unnamed x200 -> x178, local copies, waits for them, and re-layouts: 28.2 us -> 38.3 us
    pallas_call x20 -> x17, Pallas kernels: 316 us -> 314 us  [grid_call(): return lambda spot, *arrays: run(spot, *deps, *arrays)]
  transfers between devices with their start and end apart: 86 -> 80, of which waited for: 34 -> 35; matrix products, arithmetic and copies ran while one was open for 9% -> 9% of each run, Pallas kernels for 30% -> 31%
where the time goes in v3:
time: 1110 us
  waiting for transfers between devices  491 us (44%)
  Pallas kernels  376 us (34%)
  other arithmetic  84.4 us (8%)
  starting transfers between devices  71.1 us (6%)
  local copies, waits for them, and re-layouts  67.3 us (6%)
  between operations  15.1 us (1%)
    pallas_call x17, Pallas kernels, grid_call(): return lambda spot, *arrays: run(spot, *deps, *arrays)  314 us
    ppermute x56, waiting for transfers between devices, hop(): return lax.ppermute(a, 'dp', [(i, i ^ bits) for i in range(n)])  308 us
    all_gather x4, waiting for transfers between devices, along(): return lax.all_gather(a, 'tensor', axis=0, tiled=False)  93.7 us
    ppermute x15, waiting for transfers between devices, shift(): return lax.ppermute(a, 'tensor', [(i, (i + step) % n) for i in range(n)])  58.6 us
    ppermute x56, starting transfers between devices, hop(): return lax.ppermute(a, 'dp', [(i, i ^ bits) for i in range(n)])  46.9 us
    unnamed x178, local copies, waits for them, and re-layouts  38.3 us
    pallas_call x1, Pallas kernels, unattend(): call(functools.partial(unattend_kernel, count, group, len(deps)), flops=r...  35.1 us
    convert_element_type x6, other arithmetic, added(): return (a.astype(f32) + b.astype(f32)).astype(a.dtype)  31.3 us
  transfers between devices with their start and end apart: 80, of which 35 were waited for; matrix products, arithmetic and copies ran while one was open for 9% of the time, Pallas kernels for 31%

profile of v3, /device:TPU:0, one launch (start us, length us, event | category | flops | bytes accessed | tf_op | source)
XLA Modules:
  0.0 1105.6 jit_solution(11748267220732974279)
XLA Ops:
  35.9 30.0 %all-gather.11.cloned.1.call-done = bf16[32,272,256]{2,1,0:T(8,128)(2,1)} async-done(((bf16[4,272,256]{2,1,0:T(8,128)(2,1)}), bf16[32,272,256]{2,1,0:T(8,128)(2,1)}) %all-gather.11.cloned.1.call-update) | async-done | bytes 4456464 | tf_op jit(solution)/shard_map/all_gather | solution.py:1055
  93.9 22.9 %collective-permute-done.6.refs_2_.refs_1_.refs_3_ = bf16[4,256,512]{2,1,0:T(8,128)(2,1)} collective-permute-done((bf16[4,256,512]{2,1,0:T(8,128)(2,1)}, bf16[4,256,512]{2,1,0:T(8,128)(2,1)}, u32[]{:S(2)}, u32[]{:S(2)}) %collective-permute-start.6) | collective-permute-done | bytes 1048608 | tf_op jit(solution)/shard_map/ppermute | solution.py:888
  116.8 21.2 %collective-permute-done.7.refs_3_.refs_2_.refs_4_ = bf16[4,256,512]{2,1,0:T(8,128)(2,1)} collective-permute-done((bf16[4,256,512]{2,1,0:T(8,128)(2,1)}, bf16[4,256,512]{2,1,0:T(8,128)(2,1)}, u32[]{:S(2)}, u32[]{:S(2)}) %collective-permute-start.7) | collective-permute-done | bytes 1048608 | tf_op jit(solution)/shard_map/ppermute | solution.py:888
  176.2 16.3 %collective-permute-done.14 = bf16[3,256,512]{2,1,0:T(8,128)(2,1)} collective-permute-done((bf16[3,256,512]{2,1,0:T(8,128)(2,1)}, bf16[3,256,512]{2,1,0:T(8,128)(2,1)}, u32[]{:S(2)}, u32[]{:S(2)}) %collective-permute-start.14) | collective-permute-done | bytes 786464 | tf_op jit(solution)/shard_map/ppermute | solution.py:888
  206.3 27.1 %shard_map.207 = (bf16[512,2048]{1,0:T(8,128)(2,1)S(1)}, f32[2,4,8,256]{3,2,1,0:T(8,128)S(1)}) custom-call(s32[3]{0:T(128)S(1)} %pad_add_fusion.spot.place, bf16[512,2048]{1,0:T(8,128)(2,1)} %shard_map.206.refs_0_.refs_1_.refs_4_, bf16[4,2,512,512]{3,2,1,0:T(8,128)(2,1)} %bitcast.229, bf16[4,2,512,512]{3,2,1,0:T(8,128)(2,1)} %bitcast.230, ...), custom_call_target="tpu_custom_call" | custom-call | flops 8589934592 | bytes 4194304 | tf_op jit(solution)/shard_map/pallas_call | solution.py:123
  234.8 14.9 %collective-permute-done.17.refs_0_ = bf16[4,256,512]{2,1,0:T(8,128)(2,1)S(1)} collective-permute-done((bf16[4,256,512]{2,1,0:T(8,128)(2,1)}, bf16[4,256,512]{2,1,0:T(8,128)(2,1)S(1)}, u32[]{:S(2)}, u32[]{:S(2)}) %collective-permute-start.17) | collective-permute-done | bytes 1048608 | tf_op jit(solution)/shard_map/ppermute | solution.py:888
  277.2 22.4 %collective-permute-done.23.refs_1_.refs_9_ = bf16[256,2048]{1,0:T(8,128)(2,1)S(1)} collective-permute-done((bf16[256,2048]{1,0:T(8,128)(2,1)}, bf16[256,2048]{1,0:T(8,128)(2,1)S(1)}, u32[]{:S(2)}, u32[]{:S(2)}) %collective-permute-start.23) | collective-permute-done | bytes 1048608 | tf_op jit(solution)/shard_map/ppermute | solution.py:888
  299.6 22.1 %collective-permute-done.24.refs_2_.refs_10_ = bf16[256,2048]{1,0:T(8,128)(2,1)S(1)} collective-permute-done((bf16[256,2048]{1,0:T(8,128)(2,1)}, bf16[256,2048]{1,0:T(8,128)(2,1)S(1)}, u32[]{:S(2)}, u32[]{:S(2)}) %collective-permute-start.24) | collective-permute-done | bytes 1048608 | tf_op jit(solution)/shard_map/ppermute | solution.py:888
  326.2 31.9 %all-gather.17.cloned.1.call-done = bf16[4096,512]{1,0:T(8,128)(2,1)} async-done(((bf16[1024,512]{1,0:T(8,128)(2,1)}), bf16[4096,512]{1,0:T(8,128)(2,1)}) %all-gather.17.cloned.1.call-update) | async-done | bytes 4194320 | tf_op jit(solution)/shard_map/all_gather | solution.py:1051
  377.1 61.8 %all-gather.19.cloned.1.call-done = bf16[16,256,512]{2,1,0:T(8,128)(2,1)} async-done(((bf16[4,256,512]{2,1,0:T(8,128)(2,1)}), bf16[16,256,512]{2,1,0:T(8,128)(2,1)}) %all-gather.19.cloned.1.call-update) | async-done | bytes 4194320 | tf_op jit(solution)/shard_map/all_gather | solution.py:1051
  441.5 43.1 %shard_map.221 = (bf16[2048,2048]{1,0:T(8,128)(2,1)}, bf16[2048,2048]{1,0:T(8,128)(2,1)}, bf16[2048,2048]{1,0:T(8,128)(2,1)}) custom-call(s32[3]{0:T(128)S(1)} %pad_add_fusion.spot.place, bf16[256,2048]{1,0:T(8,128)(2,1)} %get-tuple-element.119.refs_0_.refs_8_, bf16[256,2048]{1,0:T(8,128)(2,1)S(1)} %copy-done.19, bf16[256,2048]{1,0:T(8,128)(2,1)S(1)} %copy-done.21, ...), custom_call_target="tpu_custom_call" | custom-call | flops 34359738368 | bytes 58720256 | tf_op jit(solution)/shard_map/pallas_call | solution.py:295
  484.6 26.4 %shard_map.223 = (bf16[4,4,256,512]{3,2,1,0:T(8,128)(2,1)}, bf16[4,4,256,512]{3,2,1,0:T(8,128)(2,1)}) custom-call(s32[3]{0:T(128)S(1)} %pad_add_fusion.spot.place, bf16[2048,2048]{1,0:T(8,128)(2,1)} %get-tuple-element.50.refs_0_.refs_1_, bf16[512,2048]{1,0:T(8,128)(2,1)S(1)} %copy-done.13, ...), custom_call_target="tpu_custom_call" | custom-call | flops 17179869184 | bytes 33554432 | tf_op jit(solution)/shard_map/pallas_call | solution.py:295
  513.3 38.9 %shard_map.225 = (bf16[1024,2048]{1,0:T(8,128)(2,1)}, bf16[1024,2048]{1,0:T(8,128)(2,1)}, bf16[256,2048]{1,0:T(8,128)(2,1)S(1)}, bf16[256,2048]{1,0:T(8,128)(2,1...) custom-call(s32[3]{0:T(128)S(1)} %pad_add_fusion.spot.place, ...), custom_call_target="tpu_custom_call" | custom-call | flops 25769803776 | bytes 58720256 | tf_op jit(solution)/shard_map/pallas_call | solution.py:295
  564.6 39.1 %shard_map.227 = (bf16[1024,2048]{1,0:T(8,128)(2,1)}, bf16[1024,2048]{1,0:T(8,128)(2,1)}, bf16[256,2048]{1,0:T(8,128)(2,1)S(1)}, bf16[256,2048]{1,0:T(8,128)(2,1...) custom-call(s32[3]{0:T(128)S(1)} %pad_add_fusion.spot.place, bf16[256,2048]{1,0:T(8,128)(2,1)} %copy-done.29, ...), custom_call_target="tpu_custom_call" | custom-call | flops 25769803776 | bytes 58720256 | tf_op jit(solution)/shard_map/pallas_call | solution.py:295
  611.8 49.2 %shard_map.228 = (bf16[4,4,256,512]{3,2,1,0:T(8,128)(2,1)}, bf16[4,4,256,512]{3,2,1,0:T(8,128)(2,1)}, bf16[4,4,256,512]{3,2,1,0:T(8,128)(2,1)}, bf16[4,4,256,512]{3,2,1,0:T(8,128)(2,1)}) custom-call(s32[3]{0:T(128)S(1)} %pad_add_fusion.spot.place, bf16[4,4,256,512]{3,2,1,0:T(8,128)(2,1)} %add_convert_fusion.4.refs_0_, ...), custom_call_target="tpu_custom_call" | custom-call | flops 34359738368 | bytes 67108864 | tf_op jit(solution)/shard_map/pallas_call | solution.py:295
  676.8 24.2 %shard_map.231 = (bf16[512,2048]{1,0:T(8,128)(2,1)S(1)}, bf16[512,2048]{1,0:T(8,128)(2,1)}, bf16[512,2048]{1,0:T(8,128)(2,1)}, bf16[512,2048]{1,0:T(8,128)(2,1)}) custom-call(s32[3]{0:T(128)S(1)} %pad_add_fusion.spot.place, bf16[512,2048]{1,0:T(8,128)(2,1)} %get-tuple-element.68.refs_1_.refs_0_.refs_3_, ...), custom_call_target="tpu_custom_call" | custom-call | flops 17179869184 | bytes 25165824 | tf_op jit(solution)/shard_map/pallas_call | solution.py:295
  739.0 35.1 %shard_map.237 = (bf16[512,2048]{1,0:T(8,128)(2,1)S(1)}, bf16[4,2,512,512]{3,2,1,0:T(8,128)(2,1)}) custom-call(s32[3]{0:T(128)S(1)} %pad_add_fusion.spot.place, bf16[4,4,256,512]{3,2,1,0:T(8,128)(2,1)} %get-tuple-element.69.refs_1_.refs_0_, bf16[4,4,256,512]{3,2,1,0:T(8,128)(2,1)} %get-tuple-element.70.refs_2_.refs_1_.refs_0_, ...), custom_call_target="tpu_custom_call" | custom-call | flops 21474836480 | bytes 8388608 | tf_op jit(solution)/shard_map/pallas_call | solution.py:235
  784.1 44.3 %collective-permute-done.45.refs_2_.refs_5_ = bf16[512,2048]{1,0:T(8,128)(2,1)} collective-permute-done((bf16[512,2048]{1,0:T(8,128)(2,1)}, bf16[512,2048]{1,0:T(8,128)(2,1)}, u32[]{:S(2)}, u32[]{:S(2)}) %collective-permute-start.45) | collective-permute-done | bytes 2097184 | tf_op jit(solution)/shard_map/ppermute | solution.py:888
  859.5 14.7 %collective-permute-done.50 = bf16[4,256,512]{2,1,0:T(8,128)(2,1)S(1)} collective-permute-done((bf16[4,256,512]{2,1,0:T(8,128)(2,1)S(1)}, bf16[4,256,512]{2,1,0:T(8,128)(2,1)S(1)}, u32[]{:S(2)}, u32[]{:S(2)}) %collective-permute-start.50) | collective-permute-done | bytes 1048608 | tf_op jit(solution)/shard_map/ppermute | solution.py:888
  878.0 18.8 %collective-permute-done.49 = bf16[4,256,512]{2,1,0:T(8,128)(2,1)} collective-permute-done((bf16[4,256,512]{2,1,0:T(8,128)(2,1)}, bf16[4,256,512]{2,1,0:T(8,128)(2,1)}, u32[]{:S(2)}, u32[]{:S(2)}) %collective-permute-start.49) | collective-permute-done | bytes 1048608 | tf_op jit(solution)/shard_map/ppermute | solution.py:888
  900.2 19.1 %collective-permute-done.54 = bf16[4,256,512]{2,1,0:T(8,128)(2,1)} collective-permute-done((bf16[4,256,512]{2,1,0:T(8,128)(2,1)}, bf16[4,256,512]{2,1,0:T(8,128)(2,1)}, u32[]{:S(2)}, u32[]{:S(2)}) %collective-permute-start.54) | collective-permute-done | bytes 1048608 | tf_op jit(solution)/shard_map/ppermute | solution.py:888
  919.3 22.0 %collective-permute-done.53 = bf16[4,256,512]{2,1,0:T(8,128)(2,1)} collective-permute-done((bf16[4,256,512]{2,1,0:T(8,128)(2,1)}, bf16[4,256,512]{2,1,0:T(8,128)(2,1)}, u32[]{:S(2)}, u32[]{:S(2)}) %collective-permute-start.53) | collective-permute-done | bytes 1048608 | tf_op jit(solution)/shard_map/ppermute | solution.py:888
  969.9 16.0 %collective-permute-done.69 = bf16[3,256,512]{2,1,0:T(8,128)(2,1)} collective-permute-done((bf16[3,256,512]{2,1,0:T(8,128)(2,1)}, bf16[3,256,512]{2,1,0:T(8,128)(2,1)}, u32[]{:S(2)}, u32[]{:S(2)}) %collective-permute-start.69) | collective-permute-done | bytes 786464 | tf_op jit(solution)/shard_map/ppermute | solution.py:888
  1059.9 14.4 %collective-permute-done.66 = bf16[256,512]{1,0:T(8,128)(2,1)S(1)} collective-permute-done((bf16[256,512]{1,0:T(8,128)(2,1)S(1)}, bf16[256,512]{1,0:T(8,128)(2,1)S(1)}, u32[]{:S(2)}, u32[]{:S(2)}) %collective-permute-start.66) | collective-permute-done | bytes 262176 | tf_op jit(solution)/shard_map/ppermute | solution.py:916
  (454 shorter events, 414.6 us)
Async XLA Ops:
  7.2 58.6 %all-gather.11.cloned.1.call-start = ((), (), s32[]{:S(2)}) async-start(), calls=%async_computation.8 | async-start | bytes 5013504 | tf_op jit(solution)/shard_map/all_gather | solution.py:1055
  27.5 178.9 %all-gather.13.cloned.1.call-start = ((), (), s32[]{:S(2)}) async-start(), calls=%async_computation.9 | async-start | bytes 5242880 | tf_op jit(solution)/shard_map/all_gather | solution.py:1051
  86.3 239.9 %all-gather.15.cloned.1.call-start = ((), (), s32[]{:S(2)}) async-start(), calls=%async_computation.10 | async-start | bytes 5242880 | tf_op jit(solution)/shard_map/all_gather | solution.py:1051
  93.9 62.2 %collective-permute-start.9 = (bf16[4,256,512]{2,1,0:T(8,128)(2,1)}, bf16[4,256,512]{2,1,0:T(8,128)(2,1)}, u32[]{:S(2)}, u32[]{:S(2)}) collective-permute-start(bf16[4,256,512]{2,1,0:T(8,128)(2,1)} %shard_map.205.refs_1_.refs_2_), channel_id=1, source_target_pairs={{0,4},{4,0},{8,12},{12,8},{16,20},{20,16},{24,28},{28,24},{1,5},{5... | collective-permute-start | bytes 3145736 | tf_op jit(solution)/shard_map/ppermute | solution.py:888
  197.8 160.3 %all-gather.17.cloned.1.call-start = ((), (), s32[]{:S(2)}) async-start(), calls=%async_computation.11 | async-start | bytes 5242880 | tf_op jit(solution)/shard_map/all_gather | solution.py:1051
  198.4 240.5 %all-gather.19.cloned.1.call-start = ((), (), s32[]{:S(2)}) async-start(), calls=%async_computation.12 | async-start | bytes 5242880 | tf_op jit(solution)/shard_map/all_gather | solution.py:1051
  276.9 387.1 %reduce-scatter.5.cloned.1.call-start = ((), (), s32[]{:S(2)}) async-start(), calls=%async_computation.4 | async-start | bytes 5242880 | tf_op jit(solution)/shard_map/reduce_scatter | solution.py:1146
  326.2 50.9 %collective-permute-start.29 = (bf16[4,1024,512]{2,1,0:T(8,128)(2,1)}, bf16[4,1024,512]{2,1,0:T(8,128)(2,1)}, u32[]{:S(2)}, u32[]{:S(2)}) collective-permute-start(bf16[4,1024,512]{2,1,0:T(8,128)(2,1)} %shard_map.218.refs_8_.refs_10_.refs_12_), channel_id=1, source_target_pairs={{0,4},{4,0},{8,12},{12,8},{16,20},{20,16},{24,28},{28,24},{1,5},{5... | collective-permute-start | bytes 12582920 | tf_op jit(solution)/shard_map/ppermute | solution.py:888
  370.7 68.2 %collective-permute-start.30 = (bf16[4,1024,512]{2,1,0:T(8,128)(2,1)}, bf16[4,1024,512]{2,1,0:T(8,128)(2,1)}, u32[]{:S(2)}, u32[]{:S(2)}) collective-permute-start(bf16[4,1024,512]{2,1,0:T(8,128)(2,1)} %shard_map.220.refs_9_.refs_11_.refs_13_), channel_id=1, source_target_pairs={{0,4},{4,0},{8,12},{12,8},{16,20},{20,16},{24,28},{28,24},{1,5},{5... | collective-permute-start | bytes 12582920 | tf_op jit(solution)/shard_map/ppermute | solution.py:888
  373.6 111.0 %collective-permute-start.31 = (bf16[512,2048]{1,0:T(8,128)(2,1)}, bf16[512,2048]{1,0:T(8,128)(2,1)}, u32[]{:S(2)}, u32[]{:S(2)}) collective-permute-start(bf16[512,2048]{1,0:T(8,128)(2,1)} %shard_map.222.refs_1_.refs_5_.refs_2_.refs_4_), channel_id=1, source_target_pairs={{0,8},{4,12},{8,0},{12,4},{16,24},{20,28},{24,16},{28,20},{1,9},{5... | collective-permute-start | bytes 6291464 | tf_op jit(solution)/shard_map/ppermute | solution.py:888
  373.6 111.0 %collective-permute-start.32 = (bf16[512,2048]{1,0:T(8,128)(2,1)}, bf16[512,2048]{1,0:T(8,128)(2,1)}, u32[]{:S(2)}, u32[]{:S(2)}) collective-permute-start(bf16[512,2048]{1,0:T(8,128)(2,1)} %shard_map.222.refs_1_.refs_5_.refs_2_.refs_4_), channel_id=1, source_target_pairs={{0,16},{4,20},{8,24},{12,28},{16,0},{20,4},{24,8},{28,12},{1,17},{... | collective-permute-start | bytes 6291464 | tf_op jit(solution)/shard_map/ppermute | solution.py:888
  375.6 109.0 %collective-permute-start.33 = (bf16[512,2048]{1,0:T(8,128)(2,1)}, bf16[512,2048]{1,0:T(8,128)(2,1)}, u32[]{:S(2)}, u32[]{:S(2)}) collective-permute-start(bf16[512,2048]{1,0:T(8,128)(2,1)} %shard_map.222.refs_1_.refs_5_.refs_2_.refs_4_), channel_id=1, source_target_pairs={{0,24},{4,28},{8,16},{12,20},{16,8},{20,12},{24,0},{28,4},{1,25},{... | collective-permute-start | bytes 6291464 | tf_op jit(solution)/shard_map/ppermute | solution.py:888
  438.9 72.5 %collective-permute-start.34 = (bf16[4,4,256,512]{3,2,1,0:T(8,128)(2,1)}, bf16[4,4,256,512]{3,2,1,0:T(8,128)(2,1)S(1)}, u32[]{:S(2)}, u32[]{:S(2)}) collective-permute-start(bf16[4,4,256,512]{3,2,1,0:T(8,128)(2,1)} %bitcast.281), channel_id=1, source_target_pairs={{0,4},{4,0},{8,12},{12,8},{16,20},{20,16},{24,28},{28,24},{1,5},{5... | collective-permute-start | bytes 12582920 | tf_op jit(solution)/shard_map/ppermute | solution.py:888
  561.0 269.2 %reduce-scatter.7.cloned.1.call-start = ((), (), s32[]{:S(2)}) async-start(), calls=%async_computation.5 | async-start | bytes 5242880 | tf_op jit(solution)/shard_map/reduce_scatter | solution.py:1146
  603.7 58.3 %collective-permute-start.39 = (bf16[256,2048]{1,0:T(8,128)(2,1)S(1)}, bf16[256,2048]{1,0:T(8,128)(2,1)S(1)}, u32[]{:S(2)}, u32[]{:S(2)}) collective-permute-start(bf16[256,2048]{1,0:T(8,128)(2,1)S(1)} %get-tuple-element.61.refs_2_), channel_id=1, source_target_pairs={{0,8},{4,12},{8,0},{12,4},{16,24},{20,28},{24,16},{28,20},{1,9},{5... | collective-permute-start | bytes 3145736 | tf_op jit(solution)/shard_map/ppermute | solution.py:888
  605.4 56.6 %collective-permute-start.40 = (bf16[256,2048]{1,0:T(8,128)(2,1)S(1)}, bf16[256,2048]{1,0:T(8,128)(2,1)S(1)}, u32[]{:S(2)}, u32[]{:S(2)}) collective-permute-start(bf16[256,2048]{1,0:T(8,128)(2,1)S(1)} %get-tuple-element.62.refs_3_), channel_id=1, source_target_pairs={{0,16},{4,20},{8,24},{12,28},{16,0},{20,4},{24,8},{28,12},{1,17},{... | collective-permute-start | bytes 3145736 | tf_op jit(solution)/shard_map/ppermute | solution.py:888
  606.9 57.1 %collective-permute-start.41 = (bf16[256,2048]{1,0:T(8,128)(2,1)}, bf16[256,2048]{1,0:T(8,128)(2,1)}, u32[]{:S(2)}, u32[]{:S(2)}) collective-permute-start(bf16[256,2048]{1,0:T(8,128)(2,1)} %get-tuple-element.63.refs_4_), channel_id=1, source_target_pairs={{0,24},{4,28},{8,16},{12,20},{16,8},{20,12},{24,0},{28,4},{1,25},{... | collective-permute-start | bytes 3145736 | tf_op jit(solution)/shard_map/ppermute | solution.py:888
  709.1 165.6 %reduce-scatter.11.cloned.1.call-start = ((), (), s32[]{:S(2)}) async-start(), calls=%async_computation.7 | async-start | bytes 5242880 | tf_op jit(solution)/shard_map/reduce_scatter | solution.py:1146
  735.4 257.3 %reduce-scatter.9.cloned.1.call-start = ((), (), s32[]{:S(2)}) async-start(), calls=%async_computation.6 | async-start | bytes 5242880 | tf_op jit(solution)/shard_map/reduce_scatter | solution.py:1146
  737.0 91.5 %collective-permute-start.45 = (bf16[512,2048]{1,0:T(8,128)(2,1)}, bf16[512,2048]{1,0:T(8,128)(2,1)}, u32[]{:S(2)}, u32[]{:S(2)}) collective-permute-start(bf16[512,2048]{1,0:T(8,128)(2,1)} %get-tuple-element.78), channel_id=1, source_target_pairs={{0,16},{4,20},{8,24},{12,28},{16,0},{20,4},{24,8},{28,12},{1,17},{... | collective-permute-start | bytes 6291464 | tf_op jit(solution)/shard_map/ppermute | solution.py:888
  737.6 92.6 %collective-permute-start.46 = (bf16[512,2048]{1,0:T(8,128)(2,1)}, bf16[512,2048]{1,0:T(8,128)(2,1)}, u32[]{:S(2)}, u32[]{:S(2)}) collective-permute-start(bf16[512,2048]{1,0:T(8,128)(2,1)} %get-tuple-element.79), channel_id=1, source_target_pairs={{0,24},{4,28},{8,16},{12,20},{16,8},{20,12},{24,0},{28,4},{1,25},{... | collective-permute-start | bytes 6291464 | tf_op jit(solution)/shard_map/ppermute | solution.py:888
  857.5 61.8 %collective-permute-start.54 = (bf16[4,256,512]{2,1,0:T(8,128)(2,1)}, bf16[4,256,512]{2,1,0:T(8,128)(2,1)}, u32[]{:S(2)}, u32[]{:S(2)}) collective-permute-start(bf16[4,256,512]{2,1,0:T(8,128)(2,1)} %get-tuple-element.96), channel_id=1, source_target_pairs={{0,24},{4,28},{8,16},{12,20},{16,8},{20,12},{24,0},{28,4},{1,25},{... | collective-permute-start | bytes 3145736 | tf_op jit(solution)/shard_map/ppermute | solution.py:888
  859.2 82.1 %collective-permute-start.53 = (bf16[4,256,512]{2,1,0:T(8,128)(2,1)}, bf16[4,256,512]{2,1,0:T(8,128)(2,1)}, u32[]{:S(2)}, u32[]{:S(2)}) collective-permute-start(bf16[4,256,512]{2,1,0:T(8,128)(2,1)} %get-tuple-element.97), channel_id=1, source_target_pairs={{0,16},{4,20},{8,24},{12,28},{16,0},{20,4},{24,8},{28,12},{1,17},{... | collective-permute-start | bytes 3145736 | tf_op jit(solution)/shard_map/ppermute | solution.py:888
  874.2 67.1 %collective-permute-start.52 = (bf16[4,256,512]{2,1,0:T(8,128)(2,1)}, bf16[4,256,512]{2,1,0:T(8,128)(2,1)}, u32[]{:S(2)}, u32[]{:S(2)}) collective-permute-start(bf16[4,256,512]{2,1,0:T(8,128)(2,1)} %get-tuple-element.95), channel_id=1, source_target_pairs={{0,8},{4,12},{8,0},{12,4},{16,24},{20,28},{24,16},{28,20},{1,9},{5... | collective-permute-start | bytes 3145736 | tf_op jit(solution)/shard_map/ppermute | solution.py:888
  (138 other events, 2620.8 us)
Sparse Core Ops, SparseCore 0:
  27.6 38.1 all-gather.10
  86.4 79.0 all-gather.12
  197.9 79.4 all-gather.14
  278.8 79.2 all-gather.16
  359.5 79.2 all-gather.18
  561.1 75.3 reduce-scatter.4
  709.3 75.0 reduce-scatter.6
  786.6 77.2 reduce-scatter.10
  866.3 77.2 reduce-scatter.8

commit v4 on v3

--- a/solution.py
+++ b/solution.py
@@ -423,17 +423,48 @@
     )(spot, grads, *weights)
 
 
-def unproject_in(spot, dq, dkv, w_q, w_kv):
+def still(shape, index):
+    return pl.BlockSpec(shape, index, pipeline_mode=pl.Buffered(1))
+
+
+def unproject_queries(spot, dq, w_q, deps=()):
     rows, width = dq.shape
     shards, depth, cols = w_q[0].shape
-    thin = w_kv.shape[3] // 2
     count = len(w_q)
     tall = min(256, rows)
 
-    def body(spot, *refs):
-        q_ref, kv_ref, wq_refs, wkv_ref, o_ref = *refs[:2], refs[2 : 2 + count], *refs[2 + count :]
+    def body(spot, q_ref, *refs):
         left = by_slot(q_ref, spot, shards, cols)
-        thin_left = jnp.concatenate(
+        for n, w_ref in enumerate(refs[:-1]):
+            at = block_home(spot, n // PLANE, n % PLANE)
+            y = nt(left, jnp.concatenate([w_ref[s] for s in range(shards)], 1))
+            refs[-1][:, pl.ds(pl.multiple_of(at * depth, depth), depth)] = y
+
+    tile = pl.BlockSpec((tall, width), lambda m, _: (m, 0))
+    return grid_call(
+        body,
+        (rows // tall,),
+        [tile] + [still(w.shape, lambda m, _: (0, 0, 0)) for w in w_q],
+        pl.BlockSpec((tall, count * depth), lambda m, _: (m, 0)),
+        jax.ShapeDtypeStruct((rows, count * depth), f32),
+        2 * rows * count * depth * shards * cols,
+        count * depth * shards * cols * 2 + rows * width * 6,
+        deps=deps,
+    )(spot, dq, *w_q)
+
+
+def unproject_pairs(spot, partial, dkv, w_kv, scaled, deps=()):
+    rows, width = partial.shape
+    parts, shards, _, cols = w_kv.shape
+    depth, thin = width // parts, cols // 2
+    tall = min(256, rows)
+
+    def body(spot, p_ref, kv_ref, w_ref, s_ref, o_ref, sum_ref):
+        @pl.when(pl.program_id(0) == 0)
+        def _():
+            sum_ref[...] = jnp.zeros_like(sum_ref)
+
+        left = jnp.concatenate(
             [
                 kv_ref[n, :, pl.ds(pl.multiple_of(slot_home(spot, s, shards) * thin, thin), thin)]
                 for s in range(shards)
@@ -441,24 +472,29 @@
             ],
             1,
         )
-        for n, w_ref in enumerate(wq_refs):
-            at = block_home(spot, n // PLANE, n % PLANE)
-            y = nt(left, jnp.concatenate([w_ref[s] for s in range(shards)], 1))
-            y += nt(thin_left, jnp.concatenate([wkv_ref[at, s, :depth, :] for s in range(shards)], 1))
-            o_ref[:, pl.ds(pl.multiple_of(at * depth, depth), depth)] = y
+        for i in range(parts):
+            here = slice(i * depth, (i + 1) * depth)
+            total = nt(left, jnp.concatenate([w_ref[i, s, :depth, :] for s in range(shards)], 1))
+            total += p_ref[:, here]
+            o_ref[:, here] = total
+            sum_ref[0:1, here] += jnp.sum(s_ref[:, here].astype(f32) * total, 0, keepdims=True)
 
     tile = pl.BlockSpec((tall, width), lambda m, _: (m, 0))
     return grid_call(
         body,
         (rows // tall,),
-        [tile, pl.BlockSpec((2, tall, dkv.shape[2]), lambda m, _: (0, m, 0))]
-        + [pl.BlockSpec(w.shape, lambda m, _: (0, 0, 0)) for w in w_q]
-        + [pl.BlockSpec(w_kv.shape, lambda m, _: (0, 0, 0, 0))],
-        pl.BlockSpec((tall, count * depth), lambda m, _: (m, 0)),
-        jax.ShapeDtypeStruct((rows, count * depth), f32),
-        2 * rows * count * depth * shards * (cols + 2 * thin),
-        count * depth * shards * cols * 2 + w_kv.size * 2 + rows * width * 6,
-    )(spot, dq, dkv, *w_q, w_kv)
+        [
+            tile,
+            pl.BlockSpec((2, tall, dkv.shape[2]), lambda m, _: (0, m, 0)),
+            still(w_kv.shape, lambda m, _: (0, 0, 0, 0)),
+            tile,
+        ],
+        [tile, pl.BlockSpec((8, width), lambda m, _: (0, 0))],
+        [jax.ShapeDtypeStruct((rows, width), f32), jax.ShapeDtypeStruct((8, width), f32)],
+        2 * rows * width * shards * cols,
+        w_kv.size * 2 + rows * width * 12,
+        deps=deps,
+    )(spot, partial, dkv, w_kv, scaled)
 
 
 def of_core(ref, core, depth):
@@ -553,10 +589,6 @@
         ],
         0,
     )
-
-
-def still(shape, index):
-    return pl.BlockSpec(shape, index, pipeline_mode=pl.Buffered(1))
 
 
 def gate_up(spot, xs, own, other, deps=()):
@@ -1175,19 +1207,20 @@
     gate_here = token(dq, mixed[1:], gate_sum, steps=1)
     dkv = line_sum(after(dkv, gate_here))
     up_sum = line_sum(up_pair)
+    partial = unproject_queries(spot, dq, all_q, deps=gate_here)
     out_near = plane_sum(core_sum((out_parts[0], after(out_parts[1], gate_here))), chip)
-    query_parts = in_blocks_grad(spot, normed_one, dq, None, None, tp_count, deps=gate_here)
-    grad_out = unfolded(line_scatter(after(out_near, dkv)))
+    query_parts = in_blocks_grad(spot, normed_one, dq, None, None, tp_count, deps=partial)
+    grad_out = unfolded(line_scatter(out_near))
     query_near = plane_sum(core_sum(query_parts), chip)
-    grad_query = line_scatter(after(query_near, dkv))
+    grad_query = line_scatter(query_near)
     mixed = finish_mixed(spot, residual, mixed, deps=query_parts)
     come = trade(after(jnp.stack([down_sum, gate_sum, up_sum], 1), out_near, query_near), 0, chip)
     grad_down = jnp.concatenate([jnp.concatenate([c[0, :, :block], c[0, :, block:]], 0) for c in come], 0)
     grad_gate, grad_up = (jnp.concatenate([c[n] for c in come], 1) for n in (1, 2))
 
     dkv = finish_pairs(spot, dkv, cos_rows, sin_rows, deps=[out_near, query_near])
-    grad_normed_one = unproject_in(spot, dq, dkv, all_q, all_kv)
-    gain_one_terms = jnp.sum(scaled_one.astype(f32) * grad_normed_one, 0)
+    grad_normed_one, gain_one_terms = unproject_pairs(spot, partial, dkv, all_kv, scaled_one)
+    gain_one_terms = gain_one_terms[0]
     gain_terms = jnp.stack([gain_one_terms.reshape(8, block), gain_two_terms.reshape(8, block)], 1)
     gain_terms = jnp.pad(gain_terms, ((0, 0), (0, 14), (0, kv_cols - block)))
     kv_parts = in_blocks_grad(spot, normed_one, dq, dkv, gain_terms, tp_count)

time: 1110 us -> 1090 us (0.982)
  waiting for transfers between devices: 491 us -> 455 us
  starting transfers between devices: 71.1 us -> 84 us
    ppermute x15, waiting for transfers between devices: 58.6 us -> 33.2 us  [shift(): return lax.ppermute(a, 'tensor', [(i, (i + step) % n) for i in range(n)])]
    ppermute x56, waiting for transfers between devices: 308 us -> 295 us  [hop(): return lax.ppermute(a, 'dp', [(i, i ^ bits) for i in range(n)])]
    ppermute x15, starting transfers between devices: 23.3 us -> 34.8 us  [shift(): return lax.ppermute(a, 'tensor', [(i, (i + step) % n) for i in range(n)])]
    pallas_call x17 -> x18, Pallas kernels: 314 us -> 318 us  [grid_call(): return lambda spot, *arrays: run(spot, *deps, *arrays)]
    unnamed x178 -> x188, local copies, waits for them, and re-layouts: 38.3 us -> 38.1 us
  transfers between devices with their start and end apart: 80 -> 80, of which waited for: 35 -> 36; matrix products, arithmetic and copies ran while one was open for 9% -> 9% of each run, Pallas kernels for 31% -> 32%
where the time goes in v4:
time: 1090 us; the launch traced here: 1080 us
  waiting for transfers between devices  455 us (42%)
  Pallas kernels  381 us (35%)
  starting transfers between devices  84 us (8%)
  other arithmetic  78.9 us (7%)
  local copies, waits for them, and re-layouts  63.9 us (6%)
  between operations  15.1 us (1%)
    pallas_call x18, Pallas kernels, grid_call(): return lambda spot, *arrays: run(spot, *deps, *arrays)  318 us
    ppermute x56, waiting for transfers between devices, hop(): return lax.ppermute(a, 'dp', [(i, i ^ bits) for i in range(n)])  295 us
    all_gather x4, waiting for transfers between devices, along(): return lax.all_gather(a, 'tensor', axis=0, tiled=False)  95.9 us
    ppermute x56, starting transfers between devices, hop(): return lax.ppermute(a, 'dp', [(i, i ^ bits) for i in range(n)])  48.4 us
    unnamed x188, local copies, waits for them, and re-layouts  38.1 us
    pallas_call x1, Pallas kernels, unattend(): call(functools.partial(unattend_kernel, count, group, len(deps)), flops=r...  35.1 us
    ppermute x15, starting transfers between devices, shift(): return lax.ppermute(a, 'tensor', [(i, (i + step) % n) for i in range(n)])  34.8 us
    ppermute x15, waiting for transfers between devices, shift(): return lax.ppermute(a, 'tensor', [(i, (i + step) % n) for i in range(n)])  33.2 us
  transfers between devices with their start and end apart: 80, of which 36 were waited for; matrix products, arithmetic and copies ran while one was open for 9% of the time, Pallas kernels for 32%

profile of v4, /device:TPU:0, one launch (start us, length us, event | category | flops | bytes accessed | tf_op | source)
XLA Modules:
  0.0 1077.4 jit_solution(10163847672256786682)
XLA Ops:
  35.9 30.0 %all-gather.11.cloned.1.call-done = bf16[32,272,256]{2,1,0:T(8,128)(2,1)} async-done(((bf16[4,272,256]{2,1,0:T(8,128)(2,1)}), bf16[32,272,256]{2,1,0:T(8,128)(2,1)}) %all-gather.11.cloned.1.call-update) | async-done | bytes 4456464 | tf_op jit(solution)/shard_map/all_gather | solution.py:1087
  93.2 22.9 %collective-permute-done.6.refs_2_.refs_1_.refs_3_ = bf16[4,256,512]{2,1,0:T(8,128)(2,1)} collective-permute-done((bf16[4,256,512]{2,1,0:T(8,128)(2,1)}, bf16[4,256,512]{2,1,0:T(8,128)(2,1)}, u32[]{:S(2)}, u32[]{:S(2)}) %collective-permute-start.6) | collective-permute-done | bytes 1048608 | tf_op jit(solution)/shard_map/ppermute | solution.py:920
  116.1 21.2 %collective-permute-done.7.refs_3_.refs_2_.refs_4_ = bf16[4,256,512]{2,1,0:T(8,128)(2,1)} collective-permute-done((bf16[4,256,512]{2,1,0:T(8,128)(2,1)}, bf16[4,256,512]{2,1,0:T(8,128)(2,1)}, u32[]{:S(2)}, u32[]{:S(2)}) %collective-permute-start.7) | collective-permute-done | bytes 1048608 | tf_op jit(solution)/shard_map/ppermute | solution.py:920
  175.7 16.3 %collective-permute-done.14 = bf16[3,256,512]{2,1,0:T(8,128)(2,1)} collective-permute-done((bf16[3,256,512]{2,1,0:T(8,128)(2,1)}, bf16[3,256,512]{2,1,0:T(8,128)(2,1)}, u32[]{:S(2)}, u32[]{:S(2)}) %collective-permute-start.14) | collective-permute-done | bytes 786464 | tf_op jit(solution)/shard_map/ppermute | solution.py:920
  204.7 27.2 %shard_map.207 = (bf16[512,2048]{1,0:T(8,128)(2,1)S(1)}, f32[2,4,8,256]{3,2,1,0:T(8,128)S(1)}) custom-call(s32[3]{0:T(128)S(1)} %pad_add_fusion.spot.place, bf16[512,2048]{1,0:T(8,128)(2,1)} %shard_map.206.refs_0_.refs_1_.refs_4_, bf16[4,2,512,512]{3,2,1,0:T(8,128)(2,1)} %bitcast.229, bf16[4,2,512,512]{3,2,1,0:T(8,128)(2,1)} %bitcast.230, ...), custom_call_target="tpu_custom_call" | custom-call | flops 8589934592 | bytes 4194304 | tf_op jit(solution)/shard_map/pallas_call | solution.py:123
  233.2 14.7 %collective-permute-done.17.refs_0_ = bf16[4,256,512]{2,1,0:T(8,128)(2,1)S(1)} collective-permute-done((bf16[4,256,512]{2,1,0:T(8,128)(2,1)}, bf16[4,256,512]{2,1,0:T(8,128)(2,1)S(1)}, u32[]{:S(2)}, u32[]{:S(2)}) %collective-permute-start.17) | collective-permute-done | bytes 1048608 | tf_op jit(solution)/shard_map/ppermute | solution.py:920
  275.5 22.4 %collective-permute-done.23.refs_1_.refs_9_ = bf16[256,2048]{1,0:T(8,128)(2,1)S(1)} collective-permute-done((bf16[256,2048]{1,0:T(8,128)(2,1)}, bf16[256,2048]{1,0:T(8,128)(2,1)S(1)}, u32[]{:S(2)}, u32[]{:S(2)}) %collective-permute-start.23) | collective-permute-done | bytes 1048608 | tf_op jit(solution)/shard_map/ppermute | solution.py:920
  297.9 22.1 %collective-permute-done.24.refs_2_.refs_10_ = bf16[256,2048]{1,0:T(8,128)(2,1)S(1)} collective-permute-done((bf16[256,2048]{1,0:T(8,128)(2,1)}, bf16[256,2048]{1,0:T(8,128)(2,1)S(1)}, u32[]{:S(2)}, u32[]{:S(2)}) %collective-permute-start.24) | collective-permute-done | bytes 1048608 | tf_op jit(solution)/shard_map/ppermute | solution.py:920
  324.5 33.0 %all-gather.17.cloned.1.call-done = bf16[4096,512]{1,0:T(8,128)(2,1)} async-done(((bf16[1024,512]{1,0:T(8,128)(2,1)}), bf16[4096,512]{1,0:T(8,128)(2,1)}) %all-gather.17.cloned.1.call-update) | async-done | bytes 4194320 | tf_op jit(solution)/shard_map/all_gather | solution.py:1083
  375.4 62.9 %all-gather.19.cloned.1.call-done = bf16[16,256,512]{2,1,0:T(8,128)(2,1)} async-done(((bf16[4,256,512]{2,1,0:T(8,128)(2,1)}), bf16[16,256,512]{2,1,0:T(8,128)(2,1)}) %all-gather.19.cloned.1.call-update) | async-done | bytes 4194320 | tf_op jit(solution)/shard_map/all_gather | solution.py:1083
  440.9 43.1 %shard_map.221 = (bf16[2048,2048]{1,0:T(8,128)(2,1)}, bf16[2048,2048]{1,0:T(8,128)(2,1)}, bf16[2048,2048]{1,0:T(8,128)(2,1)}) custom-call(s32[3]{0:T(128)S(1)} %pad_add_fusion.spot.place, bf16[256,2048]{1,0:T(8,128)(2,1)} %get-tuple-element.123.refs_0_.refs_8_, bf16[256,2048]{1,0:T(8,128)(2,1)S(1)} %copy-done.22, bf16[256,2048]{1,0:T(8,128)(2,1)S(1)} %copy-done.24, ...), custom_call_target="tpu_custom_call" | custom-call | flops 34359738368 | bytes 58720256 | tf_op jit(solution)/shard_map/pallas_call | solution.py:295
  484.0 26.4 %shard_map.223 = (bf16[4,4,256,512]{3,2,1,0:T(8,128)(2,1)}, bf16[4,4,256,512]{3,2,1,0:T(8,128)(2,1)}) custom-call(s32[3]{0:T(128)S(1)} %pad_add_fusion.spot.place, bf16[2048,2048]{1,0:T(8,128)(2,1)} %get-tuple-element.52.refs_0_.refs_1_, bf16[512,2048]{1,0:T(8,128)(2,1)S(1)} %copy-done.17, ...), custom_call_target="tpu_custom_call" | custom-call | flops 17179869184 | bytes 33554432 | tf_op jit(solution)/shard_map/pallas_call | solution.py:295
  512.8 38.9 %shard_map.225 = (bf16[1024,2048]{1,0:T(8,128)(2,1)}, bf16[1024,2048]{1,0:T(8,128)(2,1)}, bf16[256,2048]{1,0:T(8,128)(2,1)S(1)}, bf16[256,2048]{1,0:T(8,128)(2,1...) custom-call(s32[3]{0:T(128)S(1)} %pad_add_fusion.spot.place, ...), custom_call_target="tpu_custom_call" | custom-call | flops 25769803776 | bytes 58720256 | tf_op jit(solution)/shard_map/pallas_call | solution.py:295
  564.0 39.1 %shard_map.227 = (bf16[1024,2048]{1,0:T(8,128)(2,1)}, bf16[1024,2048]{1,0:T(8,128)(2,1)}, bf16[256,2048]{1,0:T(8,128)(2,1)S(1)}, bf16[256,2048]{1,0:T(8,128)(2,1...) custom-call(s32[3]{0:T(128)S(1)} %pad_add_fusion.spot.place, bf16[256,2048]{1,0:T(8,128)(2,1)} %copy-done.32, ...), custom_call_target="tpu_custom_call" | custom-call | flops 25769803776 | bytes 58720256 | tf_op jit(solution)/shard_map/pallas_call | solution.py:295
  611.1 49.2 %shard_map.228 = (bf16[4,4,256,512]{3,2,1,0:T(8,128)(2,1)}, bf16[4,4,256,512]{3,2,1,0:T(8,128)(2,1)}, bf16[4,4,256,512]{3,2,1,0:T(8,128)(2,1)}, bf16[4,4,256,512]{3,2,1,0:T(8,128)(2,1)}) custom-call(s32[3]{0:T(128)S(1)} %pad_add_fusion.spot.place, bf16[4,4,256,512]{3,2,1,0:T(8,128)(2,1)} %add_convert_fusion.4.refs_0_, ...), custom_call_target="tpu_custom_call" | custom-call | flops 34359738368 | bytes 67108864 | tf_op jit(solution)/shard_map/pallas_call | solution.py:295
  676.1 24.2 %shard_map.231 = (bf16[512,2048]{1,0:T(8,128)(2,1)S(1)}, bf16[512,2048]{1,0:T(8,128)(2,1)}, bf16[512,2048]{1,0:T(8,128)(2,1)}, bf16[512,2048]{1,0:T(8,128)(2,1)}) custom-call(s32[3]{0:T(128)S(1)} %pad_add_fusion.spot.place, bf16[512,2048]{1,0:T(8,128)(2,1)} %get-tuple-element.70.refs_1_.refs_0_.refs_3_, ...), custom_call_target="tpu_custom_call" | custom-call | flops 17179869184 | bytes 25165824 | tf_op jit(solution)/shard_map/pallas_call | solution.py:295
  738.5 35.1 %shard_map.237 = (bf16[512,2048]{1,0:T(8,128)(2,1)S(1)}, bf16[4,2,512,512]{3,2,1,0:T(8,128)(2,1)}) custom-call(s32[3]{0:T(128)S(1)} %pad_add_fusion.spot.place, bf16[4,4,256,512]{3,2,1,0:T(8,128)(2,1)} %get-tuple-element.71.refs_1_.refs_0_, bf16[4,4,256,512]{3,2,1,0:T(8,128)(2,1)} %get-tuple-element.72.refs_2_.refs_1_.refs_0_, ...), custom_call_target="tpu_custom_call" | custom-call | flops 21474836480 | bytes 8388608 | tf_op jit(solution)/shard_map/pallas_call | solution.py:235
  783.6 44.2 %collective-permute-done.45.refs_2_.refs_5_ = bf16[512,2048]{1,0:T(8,128)(2,1)} collective-permute-done((bf16[512,2048]{1,0:T(8,128)(2,1)}, bf16[512,2048]{1,0:T(8,128)(2,1)}, u32[]{:S(2)}, u32[]{:S(2)}) %collective-permute-start.45) | collective-permute-done | bytes 2097184 | tf_op jit(solution)/shard_map/ppermute | solution.py:920
  869.7 13.9 %collective-permute-done.50 = bf16[4,256,512]{2,1,0:T(8,128)(2,1)S(1)} collective-permute-done((bf16[4,256,512]{2,1,0:T(8,128)(2,1)S(1)}, bf16[4,256,512]{2,1,0:T(8,128)(2,1)S(1)}, u32[]{:S(2)}, u32[]{:S(2)}) %collective-permute-start.50) | collective-permute-done | bytes 1048608 | tf_op jit(solution)/shard_map/ppermute | solution.py:920
  909.6 19.1 %collective-permute-done.54 = bf16[4,256,512]{2,1,0:T(8,128)(2,1)} collective-permute-done((bf16[4,256,512]{2,1,0:T(8,128)(2,1)}, bf16[4,256,512]{2,1,0:T(8,128)(2,1)}, u32[]{:S(2)}, u32[]{:S(2)}) %collective-permute-start.54) | collective-permute-done | bytes 1048608 | tf_op jit(solution)/shard_map/ppermute | solution.py:920
  928.7 22.0 %collective-permute-done.53 = bf16[4,256,512]{2,1,0:T(8,128)(2,1)} collective-permute-done((bf16[4,256,512]{2,1,0:T(8,128)(2,1)}, bf16[4,256,512]{2,1,0:T(8,128)(2,1)}, u32[]{:S(2)}, u32[]{:S(2)}) %collective-permute-start.53) | collective-permute-done | bytes 1048608 | tf_op jit(solution)/shard_map/ppermute | solution.py:920
  965.1 17.5 %collective-permute-start.62 = (bf16[256,512]{1,0:T(8,128)(2,1)S(1)}, bf16[256,512]{1,0:T(8,128)(2,1)S(1)}, u32[]{:S(2)}, u32[]{:S(2)}) collective-permute-start(bf16[256,512]{1,0:T(8,128)(2,1)S(1)} %get-tuple-element.127), channel_id=1, source_target_pairs={{0,1},{1,2},{2,3},{3,0},{4,5},{5,6},{6,7},{7,4},{8,9},{9,10},{10,1... | collective-permute-start | bytes 786440 | tf_op jit(solution)/shard_map/ppermute | solution.py:948
  1029.3 12.0 %collective-permute-done.58 = bf16[4,272,256]{2,1,0:T(8,128)(2,1)S(1)} collective-permute-done((bf16[4,272,256]{2,1,0:T(8,128)(2,1)S(1)}, bf16[4,272,256]{2,1,0:T(8,128)(2,1)S(1)}, u32[]{:S(2)}, u32[]{:S(2)}) %collective-permute-start.58) | collective-permute-done | bytes 557088 | tf_op jit(solution)/shard_map/ppermute | solution.py:920
  1041.3 11.5 %collective-permute-done.57 = bf16[4,272,256]{2,1,0:T(8,128)(2,1)S(1)} collective-permute-done((bf16[4,272,256]{2,1,0:T(8,128)(2,1)S(1)}, bf16[4,272,256]{2,1,0:T(8,128)(2,1)S(1)}, u32[]{:S(2)}, u32[]{:S(2)}) %collective-permute-start.57) | collective-permute-done | bytes 557088 | tf_op jit(solution)/shard_map/ppermute | solution.py:920
  (464 shorter events, 393.3 us)
Async XLA Ops:
  7.2 58.6 %all-gather.11.cloned.1.call-start = ((), (), s32[]{:S(2)}) async-start(), calls=%async_computation.8 | async-start | bytes 5013504 | tf_op jit(solution)/shard_map/all_gather | solution.py:1087
  27.5 177.2 %all-gather.13.cloned.1.call-start = ((), (), s32[]{:S(2)}) async-start(), calls=%async_computation.9 | async-start | bytes 5242880 | tf_op jit(solution)/shard_map/all_gather | solution.py:1083
  86.3 238.2 %all-gather.15.cloned.1.call-start = ((), (), s32[]{:S(2)}) async-start(), calls=%async_computation.10 | async-start | bytes 5242880 | tf_op jit(solution)/shard_map/all_gather | solution.py:1083
  93.2 62.3 %collective-permute-start.9 = (bf16[4,256,512]{2,1,0:T(8,128)(2,1)}, bf16[4,256,512]{2,1,0:T(8,128)(2,1)}, u32[]{:S(2)}, u32[]{:S(2)}) collective-permute-start(bf16[4,256,512]{2,1,0:T(8,128)(2,1)} %shard_map.205.refs_1_.refs_2_), channel_id=1, source_target_pairs={{0,4},{4,0},{8,12},{12,8},{16,20},{20,16},{24,28},{28,24},{1,5},{5... | collective-permute-start | bytes 3145736 | tf_op jit(solution)/shard_map/ppermute | solution.py:920
  197.2 160.3 %all-gather.17.cloned.1.call-start = ((), (), s32[]{:S(2)}) async-start(), calls=%async_computation.11 | async-start | bytes 5242880 | tf_op jit(solution)/shard_map/all_gather | solution.py:1083
  197.8 240.5 %all-gather.19.cloned.1.call-start = ((), (), s32[]{:S(2)}) async-start(), calls=%async_computation.12 | async-start | bytes 5242880 | tf_op jit(solution)/shard_map/all_gather | solution.py:1083
  275.2 388.1 %reduce-scatter.5.cloned.1.call-start = ((), (), s32[]{:S(2)}) async-start(), calls=%async_computation.4 | async-start | bytes 5242880 | tf_op jit(solution)/shard_map/reduce_scatter | solution.py:1178
  369.0 69.3 %collective-permute-start.30 = (bf16[4,1024,512]{2,1,0:T(8,128)(2,1)}, bf16[4,1024,512]{2,1,0:T(8,128)(2,1)}, u32[]{:S(2)}, u32[]{:S(2)}) collective-permute-start(bf16[4,1024,512]{2,1,0:T(8,128)(2,1)} %shard_map.220.refs_9_.refs_11_.refs_13_), channel_id=1, source_target_pairs={{0,4},{4,0},{8,12},{12,8},{16,20},{20,16},{24,28},{28,24},{1,5},{5... | collective-permute-start | bytes 12582920 | tf_op jit(solution)/shard_map/ppermute | solution.py:920
  371.9 112.1 %collective-permute-start.31 = (bf16[512,2048]{1,0:T(8,128)(2,1)}, bf16[512,2048]{1,0:T(8,128)(2,1)}, u32[]{:S(2)}, u32[]{:S(2)}) collective-permute-start(bf16[512,2048]{1,0:T(8,128)(2,1)} %shard_map.222.refs_1_.refs_5_.refs_2_.refs_4_), channel_id=1, source_target_pairs={{0,8},{4,12},{8,0},{12,4},{16,24},{20,28},{24,16},{28,20},{1,9},{5... | collective-permute-start | bytes 6291464 | tf_op jit(solution)/shard_map/ppermute | solution.py:920
  371.9 112.1 %collective-permute-start.32 = (bf16[512,2048]{1,0:T(8,128)(2,1)}, bf16[512,2048]{1,0:T(8,128)(2,1)}, u32[]{:S(2)}, u32[]{:S(2)}) collective-permute-start(bf16[512,2048]{1,0:T(8,128)(2,1)} %shard_map.222.refs_1_.refs_5_.refs_2_.refs_4_), channel_id=1, source_target_pairs={{0,16},{4,20},{8,24},{12,28},{16,0},{20,4},{24,8},{28,12},{1,17},{... | collective-permute-start | bytes 6291464 | tf_op jit(solution)/shard_map/ppermute | solution.py:920
  373.9 110.1 %collective-permute-start.33 = (bf16[512,2048]{1,0:T(8,128)(2,1)}, bf16[512,2048]{1,0:T(8,128)(2,1)}, u32[]{:S(2)}, u32[]{:S(2)}) collective-permute-start(bf16[512,2048]{1,0:T(8,128)(2,1)} %shard_map.222.refs_1_.refs_5_.refs_2_.refs_4_), channel_id=1, source_target_pairs={{0,24},{4,28},{8,16},{12,20},{16,8},{20,12},{24,0},{28,4},{1,25},{... | collective-permute-start | bytes 6291464 | tf_op jit(solution)/shard_map/ppermute | solution.py:920
  438.2 72.6 %collective-permute-start.34 = (bf16[4,4,256,512]{3,2,1,0:T(8,128)(2,1)}, bf16[4,4,256,512]{3,2,1,0:T(8,128)(2,1)S(1)}, u32[]{:S(2)}, u32[]{:S(2)}) collective-permute-start(bf16[4,4,256,512]{3,2,1,0:T(8,128)(2,1)} %bitcast.279), channel_id=1, source_target_pairs={{0,4},{4,0},{8,12},{12,8},{16,20},{20,16},{24,28},{28,24},{1,5},{5... | collective-permute-start | bytes 12582920 | tf_op jit(solution)/shard_map/ppermute | solution.py:920
  560.4 269.3 %reduce-scatter.7.cloned.1.call-start = ((), (), s32[]{:S(2)}) async-start(), calls=%async_computation.5 | async-start | bytes 5242880 | tf_op jit(solution)/shard_map/reduce_scatter | solution.py:1178
  603.0 58.3 %collective-permute-start.39 = (bf16[256,2048]{1,0:T(8,128)(2,1)S(1)}, bf16[256,2048]{1,0:T(8,128)(2,1)S(1)}, u32[]{:S(2)}, u32[]{:S(2)}) collective-permute-start(bf16[256,2048]{1,0:T(8,128)(2,1)S(1)} %get-tuple-element.63.refs_2_), channel_id=1, source_target_pairs={{0,8},{4,12},{8,0},{12,4},{16,24},{20,28},{24,16},{28,20},{1,9},{5... | collective-permute-start | bytes 3145736 | tf_op jit(solution)/shard_map/ppermute | solution.py:920
  604.8 56.6 %collective-permute-start.40 = (bf16[256,2048]{1,0:T(8,128)(2,1)S(1)}, bf16[256,2048]{1,0:T(8,128)(2,1)S(1)}, u32[]{:S(2)}, u32[]{:S(2)}) collective-permute-start(bf16[256,2048]{1,0:T(8,128)(2,1)S(1)} %get-tuple-element.64.refs_3_), channel_id=1, source_target_pairs={{0,16},{4,20},{8,24},{12,28},{16,0},{20,4},{24,8},{28,12},{1,17},{... | collective-permute-start | bytes 3145736 | tf_op jit(solution)/shard_map/ppermute | solution.py:920
  606.3 57.1 %collective-permute-start.41 = (bf16[256,2048]{1,0:T(8,128)(2,1)}, bf16[256,2048]{1,0:T(8,128)(2,1)}, u32[]{:S(2)}, u32[]{:S(2)}) collective-permute-start(bf16[256,2048]{1,0:T(8,128)(2,1)} %get-tuple-element.65.refs_4_), channel_id=1, source_target_pairs={{0,24},{4,28},{8,16},{12,20},{16,8},{20,12},{24,0},{28,4},{1,25},{... | collective-permute-start | bytes 3145736 | tf_op jit(solution)/shard_map/ppermute | solution.py:920
  708.5 182.7 %reduce-scatter.11.cloned.1.call-start = ((), (), s32[]{:S(2)}) async-start(), calls=%async_computation.7 | async-start | bytes 5242880 | tf_op jit(solution)/shard_map/reduce_scatter | solution.py:1178
  734.8 264.9 %reduce-scatter.9.cloned.1.call-start = ((), (), s32[]{:S(2)}) async-start(), calls=%async_computation.6 | async-start | bytes 5242880 | tf_op jit(solution)/shard_map/reduce_scatter | solution.py:1178
  736.4 91.4 %collective-permute-start.45 = (bf16[512,2048]{1,0:T(8,128)(2,1)}, bf16[512,2048]{1,0:T(8,128)(2,1)}, u32[]{:S(2)}, u32[]{:S(2)}) collective-permute-start(bf16[512,2048]{1,0:T(8,128)(2,1)} %get-tuple-element.80), channel_id=1, source_target_pairs={{0,16},{4,20},{8,24},{12,28},{16,0},{20,4},{24,8},{28,12},{1,17},{... | collective-permute-start | bytes 6291464 | tf_op jit(solution)/shard_map/ppermute | solution.py:920
  737.1 92.6 %collective-permute-start.46 = (bf16[512,2048]{1,0:T(8,128)(2,1)}, bf16[512,2048]{1,0:T(8,128)(2,1)}, u32[]{:S(2)}, u32[]{:S(2)}) collective-permute-start(bf16[512,2048]{1,0:T(8,128)(2,1)} %get-tuple-element.81), channel_id=1, source_target_pairs={{0,24},{4,28},{8,16},{12,20},{16,8},{20,12},{24,0},{28,4},{1,25},{... | collective-permute-start | bytes 6291464 | tf_op jit(solution)/shard_map/ppermute | solution.py:920
  867.6 61.1 %collective-permute-start.54 = (bf16[4,256,512]{2,1,0:T(8,128)(2,1)}, bf16[4,256,512]{2,1,0:T(8,128)(2,1)}, u32[]{:S(2)}, u32[]{:S(2)}) collective-permute-start(bf16[4,256,512]{2,1,0:T(8,128)(2,1)} %get-tuple-element.100), channel_id=1, source_target_pairs={{0,24},{4,28},{8,16},{12,20},{16,8},{20,12},{24,0},{28,4},{1,25},{... | collective-permute-start | bytes 3145736 | tf_op jit(solution)/shard_map/ppermute | solution.py:920
  869.4 81.3 %collective-permute-start.53 = (bf16[4,256,512]{2,1,0:T(8,128)(2,1)}, bf16[4,256,512]{2,1,0:T(8,128)(2,1)}, u32[]{:S(2)}, u32[]{:S(2)}) collective-permute-start(bf16[4,256,512]{2,1,0:T(8,128)(2,1)} %get-tuple-element.101), channel_id=1, source_target_pairs={{0,16},{4,20},{8,24},{12,28},{16,0},{20,4},{24,8},{28,12},{1,17},{... | collective-permute-start | bytes 3145736 | tf_op jit(solution)/shard_map/ppermute | solution.py:920
  883.6 67.1 %collective-permute-start.52 = (bf16[4,256,512]{2,1,0:T(8,128)(2,1)}, bf16[4,256,512]{2,1,0:T(8,128)(2,1)}, u32[]{:S(2)}, u32[]{:S(2)}) collective-permute-start(bf16[4,256,512]{2,1,0:T(8,128)(2,1)} %get-tuple-element.99), channel_id=1, source_target_pairs={{0,8},{4,12},{8,0},{12,4},{16,24},{20,28},{24,16},{28,20},{1,9},{5... | collective-permute-start | bytes 3145736 | tf_op jit(solution)/shard_map/ppermute | solution.py:920
  909.6 51.2 %collective-permute-start.66 = (bf16[256,512]{1,0:T(8,128)(2,1)S(1)}, bf16[256,512]{1,0:T(8,128)(2,1)}, u32[]{:S(2)}, u32[]{:S(2)}) collective-permute-start(bf16[256,512]{1,0:T(8,128)(2,1)S(1)} %get-tuple-element.126), channel_id=1, source_target_pairs={{0,2},{1,3},{2,0},{3,1},{4,6},{5,7},{6,4},{7,5},{8,10},{9,11},{10,... | collective-permute-start | bytes 786440 | tf_op jit(solution)/shard_map/ppermute | solution.py:948
  (143 other events, 2635.1 us)
Sparse Core Ops, SparseCore 0:
  27.6 38.1 all-gather.10
  86.4 79.0 all-gather.12
  197.3 79.3 all-gather.14
  278.2 79.2 all-gather.16
  358.9 79.2 all-gather.18
  560.5 75.3 reduce-scatter.4
  708.6 75.0 reduce-scatter.6
  786.0 77.2 reduce-scatter.10
  865.7 94.3 reduce-scatter.8

commit v5 on v4

--- a/solution.py
+++ b/solution.py
@@ -76,7 +76,7 @@
             lse_ref[0, 0, pl.ds(head, 1), :] = top + jnp.log2(total)
         return carry
 
-    lax.fori_loop(0, group, step, 0)
+    lax.fori_loop(0, group, step, 0, unroll=4)
     o_ref[...] = ot_ref[...].T.astype(bf16)
 
 
@@ -176,7 +176,7 @@
             dv_ref[:n, :] += nn(jnp.concatenate(all_p, 1), g_rows)
         return carry
 
-    lax.fori_loop(0, group // 2, step, 0)
+    lax.fori_loop(0, group // 2, step, 0, unroll=2)
     scale = HD**-0.5
     dq = dqt_ref[...].T * scale
     for t in range(dq.shape[1] // LANES):
@@ -1214,16 +1214,17 @@
     query_near = plane_sum(core_sum(query_parts), chip)
     grad_query = line_scatter(query_near)
     mixed = finish_mixed(spot, residual, mixed, deps=query_parts)
-    come = trade(after(jnp.stack([down_sum, gate_sum, up_sum], 1), out_near, query_near), 0, chip)
-    grad_down = jnp.concatenate([jnp.concatenate([c[0, :, :block], c[0, :, block:]], 0) for c in come], 0)
-    grad_gate, grad_up = (jnp.concatenate([c[n] for c in come], 1) for n in (1, 2))
-
     dkv = finish_pairs(spot, dkv, cos_rows, sin_rows, deps=[out_near, query_near])
     grad_normed_one, gain_one_terms = unproject_pairs(spot, partial, dkv, all_kv, scaled_one)
     gain_one_terms = gain_one_terms[0]
     gain_terms = jnp.stack([gain_one_terms.reshape(8, block), gain_two_terms.reshape(8, block)], 1)
     gain_terms = jnp.pad(gain_terms, ((0, 0), (0, 14), (0, kv_cols - block)))
     kv_parts = in_blocks_grad(spot, normed_one, dq, dkv, gain_terms, tp_count)
+    held = lambda a: after(a, kv_parts)
+    come = trade(after(jnp.stack([down_sum, gate_sum, up_sum], 1), out_near, query_near), 0, chip, held)
+    grad_down = jnp.concatenate([jnp.concatenate([c[0, :, :block], c[0, :, block:]], 0) for c in come], 0)
+    grad_gate, grad_up = (jnp.concatenate([c[n] for c in come], 1) for n in (1, 2))
+
     kv_sum = line_scatter(plane_sum(core_sum(kv_parts), chip))
     grad_tokens = grad_residual + norm_backward(grad_normed_one * gain_one, x * norm_one, norm_one)
     grad_tokens = grad_tokens.astype(bf16)

time: 1090 us -> 1070 us (0.982)
  starting transfers between devices: 84 us -> 65.5 us
  waiting for transfers between devices: 455 us -> 473 us
  Pallas kernels: 381 us -> 370 us
    ppermute x15, starting transfers between devices: 34.8 us -> 17 us  [shift(): return lax.ppermute(a, 'tensor', [(i, (i + step) % n) for i in range(n)])]
    ppermute x15, waiting for transfers between devices: 33.2 us -> 48.6 us  [shift(): return lax.ppermute(a, 'tensor', [(i, (i + step) % n) for i in range(n)])]
    unnamed x188 -> x170, local copies, waits for them, and re-layouts: 38.1 us -> 33.7 us
  transfers between devices with their start and end apart: 80 -> 80, of which waited for: 36 -> 35; matrix products, arithmetic and copies ran while one was open for 9% -> 8% of each run, Pallas kernels for 32% -> 33%
where the time goes in v5:
time: 1070 us; the launch traced here: 1060 us
  waiting for transfers between devices  473 us (44%)
  Pallas kernels  370 us (35%)
  other arithmetic  75.1 us (7%)
  starting transfers between devices  65.5 us (6%)
  local copies, waits for them, and re-layouts  63.4 us (6%)
  between operations  15.3 us (1%)
    pallas_call x18, Pallas kernels, grid_call(): return lambda spot, *arrays: run(spot, *deps, *arrays)  318 us
    ppermute x56, waiting for transfers between devices, hop(): return lax.ppermute(a, 'dp', [(i, i ^ bits) for i in range(n)])  304 us
    all_gather x4, waiting for transfers between devices, along(): return lax.all_gather(a, 'tensor', axis=0, tiled=False)  90 us
    ppermute x15, waiting for transfers between devices, shift(): return lax.ppermute(a, 'tensor', [(i, (i + step) % n) for i in range(n)])  48.6 us
    ppermute x56, starting transfers between devices, hop(): return lax.ppermute(a, 'dp', [(i, i ^ bits) for i in range(n)])  48.2 us
    unnamed x170, local copies, waits for them, and re-layouts  33.7 us
    all_gather x1, waiting for transfers between devices, in_plane(): return lax.all_gather(a, 'dp', axis=0, tiled=False)  30 us
    pallas_call x1, Pallas kernels, unattend(): call(functools.partial(unattend_kernel, count, group, len(deps)), flops=r...  28.4 us
  transfers between devices with their start and end apart: 80, of which 35 were waited for; matrix products, arithmetic and copies ran while one was open for 8% of the time, Pallas kernels for 33%

profile of v5, /device:TPU:0, one launch (start us, length us, event | category | flops | bytes accessed | tf_op | source)
XLA Modules:
  0.0 1063.3 jit_solution(5729719998248397329)
XLA Ops:
  35.9 30.0 %all-gather.11.cloned.1.call-done = bf16[32,272,256]{2,1,0:T(8,128)(2,1)} async-done(((bf16[4,272,256]{2,1,0:T(8,128)(2,1)}), bf16[32,272,256]{2,1,0:T(8,128)(2,1)}) %all-gather.11.cloned.1.call-update) | async-done | bytes 4456464 | tf_op jit(solution)/shard_map/all_gather | solution.py:1087
  93.2 22.9 %collective-permute-done.6.refs_2_.refs_1_.refs_3_ = bf16[4,256,512]{2,1,0:T(8,128)(2,1)} collective-permute-done((bf16[4,256,512]{2,1,0:T(8,128)(2,1)}, bf16[4,256,512]{2,1,0:T(8,128)(2,1)}, u32[]{:S(2)}, u32[]{:S(2)}) %collective-permute-start.6) | collective-permute-done | bytes 1048608 | tf_op jit(solution)/shard_map/ppermute | solution.py:920
  116.1 21.2 %collective-permute-done.7.refs_3_.refs_2_.refs_4_ = bf16[4,256,512]{2,1,0:T(8,128)(2,1)} collective-permute-done((bf16[4,256,512]{2,1,0:T(8,128)(2,1)}, bf16[4,256,512]{2,1,0:T(8,128)(2,1)}, u32[]{:S(2)}, u32[]{:S(2)}) %collective-permute-start.7) | collective-permute-done | bytes 1048608 | tf_op jit(solution)/shard_map/ppermute | solution.py:920
  175.7 16.3 %collective-permute-done.14 = bf16[3,256,512]{2,1,0:T(8,128)(2,1)} collective-permute-done((bf16[3,256,512]{2,1,0:T(8,128)(2,1)}, bf16[3,256,512]{2,1,0:T(8,128)(2,1)}, u32[]{:S(2)}, u32[]{:S(2)}) %collective-permute-start.14) | collective-permute-done | bytes 786464 | tf_op jit(solution)/shard_map/ppermute | solution.py:920
  206.8 23.5 %shard_map.207 = (bf16[512,2048]{1,0:T(8,128)(2,1)S(1)}, f32[2,4,8,256]{3,2,1,0:T(8,128)S(1)}) custom-call(s32[3]{0:T(128)S(1)} %pad_add_fusion.spot.place, bf16[512,2048]{1,0:T(8,128)(2,1)} %shard_map.206.refs_0_.refs_1_.refs_4_, bf16[4,2,512,512]{3,2,1,0:T(8,128)(2,1)} %bitcast.214, bf16[4,2,512,512]{3,2,1,0:T(8,128)(2,1)} %bitcast.215, ...), custom_call_target="tpu_custom_call" | custom-call | flops 8589934592 | bytes 4194304 | tf_op jit(solution)/shard_map/pallas_call | solution.py:123
  231.6 18.4 %collective-permute-done.17.refs_0_ = bf16[4,256,512]{2,1,0:T(8,128)(2,1)S(1)} collective-permute-done((bf16[4,256,512]{2,1,0:T(8,128)(2,1)}, bf16[4,256,512]{2,1,0:T(8,128)(2,1)S(1)}, u32[]{:S(2)}, u32[]{:S(2)}) %collective-permute-start.17) | collective-permute-done | bytes 1048608 | tf_op jit(solution)/shard_map/ppermute | solution.py:920
  277.4 22.7 %collective-permute-done.23.refs_1_.refs_9_ = bf16[256,2048]{1,0:T(8,128)(2,1)S(1)} collective-permute-done((bf16[256,2048]{1,0:T(8,128)(2,1)}, bf16[256,2048]{1,0:T(8,128)(2,1)S(1)}, u32[]{:S(2)}, u32[]{:S(2)}) %collective-permute-start.23) | collective-permute-done | bytes 1048608 | tf_op jit(solution)/shard_map/ppermute | solution.py:920
  300.0 22.1 %collective-permute-done.24.refs_2_.refs_10_ = bf16[256,2048]{1,0:T(8,128)(2,1)S(1)} collective-permute-done((bf16[256,2048]{1,0:T(8,128)(2,1)}, bf16[256,2048]{1,0:T(8,128)(2,1)S(1)}, u32[]{:S(2)}, u32[]{:S(2)}) %collective-permute-start.24) | collective-permute-done | bytes 1048608 | tf_op jit(solution)/shard_map/ppermute | solution.py:920
  326.6 30.1 %all-gather.17.cloned.1.call-done = bf16[4096,512]{1,0:T(8,128)(2,1)} async-done(((bf16[1024,512]{1,0:T(8,128)(2,1)}), bf16[4096,512]{1,0:T(8,128)(2,1)}) %all-gather.17.cloned.1.call-update) | async-done | bytes 4194320 | tf_op jit(solution)/shard_map/all_gather | solution.py:1083
  356.7 13.4 %collective-permute-done.27.refs_2_.refs_6_.refs_14_ = bf16[256,2048]{1,0:T(8,128)(2,1)S(1)} collective-permute-done((bf16[256,2048]{1,0:T(8,128)(2,1)}, bf16[256,2048]{1,0:T(8,128)(2,1)S(1)}, u32[]{:S(2)}, u32[]{:S(2)}) %collective-permute-start.27) | collective-permute-done | bytes 1048608 | tf_op jit(solution)/shard_map/ppermute | solution.py:920
  377.5 59.9 %all-gather.19.cloned.1.call-done = bf16[16,256,512]{2,1,0:T(8,128)(2,1)} async-done(((bf16[4,256,512]{2,1,0:T(8,128)(2,1)}), bf16[16,256,512]{2,1,0:T(8,128)(2,1)}) %all-gather.19.cloned.1.call-update) | async-done | bytes 4194320 | tf_op jit(solution)/shard_map/all_gather | solution.py:1083
  440.1 43.2 %shard_map.221 = (bf16[2048,2048]{1,0:T(8,128)(2,1)}, bf16[2048,2048]{1,0:T(8,128)(2,1)}, bf16[2048,2048]{1,0:T(8,128)(2,1)}) custom-call(s32[3]{0:T(128)S(1)} %pad_add_fusion.spot.place, bf16[256,2048]{1,0:T(8,128)(2,1)} %get-tuple-element.124.refs_0_.refs_8_, bf16[256,2048]{1,0:T(8,128)(2,1)S(1)} %copy-done.22, bf16[256,2048]{1,0:T(8,128)(2,1)S(1)} %copy-done.24, ...), custom_call_target="tpu_custom_call" | custom-call | flops 34359738368 | bytes 58720256 | tf_op jit(solution)/shard_map/pallas_call | solution.py:295
  483.3 26.4 %shard_map.223 = (bf16[4,4,256,512]{3,2,1,0:T(8,128)(2,1)}, bf16[4,4,256,512]{3,2,1,0:T(8,128)(2,1)}) custom-call(s32[3]{0:T(128)S(1)} %pad_add_fusion.spot.place, bf16[2048,2048]{1,0:T(8,128)(2,1)} %get-tuple-element.52.refs_0_.refs_1_, bf16[512,2048]{1,0:T(8,128)(2,1)S(1)} %copy-done.17, ...), custom_call_target="tpu_custom_call" | custom-call | flops 17179869184 | bytes 33554432 | tf_op jit(solution)/shard_map/pallas_call | solution.py:295
  512.0 38.6 %shard_map.225 = (bf16[1024,2048]{1,0:T(8,128)(2,1)}, bf16[1024,2048]{1,0:T(8,128)(2,1)}, bf16[256,2048]{1,0:T(8,128)(2,1)S(1)}, bf16[256,2048]{1,0:T(8,128)(2,1...) custom-call(s32[3]{0:T(128)S(1)} %pad_add_fusion.spot.place, ...), custom_call_target="tpu_custom_call" | custom-call | flops 25769803776 | bytes 58720256 | tf_op jit(solution)/shard_map/pallas_call | solution.py:295
  562.9 39.0 %shard_map.227 = (bf16[1024,2048]{1,0:T(8,128)(2,1)}, bf16[1024,2048]{1,0:T(8,128)(2,1)}, bf16[256,2048]{1,0:T(8,128)(2,1)S(1)}, bf16[256,2048]{1,0:T(8,128)(2,1...) custom-call(s32[3]{0:T(128)S(1)} %pad_add_fusion.spot.place, bf16[256,2048]{1,0:T(8,128)(2,1)} %copy-done.32, ...), custom_call_target="tpu_custom_call" | custom-call | flops 25769803776 | bytes 58720256 | tf_op jit(solution)/shard_map/pallas_call | solution.py:295
  610.1 49.2 %shard_map.228 = (bf16[4,4,256,512]{3,2,1,0:T(8,128)(2,1)}, bf16[4,4,256,512]{3,2,1,0:T(8,128)(2,1)}, bf16[4,4,256,512]{3,2,1,0:T(8,128)(2,1)}, bf16[4,4,256,512]{3,2,1,0:T(8,128)(2,1)}) custom-call(s32[3]{0:T(128)S(1)} %pad_add_fusion.spot.place, bf16[4,4,256,512]{3,2,1,0:T(8,128)(2,1)} %add_convert_fusion.4.refs_0_, ...), custom_call_target="tpu_custom_call" | custom-call | flops 34359738368 | bytes 67108864 | tf_op jit(solution)/shard_map/pallas_call | solution.py:295
  675.1 24.4 %shard_map.231 = (bf16[512,2048]{1,0:T(8,128)(2,1)S(1)}, bf16[512,2048]{1,0:T(8,128)(2,1)}, bf16[512,2048]{1,0:T(8,128)(2,1)}, bf16[512,2048]{1,0:T(8,128)(2,1)}) custom-call(s32[3]{0:T(128)S(1)} %pad_add_fusion.spot.place, bf16[512,2048]{1,0:T(8,128)(2,1)} %get-tuple-element.70.refs_1_.refs_0_.refs_3_, ...), custom_call_target="tpu_custom_call" | custom-call | flops 17179869184 | bytes 25165824 | tf_op jit(solution)/shard_map/pallas_call | solution.py:295
  737.5 28.4 %shard_map.237 = (bf16[512,2048]{1,0:T(8,128)(2,1)S(1)}, bf16[4,2,512,512]{3,2,1,0:T(8,128)(2,1)}) custom-call(s32[3]{0:T(128)S(1)} %pad_add_fusion.spot.place, bf16[4,4,256,512]{3,2,1,0:T(8,128)(2,1)} %get-tuple-element.71.refs_1_.refs_0_, bf16[4,4,256,512]{3,2,1,0:T(8,128)(2,1)} %get-tuple-element.72.refs_2_.refs_1_.refs_0_, ...), custom_call_target="tpu_custom_call" | custom-call | flops 21474836480 | bytes 8388608 | tf_op jit(solution)/shard_map/pallas_call | solution.py:235
  767.2 15.5 %collective-permute-done.44.refs_1_.refs_4_ = bf16[512,2048]{1,0:T(8,128)(2,1)S(1)} collective-permute-done((bf16[512,2048]{1,0:T(8,128)(2,1)}, bf16[512,2048]{1,0:T(8,128)(2,1)S(1)}, u32[]{:S(2)}, u32[]{:S(2)}) %collective-permute-start.44) | collective-permute-done | bytes 2097184 | tf_op jit(solution)/shard_map/ppermute | solution.py:920
  782.7 44.3 %collective-permute-done.45.refs_2_.refs_5_ = bf16[512,2048]{1,0:T(8,128)(2,1)} collective-permute-done((bf16[512,2048]{1,0:T(8,128)(2,1)}, bf16[512,2048]{1,0:T(8,128)(2,1)}, u32[]{:S(2)}, u32[]{:S(2)}) %collective-permute-start.45) | collective-permute-done | bytes 2097184 | tf_op jit(solution)/shard_map/ppermute | solution.py:920
  866.1 16.2 %collective-permute-done.50 = bf16[4,256,512]{2,1,0:T(8,128)(2,1)S(1)} collective-permute-done((bf16[4,256,512]{2,1,0:T(8,128)(2,1)S(1)}, bf16[4,256,512]{2,1,0:T(8,128)(2,1)S(1)}, u32[]{:S(2)}, u32[]{:S(2)}) %collective-permute-start.50) | collective-permute-done | bytes 1048608 | tf_op jit(solution)/shard_map/ppermute | solution.py:920
  909.1 18.3 %collective-permute-done.54 = bf16[4,256,512]{2,1,0:T(8,128)(2,1)} collective-permute-done((bf16[4,256,512]{2,1,0:T(8,128)(2,1)}, bf16[4,256,512]{2,1,0:T(8,128)(2,1)}, u32[]{:S(2)}, u32[]{:S(2)}) %collective-permute-start.54) | collective-permute-done | bytes 1048608 | tf_op jit(solution)/shard_map/ppermute | solution.py:920
  927.5 21.4 %collective-permute-done.53 = bf16[4,256,512]{2,1,0:T(8,128)(2,1)} collective-permute-done((bf16[4,256,512]{2,1,0:T(8,128)(2,1)}, bf16[4,256,512]{2,1,0:T(8,128)(2,1)}, u32[]{:S(2)}, u32[]{:S(2)}) %collective-permute-start.53) | collective-permute-done | bytes 1048608 | tf_op jit(solution)/shard_map/ppermute | solution.py:920
  966.4 20.3 %collective-permute-done.63 = bf16[256,512]{1,0:T(8,128)(2,1)} collective-permute-done((bf16[256,512]{1,0:T(8,128)(2,1)}, bf16[256,512]{1,0:T(8,128)(2,1)}, u32[]{:S(2)}, u32[]{:S(2)}) %collective-permute-start.63) | collective-permute-done | bytes 262176 | tf_op jit(solution)/shard_map/ppermute | solution.py:948
  (448 shorter events, 382.3 us)
Async XLA Ops:
  7.2 58.6 %all-gather.11.cloned.1.call-start = ((), (), s32[]{:S(2)}) async-start(), calls=%async_computation.8 | async-start | bytes 5013504 | tf_op jit(solution)/shard_map/all_gather | solution.py:1087
  27.5 179.3 %all-gather.13.cloned.1.call-start = ((), (), s32[]{:S(2)}) async-start(), calls=%async_computation.9 | async-start | bytes 5242880 | tf_op jit(solution)/shard_map/all_gather | solution.py:1083
  86.3 240.3 %all-gather.15.cloned.1.call-start = ((), (), s32[]{:S(2)}) async-start(), calls=%async_computation.10 | async-start | bytes 5242880 | tf_op jit(solution)/shard_map/all_gather | solution.py:1083
  93.2 62.3 %collective-permute-start.9 = (bf16[4,256,512]{2,1,0:T(8,128)(2,1)}, bf16[4,256,512]{2,1,0:T(8,128)(2,1)}, u32[]{:S(2)}, u32[]{:S(2)}) collective-permute-start(bf16[4,256,512]{2,1,0:T(8,128)(2,1)} %shard_map.205.refs_1_.refs_2_), channel_id=1, source_target_pairs={{0,4},{4,0},{8,12},{12,8},{16,20},{20,16},{24,28},{28,24},{1,5},{5... | collective-permute-start | bytes 3145736 | tf_op jit(solution)/shard_map/ppermute | solution.py:920
  196.4 160.3 %all-gather.17.cloned.1.call-start = ((), (), s32[]{:S(2)}) async-start(), calls=%async_computation.11 | async-start | bytes 5242880 | tf_op jit(solution)/shard_map/all_gather | solution.py:1083
  197.0 240.4 %all-gather.19.cloned.1.call-start = ((), (), s32[]{:S(2)}) async-start(), calls=%async_computation.12 | async-start | bytes 5242880 | tf_op jit(solution)/shard_map/all_gather | solution.py:1083
  277.3 385.0 %reduce-scatter.5.cloned.1.call-start = ((), (), s32[]{:S(2)}) async-start(), calls=%async_computation.4 | async-start | bytes 5242880 | tf_op jit(solution)/shard_map/reduce_scatter | solution.py:1178
  371.1 66.3 %collective-permute-start.30 = (bf16[4,1024,512]{2,1,0:T(8,128)(2,1)}, bf16[4,1024,512]{2,1,0:T(8,128)(2,1)}, u32[]{:S(2)}, u32[]{:S(2)}) collective-permute-start(bf16[4,1024,512]{2,1,0:T(8,128)(2,1)} %shard_map.220.refs_9_.refs_11_.refs_13_), channel_id=1, source_target_pairs={{0,4},{4,0},{8,12},{12,8},{16,20},{20,16},{24,28},{28,24},{1,5},{5... | collective-permute-start | bytes 12582920 | tf_op jit(solution)/shard_map/ppermute | solution.py:920
  374.1 109.2 %collective-permute-start.31 = (bf16[512,2048]{1,0:T(8,128)(2,1)}, bf16[512,2048]{1,0:T(8,128)(2,1)}, u32[]{:S(2)}, u32[]{:S(2)}) collective-permute-start(bf16[512,2048]{1,0:T(8,128)(2,1)} %shard_map.222.refs_1_.refs_5_.refs_2_.refs_4_), channel_id=1, source_target_pairs={{0,8},{4,12},{8,0},{12,4},{16,24},{20,28},{24,16},{28,20},{1,9},{5... | collective-permute-start | bytes 6291464 | tf_op jit(solution)/shard_map/ppermute | solution.py:920
  374.1 109.2 %collective-permute-start.32 = (bf16[512,2048]{1,0:T(8,128)(2,1)}, bf16[512,2048]{1,0:T(8,128)(2,1)}, u32[]{:S(2)}, u32[]{:S(2)}) collective-permute-start(bf16[512,2048]{1,0:T(8,128)(2,1)} %shard_map.222.refs_1_.refs_5_.refs_2_.refs_4_), channel_id=1, source_target_pairs={{0,16},{4,20},{8,24},{12,28},{16,0},{20,4},{24,8},{28,12},{1,17},{... | collective-permute-start | bytes 6291464 | tf_op jit(solution)/shard_map/ppermute | solution.py:920
  376.0 107.2 %collective-permute-start.33 = (bf16[512,2048]{1,0:T(8,128)(2,1)}, bf16[512,2048]{1,0:T(8,128)(2,1)}, u32[]{:S(2)}, u32[]{:S(2)}) collective-permute-start(bf16[512,2048]{1,0:T(8,128)(2,1)} %shard_map.222.refs_1_.refs_5_.refs_2_.refs_4_), channel_id=1, source_target_pairs={{0,24},{4,28},{8,16},{12,20},{16,8},{20,12},{24,0},{28,4},{1,25},{... | collective-permute-start | bytes 6291464 | tf_op jit(solution)/shard_map/ppermute | solution.py:920
  437.5 72.6 %collective-permute-start.34 = (bf16[4,4,256,512]{3,2,1,0:T(8,128)(2,1)}, bf16[4,4,256,512]{3,2,1,0:T(8,128)(2,1)S(1)}, u32[]{:S(2)}, u32[]{:S(2)}) collective-permute-start(bf16[4,4,256,512]{3,2,1,0:T(8,128)(2,1)} %bitcast.264), channel_id=1, source_target_pairs={{0,4},{4,0},{8,12},{12,8},{16,20},{20,16},{24,28},{28,24},{1,5},{5... | collective-permute-start | bytes 12582920 | tf_op jit(solution)/shard_map/ppermute | solution.py:920
  559.3 269.4 %reduce-scatter.7.cloned.1.call-start = ((), (), s32[]{:S(2)}) async-start(), calls=%async_computation.5 | async-start | bytes 5242880 | tf_op jit(solution)/shard_map/reduce_scatter | solution.py:1178
  601.9 58.4 %collective-permute-start.39 = (bf16[256,2048]{1,0:T(8,128)(2,1)S(1)}, bf16[256,2048]{1,0:T(8,128)(2,1)S(1)}, u32[]{:S(2)}, u32[]{:S(2)}) collective-permute-start(bf16[256,2048]{1,0:T(8,128)(2,1)S(1)} %get-tuple-element.63.refs_2_), channel_id=1, source_target_pairs={{0,8},{4,12},{8,0},{12,4},{16,24},{20,28},{24,16},{28,20},{1,9},{5... | collective-permute-start | bytes 3145736 | tf_op jit(solution)/shard_map/ppermute | solution.py:920
  603.6 56.7 %collective-permute-start.40 = (bf16[256,2048]{1,0:T(8,128)(2,1)S(1)}, bf16[256,2048]{1,0:T(8,128)(2,1)S(1)}, u32[]{:S(2)}, u32[]{:S(2)}) collective-permute-start(bf16[256,2048]{1,0:T(8,128)(2,1)S(1)} %get-tuple-element.64.refs_3_), channel_id=1, source_target_pairs={{0,16},{4,20},{8,24},{12,28},{16,0},{20,4},{24,8},{28,12},{1,17},{... | collective-permute-start | bytes 3145736 | tf_op jit(solution)/shard_map/ppermute | solution.py:920
  605.1 57.1 %collective-permute-start.41 = (bf16[256,2048]{1,0:T(8,128)(2,1)}, bf16[256,2048]{1,0:T(8,128)(2,1)}, u32[]{:S(2)}, u32[]{:S(2)}) collective-permute-start(bf16[256,2048]{1,0:T(8,128)(2,1)} %get-tuple-element.65.refs_4_), channel_id=1, source_target_pairs={{0,24},{4,28},{8,16},{12,20},{16,8},{20,12},{24,0},{28,4},{1,25},{... | collective-permute-start | bytes 3145736 | tf_op jit(solution)/shard_map/ppermute | solution.py:920
  707.6 182.3 %reduce-scatter.11.cloned.1.call-start = ((), (), s32[]{:S(2)}) async-start(), calls=%async_computation.7 | async-start | bytes 5242880 | tf_op jit(solution)/shard_map/reduce_scatter | solution.py:1178
  733.9 254.8 %reduce-scatter.9.cloned.1.call-start = ((), (), s32[]{:S(2)}) async-start(), calls=%async_computation.6 | async-start | bytes 5242880 | tf_op jit(solution)/shard_map/reduce_scatter | solution.py:1178
  735.5 91.5 %collective-permute-start.45 = (bf16[512,2048]{1,0:T(8,128)(2,1)}, bf16[512,2048]{1,0:T(8,128)(2,1)}, u32[]{:S(2)}, u32[]{:S(2)}) collective-permute-start(bf16[512,2048]{1,0:T(8,128)(2,1)} %get-tuple-element.80), channel_id=1, source_target_pairs={{0,16},{4,20},{8,24},{12,28},{16,0},{20,4},{24,8},{28,12},{1,17},{... | collective-permute-start | bytes 6291464 | tf_op jit(solution)/shard_map/ppermute | solution.py:920
  736.2 92.6 %collective-permute-start.46 = (bf16[512,2048]{1,0:T(8,128)(2,1)}, bf16[512,2048]{1,0:T(8,128)(2,1)}, u32[]{:S(2)}, u32[]{:S(2)}) collective-permute-start(bf16[512,2048]{1,0:T(8,128)(2,1)} %get-tuple-element.81), channel_id=1, source_target_pairs={{0,24},{4,28},{8,16},{12,20},{16,8},{20,12},{24,0},{28,4},{1,25},{... | collective-permute-start | bytes 6291464 | tf_op jit(solution)/shard_map/ppermute | solution.py:920
  864.1 63.3 %collective-permute-start.54 = (bf16[4,256,512]{2,1,0:T(8,128)(2,1)}, bf16[4,256,512]{2,1,0:T(8,128)(2,1)}, u32[]{:S(2)}, u32[]{:S(2)}) collective-permute-start(bf16[4,256,512]{2,1,0:T(8,128)(2,1)} %get-tuple-element.96), channel_id=1, source_target_pairs={{0,24},{4,28},{8,16},{12,20},{16,8},{20,12},{24,0},{28,4},{1,25},{... | collective-permute-start | bytes 3145736 | tf_op jit(solution)/shard_map/ppermute | solution.py:920
  865.9 83.0 %collective-permute-start.53 = (bf16[4,256,512]{2,1,0:T(8,128)(2,1)}, bf16[4,256,512]{2,1,0:T(8,128)(2,1)}, u32[]{:S(2)}, u32[]{:S(2)}) collective-permute-start(bf16[4,256,512]{2,1,0:T(8,128)(2,1)} %get-tuple-element.97), channel_id=1, source_target_pairs={{0,16},{4,20},{8,24},{12,28},{16,0},{20,4},{24,8},{28,12},{1,17},{... | collective-permute-start | bytes 3145736 | tf_op jit(solution)/shard_map/ppermute | solution.py:920
  882.4 66.5 %collective-permute-start.52 = (bf16[4,256,512]{2,1,0:T(8,128)(2,1)}, bf16[4,256,512]{2,1,0:T(8,128)(2,1)}, u32[]{:S(2)}, u32[]{:S(2)}) collective-permute-start(bf16[4,256,512]{2,1,0:T(8,128)(2,1)} %get-tuple-element.95), channel_id=1, source_target_pairs={{0,8},{4,12},{8,0},{12,4},{16,24},{20,28},{24,16},{28,20},{1,9},{5... | collective-permute-start | bytes 3145736 | tf_op jit(solution)/shard_map/ppermute | solution.py:920
  909.1 51.0 %collective-permute-start.66 = (bf16[256,512]{1,0:T(8,128)(2,1)S(1)}, bf16[256,512]{1,0:T(8,128)(2,1)}, u32[]{:S(2)}, u32[]{:S(2)}) collective-permute-start(bf16[256,512]{1,0:T(8,128)(2,1)S(1)} %get-tuple-element.127), channel_id=1, source_target_pairs={{0,2},{1,3},{2,0},{3,1},{4,6},{5,7},{6,4},{7,5},{8,10},{9,11},{10,... | collective-permute-start | bytes 786440 | tf_op jit(solution)/shard_map/ppermute | solution.py:948
  (134 other events, 2649.7 us)
Sparse Core Ops, SparseCore 0:
  27.6 38.1 all-gather.10
  86.4 79.0 all-gather.12
  196.5 79.3 all-gather.14
  277.4 79.2 all-gather.16
  358.1 79.2 all-gather.18
  559.4 75.3 reduce-scatter.4
  707.7 75.0 reduce-scatter.6
  785.2 77.2 reduce-scatter.10
  864.9 95.0 reduce-scatter.8
